TPU v7x, 128 devices: a whole 4x4x4 slice. The times are simulated.
128 devices in a mesh: grp: 8 (over z_hi, x), sub: 16 (over y, z_lo, core).
Axes of the slice: x: 4, y: 4, z: 4 (z_hi: 2, z_lo: 2; z = z_hi * 2 + z_lo), core: 2. Of those that a mesh axis runs over, the one named last changes fastest.
Arguments:
- bem_tiles: float32 [16384, 16384], P('grp', 'sub'), may hold values from -0.03125 to 0.03125
- leaf_inverse: float32 [8, 32, 1024, 1024], P('grp', 'sub'), may hold values from -1.5 to 1.5
- coupling: float32 [8, 32, 1024, 512], P('grp', 'sub'), may hold values from -0.0625 to 0.0625
- schur_inverse: float32 [8, 512, 512], P('grp', None, 'sub'), may hold values from -1.5 to 1.5
- leaf_load: float32 [8, 32, 1024, 128], P('grp', 'sub'), may hold values from -6 to 6
- sep_load: float32 [8, 512, 128], P('grp'), may hold values from -6 to 6
- surf_load: float32 [16384, 128], P(('grp', 'sub')), may hold values from -6 to 6
- surf_start: float32 [16384, 128], P(('grp', 'sub')), may hold values from -6 to 6
- flux_weight: float32 [8, 32, 8, 128], P('grp', 'sub'), may hold values from 0.25 to 1
- trace_weight: float32 [8, 32, 8, 128], P('grp', 'sub'), may hold values from 0.25 to 1
- leaf_sizes: int32 [8, 32], P('grp', 'sub'), may hold values from 512 to 1024
- block_counts: int32 [8, 32], P('grp', 'sub'), may hold values from 4 to 8
- block_owner: int32 [8, 32, 8, 1], P('grp', 'sub'), may hold values from 0 to 15; in each aligned block of 16 rows (0 to 15, 16 to 31, ..., all dimensions but the last counted through in order) at most 2 rows name the same one
Outputs:
- solution: float32 [8, 32, 1024, 128], P('grp', 'sub')
- sep_value: float32 [8, 512, 128], P('grp', 'sub')
- pressure: float32 [16384, 128], P(('grp', 'sub'))
Inputs may be any that keep to these rules, and one draw needn't show every extreme that they name: `block_owner`: of the 16 entries of one device, live or not, at most 2 name the same owner, and some device has 2 entries naming one owner.
All inputs are finite; a program needn't handle non-finite values.
Results may differ from a plain program's by a relative error of at most 0.00018.
Values sent between devices are 32-bit elements; how exact they have to be, the bound alone decides.
No kernel may reach another device: no remote copies, remote signals or barrier semaphores. Data moves between devices by JAX's collectives and lax.ppermute only.
A program may use at most 128 MiB of HBM per device.

v0:
```python
import jax
import jax.numpy as jnp
from jax import lax
from jax.sharding import PartitionSpec as P

SWEEPS = 3
PREC = lax.Precision.HIGH


def mm(spec, a, b):
    return jnp.einsum(spec, a, b, precision=PREC, preferred_element_type=jnp.float32)


def on_device(
    bem_tiles,
    leaf_inverse,
    coupling,
    schur_inverse,
    leaf_load,
    sep_load,
    surf_load,
    surf_start,
    flux_weight,
    trace_weight,
    leaf_sizes,
    block_counts,
    block_owner,
):
    parts = lax.axis_size("sub")
    here = lax.axis_index("sub")
    core = lax.rem(here, 2)
    chips = parts // 2
    width, loads = surf_load.shape
    leaves, order = leaf_inverse.shape[1:3]
    blocks = order // width
    entries = leaves * blocks
    separator = schur_inverse.shape[1]
    share = schur_inverse.shape[2]
    same_core = [[2 * c + k for c in range(chips)] for k in range(2)]
    swap = [(i, i ^ 1) for i in range(parts)]

    def halves(z):
        pairs = z.reshape(chips, 2, *z.shape[1:])
        mine = jnp.where(core == 0, pairs[:, 0], pairs[:, 1])
        other = jnp.where(core == 0, pairs[:, 1], pairs[:, 0])
        return mine, other

    def summed(z):
        mine, other = halves(z)
        mine = mine + lax.ppermute(other, "sub", swap)
        got = lax.all_to_all(mine, "sub", 0, 0, axis_index_groups=same_core, tiled=True)
        return got.sum(0)

    def gathered(x):
        wide = jnp.broadcast_to(x[None], (chips, *x.shape))
        mine = lax.all_to_all(wide, "sub", 0, 0, axis_index_groups=same_core, tiled=True)
        other = lax.ppermute(mine, "sub", swap)
        pairs = jnp.where(
            core == 0, jnp.stack([mine, other], 1), jnp.stack([other, mine], 1)
        )
        return pairs.reshape(parts, *x.shape)

    row_mask = (jnp.arange(order, dtype=jnp.int32)[None, :] < leaf_sizes[0][:, None]).astype(
        jnp.float32
    )[:, :, None]
    active = (
        (jnp.arange(blocks, dtype=jnp.int32)[None, :] < block_counts[0][:, None])
        .astype(jnp.float32)
        .reshape(entries)
    )
    owner = block_owner[0, :, :, 0].reshape(entries)
    picker = (owner[:, None] == jnp.arange(parts, dtype=jnp.int32)[None, :]).astype(jnp.float32)
    flux_scale = (flux_weight[0].reshape(entries, width) * active[:, None])[:, :, None]
    trace_scale = (trace_weight[0].reshape(entries, width) * active[:, None])[:, :, None]

    schur_t = lax.all_gather(schur_inverse[0].T, "sub", axis=0, tiled=True)
    pressure = surf_start
    payload = surf_start
    for sweep in range(SWEEPS):
        spread = gathered(payload)
        column = lax.all_to_all(
            jnp.broadcast_to(pressure[None], (lax.axis_size("grp"), *pressure.shape)),
            "grp", 0, 0, tiled=True,
        ).reshape(-1, loads)
        surface = spread[:, :width]
        flux = mm("eo,oil->eil", picker, surface) * flux_scale
        rhs = leaf_load[0] - flux.reshape(leaves, order, loads)
        if sweep:
            total = spread[:, width:].reshape(separator, loads)
            sep_value = mm("ts,tl->sl", schur_t, sep_load[0] - total)
            rhs = rhs - mm("jrs,sl->jrl", coupling[0], sep_value)
        solution = mm("jrc,jcl->jrl", leaf_inverse[0], rhs * row_mask) * row_mask
        part = mm("jrs,jrl->sl", coupling[0], solution)
        if sweep == SWEEPS - 1:
            part = mm("ts,tl->sl", schur_t, part)
        weighted = solution.reshape(entries, width, loads) * trace_scale
        dense = mm("eo,eil->oil", picker, weighted)
        applied = mm("rc,cl->rl", bem_tiles, column).reshape(parts, width, loads)
        payload = summed(
            jnp.concatenate([applied + dense, part.reshape(parts, share, loads)], axis=1)
        )
        pressure = surf_load + payload[:width]
        payload = jnp.concatenate([pressure, payload[width:]], axis=0)
    own = mm("ts,tl->sl", lax.dynamic_slice_in_dim(schur_t, here * share, share, 1), sep_load[0])
    return (solution[None], (own - payload[width:])[None], pressure)


def solution(mesh):
    return jax.shard_map(
        on_device,
        mesh=mesh,
        in_specs=(
            P("grp", "sub"),
            P("grp", "sub", None, None),
            P("grp", "sub", None, None),
            P("grp", None, "sub"),
            P("grp", "sub", None, None),
            P("grp", None, None),
            P(("grp", "sub"), None),
            P(("grp", "sub"), None),
            P("grp", "sub", None, None),
            P("grp", "sub", None, None),
            P("grp", "sub"),
            P("grp", "sub"),
            P("grp", "sub", None, None),
        ),
        out_specs=(P("grp", "sub", None, None), P("grp", "sub", None), P(("grp", "sub"), None)),
        check_vma=False,
    )
```

profile of v0, /device:TPU:0, one launch (start us, length us, event | category | flops | bytes accessed | tf_op | source)
XLA Modules:
  0.0 272.2 jit_solution(630347414618555972)
XLA Ops:
  7.2 1.8 broadcast_in_dim.14
  9.0 15.6 %all_to_all.45 = f32[8,128,128]{2,1,0:T(8,128)S(1)} all-to-all(f32[8,128,128]{2,1,0:T(8,128)} %broadcast_in_dim.14), channel_id=1, replica_groups={{0,2,4,6,8,10,12,14},{1,3,5,7,9,11,13,15},{16,18,20,22,24,26,28,30},{17..., dimensions={0} | all-to-all | bytes 1048576 | tf_op jit(solution)/shard_map/all_to_all | solution.py:56
  24.6 7.3 %all-to-all-start = ((f32[8,128,128]{2,1,0:T(8,128)}), f32[8,128,128]{2,1,0:T(8,128)}, u32[]{:S(2)}, u32[]{:S(2)}) async-start(f32[8,128,128]{2,1,0:T(8,128)} %broadcast_in_dim.14), calls=%async_computation | async-start | bytes 1048576 | tf_op jit(solution)/shard_map/all_to_all | solution.py:81
  36.2 7.6 %fusion.37 = f32[2,1024,128]{1,2,0:T(8,128)S(1)} fusion(f32[1,2,1024,1024]{3,2,1,0:T(8,128)} %param.14, f32[2,1024,128]{1,2,0:T(8,128)S(1)} %copy.118, f32[1,2,1024,128]{2,3,1,0:T(8,128)S(1)} %copy.113, f32[2,1024]{1,0:T(2,128)S(1)} %compare_convert_fusion), kind=kOutput, calls=%fused_computation.31 | convolution fusion | flops 1611399168 | bytes 11542528 | tf_op jit(solution)/shard_map/jrc,jcl->jrl/dot_general | solution.py:11
  44.1 4.2 %fusion.49 = f32[512,128]{0,1:T(8,128)} fusion(f32[2,1024,128]{1,2,0:T(8,128)S(1)} %fusion.37, f32[1,2,1024,512]{3,2,1,0:T(8,128)} %param.15), kind=kOutput, calls=%fused_computation.39 | convolution fusion | flops 805306368 | bytes 5505024 | tf_op jit(solution)/shard_map/jrs,jrl->sl/dot_general | solution.py:11
  50.7 6.1 %convolution_add_fusion.2 = f32[16,128,128]{2,1,0:T(8,128)S(1)} fusion(f32[16,128,1024]{2,1,0:T(8,128)} %bitcast.212, f32[1024,128,1]{1,0,2:T(8,128)} %bitcast.4, f32[16,128,128]{2,0,1:T(8,128)S(1)} %fusion.64), kind=kOutput, calls=%fused_computation.25 | convolution fusion | flops 1610874880 | bytes 11010048 | tf_op jit(solution)/shard_map/rc,cl->rl/dot_general | solution.py:11
  59.3 14.7 %all_to_all.46 = f32[8,160,128]{2,1,0:T(8,128)S(1)} all-to-all(f32[8,160,128]{2,1,0:T(8,128)S(1)} %fusion.68), channel_id=1, replica_groups={{0,2,4,6,8,10,12,14},{1,3,5,7,9,11,13,15},{16,18,20,22,24,26,28,30},{17..., dimensions={0} | all-to-all | bytes 1310720 | tf_op jit(solution)/shard_map/all_to_all | solution.py:51
  74.9 4.2 %all-to-all-start.4 = ((f32[8,160,128]{2,1,0:T(8,128)}), f32[8,160,128]{2,1,0:T(8,128)}, u32[]{:S(2)}, u32[]{:S(2)}) async-start(f32[8,160,128]{2,1,0:T(8,128)} %broadcast_in_dim.16), calls=%async_computation.4 | async-start | bytes 1310720 | tf_op jit(solution)/shard_map/all_to_all | solution.py:56
  79.8 9.6 %all-to-all-done.4 = f32[8,160,128]{2,1,0:T(8,128)} async-done(((f32[8,160,128]{2,1,0:T(8,128)}), f32[8,160,128]{2,1,0:T(8,128)}, u32[]{:S(2)}, u32[]{:S(2)}) %all-to-all-start.4) | async-done | bytes 655392 | tf_op jit(solution)/shard_map/all_to_all | solution.py:56
  90.2 7.2 %all-to-all-start.3 = ((f32[8,128,128]{2,1,0:T(8,128)}), f32[8,128,128]{2,1,0:T(8,128)S(1)}, u32[]{:S(2)}, u32[]{:S(2)}) async-start(f32[8,128,128]{2,1,0:T(8,128)} %broadcast_in_dim.15), calls=%async_computation.3 | async-start | bytes 1048576 | tf_op jit(solution)/shard_map/all_to_all | solution.py:81
  97.7 10.0 %all-to-all-done.3 = f32[8,128,128]{2,1,0:T(8,128)S(1)} async-done(((f32[8,128,128]{2,1,0:T(8,128)}), f32[8,128,128]{2,1,0:T(8,128)S(1)}, u32[]{:S(2)}, u32[]{:S(2)}) %all-to-all-start.3) | async-done | bytes 524320 | tf_op jit(solution)/shard_map/all_to_all | solution.py:81
  107.7 7.8 %convolution_bitcast_fusion.1 = f32[16,8,16,128]{3,1,2,0:T(8,128)S(1)} fusion(f32[1024,128]{1,0:T(8,128)S(1)} %bitcast.235, f32[2048,1024]{1,0:T(8,128)} %param.13), kind=kOutput, calls=%fused_computation.23 | convolution fusion | flops 1610612736 | bytes 9961472 | tf_op jit(solution)/shard_map/rc,cl->rl/dot_general | solution.py:11
  116.4 1.8 maximum_select_fusion
  123.9 1.7 convolution_bitcast_fusion.4
  125.7 4.4 %fusion.31 = f32[2,1024,128]{1,2,0:T(8,128)S(1)} fusion(f32[128,512,1]{1,0,2:T(8,128)S(1)} %convolution_bitcast_fusion.4, f32[1,2,1024,512]{3,2,1,0:T(8,128)} %param.15, f32[2,1024,128]{1,2,0:T(8,128)S(1)} %copy-done.3, f32[1,2,1024,128]{2,3,1,0:T(8,128)S(1)} %copy.113, f32[2,1024]{1,0:T(2,128)S(1)} %compare_convert_fusion), kind=kOutput, calls=%fused_computation.29 | convolution fusion | flops 806092800 | bytes 7610368 | tf_op jit(solution)/shard_map/jrs,sl->jrl/dot_general | solution.py:11
  130.1 19.6 %fusion.43 = f32[2,1024,128]{1,2,0:T(8,128)S(1)} fusion(f32[2,1024,128]{1,2,0:T(8,128)S(1)} %fusion.31, f32[1,2,1024,1024]{3,2,1,0:T(8,128)} %param.14, f32[2,1024]{1,0:T(2,128)S(1)} %compare_convert_fusion), kind=kOutput, calls=%fused_computation.33 | convolution fusion | flops 1610874880 | bytes 10493952 | tf_op jit(solution)/shard_map/jrc,jcl->jrl/dot_general | solution.py:11
  149.7 2.2 fusion.52
  154.8 1.8 copy.135
  159.3 2.1 collective-permute-done.3
  161.5 15.0 %all_to_all.47 = f32[8,160,128]{2,1,0:T(8,128)S(1)} all-to-all(f32[8,160,128]{2,1,0:T(8,128)S(1)} %bitcast_add_fusion.1), channel_id=1, replica_groups={{0,2,4,6,8,10,12,14},{1,3,5,7,9,11,13,15},{16,18,20,22,24,26,28,30},{17..., dimensions={0} | all-to-all | bytes 1310720 | tf_op jit(solution)/shard_map/all_to_all | solution.py:51
  176.7 13.5 %all_to_all.48 = f32[8,160,128]{2,1,0:T(8,128)} all-to-all(f32[8,160,128]{2,1,0:T(8,128)S(1)} %broadcast_in_dim.17), channel_id=1, replica_groups={{0,2,4,6,8,10,12,14},{1,3,5,7,9,11,13,15},{16,18,20,22,24,26,28,30},{17..., dimensions={0} | all-to-all | bytes 1310720 | tf_op jit(solution)/shard_map/all_to_all | solution.py:56
  191.0 3.5 %all-to-all-start.7 = ((f32[8,128,128]{2,1,0:T(8,128)}), f32[8,128,128]{2,1,0:T(8,128)S(1)}, u32[]{:S(2)}, u32[]{:S(2)}) async-start(f32[8,128,128]{2,1,0:T(8,128)} %broadcast_in_dim.19), calls=%async_computation.7 | async-start | bytes 1048576 | tf_op jit(solution)/shard_map/all_to_all | solution.py:81
  194.6 10.0 %all-to-all-done.7 = f32[8,128,128]{2,1,0:T(8,128)S(1)} async-done(((f32[8,128,128]{2,1,0:T(8,128)}), f32[8,128,128]{2,1,0:T(8,128)S(1)}, u32[]{:S(2)}, u32[]{:S(2)}) %all-to-all-start.7) | async-done | bytes 524320 | tf_op jit(solution)/shard_map/all_to_all | solution.py:81
  204.6 7.7 %convolution_bitcast_fusion = f32[16,8,16,128]{3,1,2,0:T(8,128)S(1)} fusion(f32[1024,128]{1,0:T(8,128)S(1)} %bitcast.236, f32[2048,1024]{1,0:T(8,128)} %param.13), kind=kOutput, calls=%fused_computation.19 | convolution fusion | flops 1610612736 | bytes 9961472 | tf_op jit(solution)/shard_map/rc,cl->rl/dot_general | solution.py:11
  213.3 1.8 maximum_select_fusion.1
  218.7 2.6 copy.141
  223.5 4.5 %fusion.25 = f32[2,1024,128]{1,2,0:T(8,128)S(1)} fusion(f32[128,512,1]{1,0,2:T(8,128)S(1)} %convolution_bitcast_fusion.3, f32[1,2,1024,512]{3,2,1,0:T(8,128)} %param.15, f32[2,1024,128]{1,2,0:T(8,128)S(1)} %copy-done.4, f32[1,2,1024,128]{2,3,1,0:T(8,128)S(1)} %copy.113, f32[2,1024]{1,0:T(2,128)S(1)} %compare_convert_fusion), kind=kOutput, calls=%fused_computation.27 | convolution fusion | flops 806092800 | bytes 7610368 | tf_op jit(solution)/shard_map/jrs,sl->jrl/dot_general | solution.py:11
  228.0 8.0 %fusion.46 = f32[2,128,1024]{2,1,0:T(8,128)S(1)} fusion(f32[2,1024,128]{1,2,0:T(8,128)S(1)} %fusion.25, f32[1,2,1024,1024]{3,2,1,0:T(8,128)} %param.14, f32[2,1024]{1,0:T(2,128)S(1)} %compare_convert_fusion), kind=kOutput, calls=%fused_computation.34 | convolution fusion | flops 1610874880 | bytes 10493952 | tf_op jit(solution)/shard_map/jrc,jcl->jrl/dot_general | solution.py:11
  238.7 1.8 copy.146
  245.4 2.1 collective-permute-done.5
  248.4 3.5 %all-to-all-start.8 = ((f32[8,160,128]{2,1,0:T(8,128)}), f32[8,160,128]{2,1,0:T(8,128)S(1)}, u32[]{:S(2)}, u32[]{:S(2)}) async-start(f32[8,160,128]{2,1,0:T(8,128)} %bitcast_add_fusion), calls=%async_computation.8 | async-start | bytes 1310720 | tf_op jit(solution)/shard_map/all_to_all | solution.py:51
  253.3 10.1 %all-to-all-done.8 = f32[8,160,128]{2,1,0:T(8,128)S(1)} async-done(((f32[8,160,128]{2,1,0:T(8,128)}), f32[8,160,128]{2,1,0:T(8,128)S(1)}, u32[]{:S(2)}, u32[]{:S(2)}) %all-to-all-start.8) | async-done | bytes 655392 | tf_op jit(solution)/shard_map/all_to_all | solution.py:51
  (122 shorter events, 43.3 us)
Async XLA Ops:
  7.2 24.9 %copy-start.18 = (s32[1,2]{1,0:T(1,128)S(1)}, s32[1,2]{1,0:T(1,128)}, u32[]{:S(2)}) copy-start(s32[1,2]{1,0:T(1,128)} %param.24) | copy-start | bytes 28
  7.2 25.4 %copy-start.16 = (s32[1,2,8,1]{2,3,1,0:T(1,128)S(1)}, s32[1,2,8,1]{2,3,1,0:T(1,128)}, u32[]{:S(2)}) copy-start(s32[1,2,8,1]{2,3,1,0:T(1,128)} %param.25) | copy-start | bytes 196
  7.2 26.3 %copy-start.14 = (f32[1,2,8,128]{3,2,1,0:T(8,128)S(1)}, f32[1,2,8,128]{3,2,1,0:T(8,128)}, u32[]{:S(2)}) copy-start(f32[1,2,8,128]{3,2,1,0:T(8,128)} %param.22) | copy-start | bytes 24580
  7.2 26.3 %copy-start.15 = (f32[1,2,8,128]{3,2,1,0:T(8,128)S(1)}, f32[1,2,8,128]{3,2,1,0:T(8,128)}, u32[]{:S(2)}) copy-start(f32[1,2,8,128]{3,2,1,0:T(8,128)} %param.21) | copy-start | bytes 24580
  7.2 26.4 %copy-start.6 = (f32[1,2,1024,128]{3,2,1,0:T(8,128)S(1)}, f32[1,2,1024,128]{3,2,1,0:T(8,128)}, u32[]{:S(2)}) copy-start(f32[1,2,1024,128]{3,2,1,0:T(8,128)} %param.17) | copy-start | bytes 3145732
  24.6 26.0 %all-to-all-start = ((f32[8,128,128]{2,1,0:T(8,128)}), f32[8,128,128]{2,1,0:T(8,128)}, u32[]{:S(2)}, u32[]{:S(2)}) async-start(f32[8,128,128]{2,1,0:T(8,128)} %broadcast_in_dim.14), calls=%async_computation | async-start | bytes 1048576 | tf_op jit(solution)/shard_map/all_to_all | solution.py:81
  31.9 2.1 copy-start.17
  31.9 2.1 collective-permute-start
  33.4 16.4 %copy-start.10 = (s32[16]{0:T(128)}, s32[16]{0:T(128)S(1)}, u32[]{:S(2)}) copy-start(s32[16]{0:T(128)S(1)} %eq.10) | copy-start | bytes 196
  56.8 2.3 collective-permute-start.1
  59.2 14.7 %copy-start.9 = (f32[128,128]{1,0:T(8,128)S(1)}, f32[128,128]{1,0:T(8,128)}, u32[]{:S(2)}) copy-start(f32[128,128]{1,0:T(8,128)} %param.19) | copy-start | bytes 196612
  74.9 14.5 %all-to-all-start.4 = ((f32[8,160,128]{2,1,0:T(8,128)}), f32[8,160,128]{2,1,0:T(8,128)}, u32[]{:S(2)}, u32[]{:S(2)}) async-start(f32[8,160,128]{2,1,0:T(8,128)} %broadcast_in_dim.16), calls=%async_computation.4 | async-start | bytes 1310720 | tf_op jit(solution)/shard_map/all_to_all | solution.py:56
  79.1 44.8 %all-gather.2.cloned.1.call-start = ((), (), s32[]{:S(2)}) async-start(), calls=%async_computation.9 | async-start | bytes 1114112 | tf_op jit(solution)/shard_map/all_gather | solution.py:76
  90.2 17.5 %all-to-all-start.3 = ((f32[8,128,128]{2,1,0:T(8,128)}), f32[8,128,128]{2,1,0:T(8,128)S(1)}, u32[]{:S(2)}, u32[]{:S(2)}) async-start(f32[8,128,128]{2,1,0:T(8,128)} %broadcast_in_dim.15), calls=%async_computation.3 | async-start | bytes 1048576 | tf_op jit(solution)/shard_map/all_to_all | solution.py:81
  97.5 18.9 %collective-permute-start.2 = (f32[8,160,128]{2,1,0:T(8,128)}, f32[8,160,128]{2,1,0:T(8,128)}, u32[]{:S(2)}, u32[]{:S(2)}) collective-permute-start(f32[8,160,128]{2,1,0:T(8,128)} %all-to-all-done.4), channel_id=1, source_target_pairs={{0,1},{1,0},{2,3},{3,2},{4,5},{5,4},{6,7},{7,6},{8,9},{9,8},{10,11... | collective-permute-start | bytes 1966088 | tf_op jit(solution)/shard_map/ppermute | solution.py:57
  118.2 1.7 copy-start.11
  120.8 2.4 copy-start.5
  123.2 2.5 copy-start.3
  130.1 19.6 %copy-start = (f32[1,2,1024,512]{3,2,1,0:T(8,128)S(1)}, f32[1,2,1024,512]{3,2,1,0:T(8,128)}, u32[]{:S(2)}) copy-start(f32[1,2,1024,512]{3,2,1,0:T(8,128)} %param.15) | copy-start | bytes 12582916
  158.2 1.0 copy-start.8
  159.2 2.2 collective-permute-start.3
  191.0 13.6 %all-to-all-start.7 = ((f32[8,128,128]{2,1,0:T(8,128)}), f32[8,128,128]{2,1,0:T(8,128)S(1)}, u32[]{:S(2)}, u32[]{:S(2)}) async-start(f32[8,128,128]{2,1,0:T(8,128)} %broadcast_in_dim.19), calls=%async_computation.7 | async-start | bytes 1048576 | tf_op jit(solution)/shard_map/all_to_all | solution.py:81
  194.5 18.8 %collective-permute-start.4 = (f32[8,160,128]{2,1,0:T(8,128)}, f32[8,160,128]{2,1,0:T(8,128)}, u32[]{:S(2)}, u32[]{:S(2)}) collective-permute-start(f32[8,160,128]{2,1,0:T(8,128)} %all_to_all.48), channel_id=1, source_target_pairs={{0,1},{1,0},{2,3},{3,2},{4,5},{5,4},{6,7},{7,6},{8,9},{9,8},{10,11... | collective-permute-start | bytes 1966088 | tf_op jit(solution)/shard_map/ppermute | solution.py:57
  215.1 1.7 copy-start.12
  218.7 3.7 %copy-start.2 = (f32[512,512]{1,0:T(8,128)S(1)}, f32[512,512]{1,0:T(8,128)}, u32[]{:S(2)}) copy-start(f32[512,512]{1,0:T(8,128)} %all-gather.2.cloned.1.call-done) | copy-start | bytes 3145732
  222.3 1.2 copy-start.4
  228.0 8.0 %copy-start.1 = (f32[1,2,1024,512]{3,2,1,0:T(8,128)S(1)}, f32[1,2,1024,512]{3,2,1,0:T(8,128)}, u32[]{:S(2)}) copy-start(f32[1,2,1024,512]{3,2,1,0:T(8,128)} %param.15) | copy-start | bytes 12582916
  241.8 1.6 copy-start.13
  244.2 1.0 copy-start.7
  245.3 2.2 collective-permute-start.5
  248.4 15.0 %all-to-all-start.8 = ((f32[8,160,128]{2,1,0:T(8,128)}), f32[8,160,128]{2,1,0:T(8,128)S(1)}, u32[]{:S(2)}, u32[]{:S(2)}) async-start(f32[8,160,128]{2,1,0:T(8,128)} %bitcast_add_fusion), calls=%async_computation.8 | async-start | bytes 1310720 | tf_op jit(solution)/shard_map/all_to_all | solution.py:51
Sparse Core Ops, SparseCore 0:
  81.6 35.5 all-gather.1
where the time goes:
time: 277 us; the launch traced here: 272 us
  matrix products  82.9 us (30%)
  blocking collectives  58.8 us (21%)
  waiting for transfers between devices  46.3 us (17%)
  local copies, waits for them, and re-layouts  31.3 us (11%)
  starting transfers between devices  27 us (10%)
  between operations  15 us (5%)
  other arithmetic  11 us (4%)
    dot_general x21, matrix products, mm(): jnp.einsum(spec, a, b, precision=PREC, preferred_element_type=jnp.float32)  82.9 us
    all_to_all x2, blocking collectives, summed(): lax.all_to_all(mine, 'sub', 0, 0, axis_index_groups=same_core, tiled=True)  29.7 us
    all_to_all x2, blocking collectives, gathered(): lax.all_to_all(wide, 'sub', 0, 0, axis_index_groups=same_core, tiled=True)  29.1 us
    all_to_all x3, waiting for transfers between devices, on_device(): lax.all_to_all(jnp.broadcast_to(pressure[None], (lax.axis_size('grp'), *p...  20 us
    all_to_all x3, starting transfers between devices, on_device(): lax.all_to_all(jnp.broadcast_to(pressure[None], (lax.axis_size('grp'), *p...  18 us
    all_to_all x1, waiting for transfers between devices, summed(): lax.all_to_all(mine, 'sub', 0, 0, axis_index_groups=same_core, tiled=True)  10.1 us
    all_to_all x1, waiting for transfers between devices, gathered(): lax.all_to_all(wide, 'sub', 0, 0, axis_index_groups=same_core, tiled=True)  9.58 us
    ppermute x3, waiting for transfers between devices, summed(): mine = mine + lax.ppermute(other, 'sub', swap)  5.89 us
  transfers between devices with their start and end apart: 12, of which 7 were waited for; matrix products, arithmetic and copies ran while one was open for 17% of the time, Pallas kernels for 0%

commit v1 on v0

v1 whole, which is shorter than its diff:
```python
import functools

import jax
import jax.numpy as jnp
from jax import lax
from jax.experimental import pallas as pl
from jax.experimental.pallas import tpu as pltpu
from jax.sharding import PartitionSpec as P

SWEEPS = 3
F32, BF16 = jnp.float32, jnp.bfloat16
VM = pl.BlockSpec(memory_space=pltpu.VMEM)
SM = pl.BlockSpec(memory_space=pltpu.SMEM)
AN = pl.BlockSpec(memory_space=pltpu.HBM)
MIB = 2**20


GRP_STEPS = (4, 1, 3)
SUB_STEPS = (2, 4, 12, 1)


def origins(steps):
    found = [0]
    for step in steps:
        found += [step ^ origin for origin in found]
    return found


def call(body, name, out, ins, scratch=(), limit=6, flops=0, moved=0):
    return pl.pallas_call(
        body,
        out_shape=out,
        in_specs=ins,
        out_specs=jax.tree.map(lambda _: VM, out),
        scratch_shapes=list(scratch),
        compiler_params=pltpu.CompilerParams(vmem_limit_bytes=limit * MIB),
        cost_estimate=pl.CostEstimate(flops=flops, bytes_accessed=moved, transcendentals=0),
        name=name,
    )


def shaped(shape, dtype=F32):
    return jax.ShapeDtypeStruct(shape, dtype)


def parted(x):
    hi = x.astype(BF16)
    return hi, (x - hi.astype(F32)).astype(BF16)


def widened(x):
    return jnp.concatenate(parted(x), axis=1)


def dot(a, b):
    return jnp.dot(a, b, preferred_element_type=F32)


def product(hi, lo, wide):
    n = wide.shape[1] // 2
    both = dot(hi, wide)
    return both[:, :n] + both[:, n:] + dot(lo, wide[:, :n])


def streamed(src, buf, sems, tile, use):
    slots = buf.shape[0]
    count = src.shape[0] // tile

    def copy(i, slot):
        return pltpu.make_async_copy(src.at[pl.ds(i * tile, tile)], buf.at[slot], sems.at[slot])

    for i in range(min(slots, count)):
        copy(i, i).start()
    for i in range(count):
        copy(i, i % slots).wait()
        use(i, buf[i % slots])
        if i + slots < count:
            copy(i + slots, i % slots).start()


def split_rows(tile, src, hi_ref, lo_ref, buf, sems):
    def use(i, x):
        rows = slice(i * tile, (i + 1) * tile)
        hi_ref[rows], lo_ref[rows] = parted(x)

    streamed(src, buf, sems, tile, use)


def split_cores(tile, width, src, hi_ref, lo_ref, buf, sems):
    def use(i, x):
        for b in range(tile // width):
            block = i * (tile // width) + b
            chip, core = block // 2, block % 2
            rows = slice(chip * width, (chip + 1) * width)
            hi, lo = parted(x[b * width : (b + 1) * width])
            hi_ref[core, rows], lo_ref[core, rows] = hi, lo

    streamed(src, buf, sems, tile, use)


def split_turned(tile, src, hi_ref, lo_ref, hi_t_ref, lo_t_ref, buf, sems):
    def use(i, x):
        rows = slice(i * tile, (i + 1) * tile)
        hi_ref[rows], lo_ref[rows] = parted(x)
        hi_t_ref[:, rows], lo_t_ref[:, rows] = parted(x.T)

    streamed(src, buf, sems, tile, use)


def split_call(x, body, name, outs, tile):
    slots = 4
    return call(
        body,
        name,
        tuple(shaped(s, BF16) for s in outs),
        [AN],
        [pltpu.VMEM((slots, tile, x.shape[1]), F32), pltpu.SemaphoreType.DMA((slots,))],
        limit=8,
        moved=4 * x.size,
    )(x)


def laid(pieces, steps, here, whole):
    rows = pieces[0].shape[0]
    block = 0
    for piece in pieces:
        for i in range(piece.shape[0] // rows):
            at = pl.multiple_of((here ^ origins(steps)[block]) * rows, rows)
            whole[pl.ds(at, rows)] = piece[i * rows : (i + 1) * rows]
            block += 1


def turn_kernel(here_ref, *rest):
    *pieces, hi_ref, lo_ref, whole = rest
    laid(pieces, SUB_STEPS, here_ref[0], whole)
    hi_ref[...], lo_ref[...] = parted(whole[...].T)


def leaf_kernel(
    width, first, last,
    here_ref, owner_ref, size_ref,
    load, flux_t, trace_t, inv_hi, inv_lo, cpl_t_hi, cpl_t_lo, sep_load,
    *rest,
):
    if first:
        *rest, field = rest
    *rest, sol, dense, part, gathered, wide, wide_sol = rest
    leaves, order, loads = load.shape
    blocks = order // width
    chips = dense.shape[1]
    share = part.shape[0] // (2 * chips)
    here = here_ref[0]
    core = here % 2

    if first:
        laid(rest, SUB_STEPS, here, field)

        def surface(o):
            return field[pl.ds(pl.multiple_of(o * width, width), width)]

    else:
        cpl_hi, cpl_lo, sch_hi, sch_lo, mine, other = rest

        def surface(o):
            chip = o // 2
            return jnp.where(o - 2 * chip == core, mine[chip, :width], other[chip, :width])

    if not first:
        for chip in range(chips):
            a, b = mine[chip, width:], other[chip, width:]
            at = 2 * chip * share
            gathered[at : at + share] = jnp.where(core == 0, a, b)
            gathered[at + share : at + 2 * share] = jnp.where(core == 0, b, a)
        sep_wide = widened(product(sch_hi[...], sch_lo[...], widened(gathered[...])))
    dense[...] = jnp.zeros_like(dense)
    for j in range(leaves):
        rows = slice(j * order, (j + 1) * order)
        if not first:
            pulled = product(cpl_hi[rows], cpl_lo[rows], sep_wide)
        for k in range(blocks):
            e = j * blocks + k
            o = owner_ref[e]
            at = slice(k * width, (k + 1) * width)
            rhs = load[j, at] - surface(o) * flux_t[:, e : e + 1]
            if not first:
                rhs = rhs - pulled[at]
            row = k * width + lax.broadcasted_iota(jnp.int32, (width, loads), 0)
            wide[at] = widened(jnp.where(row < size_ref[j], rhs, 0.0))
        got = product(inv_hi[rows], inv_lo[rows], wide[...])
        for k in range(blocks):
            e = j * blocks + k
            o = owner_ref[e]
            chip = o // 2
            at = slice(k * width, (k + 1) * width)
            row = k * width + lax.broadcasted_iota(jnp.int32, (width, loads), 0)
            block = jnp.where(row < size_ref[j], got[at], 0.0)
            sol[j, at] = block
            dense[o - 2 * chip, chip] += block * trace_t[:, e : e + 1]
            wide_sol[j * order + k * width : j * order + (k + 1) * width] = widened(block)
    left = jnp.where(here == 0, sep_load[...], 0.0) - product(
        cpl_t_hi[...], cpl_t_lo[...], wide_sol[...]
    )
    if last:
        left = product(sch_hi[...], sch_lo[...], widened(left))
    part[...] = left


def surface_kernel(width, pick_ref, group_ref, hi, lo, *rest):
    *pieces, dense, part, out, wide = rest
    pick = pick_ref[0]
    chips = out.shape[0]
    share = part.shape[0] // (2 * chips)
    block = 0
    for piece in pieces:
        for i in range(piece.shape[0] // width):
            at = pl.multiple_of((group_ref[0] ^ origins(GRP_STEPS)[block]) * width, width)
            wide[pl.ds(at, width)] = widened(piece[i * width : (i + 1) * width])
            block += 1
    got = product(hi[pick], lo[pick], wide[...])
    for chip in range(chips):
        out[chip, :width] = dense[pick, chip] + got[chip * width : (chip + 1) * width]
        at = pl.multiple_of((2 * chip + pick) * share, share)
        out[chip, width:] = part[pl.ds(at, share)]


def total_kernel(width, got, load, wide, again):
    chips = got.shape[0]
    total = got[0]
    for chip in range(1, chips):
        total = total + got[chip]
    field = load[...] + total[:width]
    for chip in range(chips):
        wide[chip, :width] = field
        wide[chip, width:] = total[width:]
    again[...] = field


def final_kernel(width, got, load, field, separator):
    total = got[0]
    for chip in range(1, got.shape[0]):
        total = total + got[chip]
    field[...] = load[...] + total[:width]
    separator[...] = total[width:]


def on_device(
    bem_tiles,
    leaf_inverse,
    coupling,
    schur_inverse,
    leaf_load,
    sep_load,
    surf_load,
    surf_start,
    flux_weight,
    trace_weight,
    leaf_sizes,
    block_counts,
    block_owner,
):
    parts = lax.axis_size("sub")
    here = lax.axis_index("sub")
    core = lax.rem(here, 2).astype(jnp.int32)
    mine_id, other_id = core.reshape(1), (1 - core).reshape(1)
    here_id = here.astype(jnp.int32).reshape(1)
    group = lax.axis_index("grp").astype(jnp.int32).reshape(1)
    chips = parts // 2
    width, loads = surf_load.shape
    leaves, order = leaf_inverse.shape[1:3]
    blocks = order // width
    entries = leaves * blocks
    separator = schur_inverse.shape[1]
    share = schur_inverse.shape[2]
    rows = bem_tiles.shape[0]
    columns = bem_tiles.shape[1]
    same_core = [[2 * c + k for c in range(chips)] for k in range(2)]
    swap = [(i, i ^ 1) for i in range(parts)]

    def over_chips(x):
        return lax.all_to_all(x, "sub", 0, 0, axis_index_groups=same_core, tiled=True)

    def doubled(x, axis, steps):
        size = lax.axis_size(axis)
        pieces = [x]
        for step in steps:
            held = pieces[0] if len(pieces) == 1 else jnp.concatenate(pieces, axis=0)
            pieces.append(lax.ppermute(held, axis, [(i, i ^ step) for i in range(size)]))
        return pieces

    inv = leaf_inverse.reshape(leaves * order, order)
    cpl = coupling.reshape(leaves * order, separator)
    inv_hi, inv_lo = split_call(
        inv, functools.partial(split_rows, 256), "split_leaf", [inv.shape] * 2, 256
    )
    cpl_hi, cpl_lo, cpl_t_hi, cpl_t_lo = split_call(
        cpl, functools.partial(split_turned, 256), "split_coupling",
        [cpl.shape] * 2 + [cpl.shape[::-1]] * 2, 256,
    )
    bem_hi, bem_lo = split_call(
        bem_tiles, functools.partial(split_cores, 2 * width, width), "split_surface",
        [(2, rows // 2, columns)] * 2, 2 * width,
    )
    active = (
        (jnp.arange(blocks, dtype=jnp.int32)[None, :] < block_counts[0][:, None])
        .astype(F32)
        .reshape(entries, 1)
    )
    owner = block_owner.reshape(entries)
    sizes = leaf_sizes.reshape(leaves)
    flux_t = (flux_weight.reshape(entries, width) * active).T
    trace_t = (trace_weight.reshape(entries, width) * active).T
    field = surf_start
    for sweep in range(SWEEPS):
        first, last = sweep == 0, sweep == SWEEPS - 1
        if first:
            known = doubled(surf_start, "sub", SUB_STEPS)
        else:
            mine = over_chips(wide)
            mine, field = lax.optimization_barrier((mine, field))
            known = [mine, lax.ppermute(mine, "sub", swap)]
        pieces = doubled(field, "grp", GRP_STEPS)
        if first:
            schur_pieces = doubled(schur_inverse[0].T, "sub", SUB_STEPS)
            sch_hi, sch_lo = call(
                turn_kernel, "split_schur", (shaped((separator, separator), BF16),) * 2,
                [SM] + [VM] * len(schur_pieces),
                [pltpu.VMEM((separator, separator), F32)],
                moved=8 * separator * separator,
            )(here_id, *schur_pieces)
        operands = [here_id, owner, sizes, leaf_load[0], flux_t, trace_t]
        operands += [inv_hi, inv_lo, cpl_t_hi, cpl_t_lo, sep_load[0]]
        if not first:
            operands += [cpl_hi, cpl_lo, sch_hi, sch_lo]
        operands += known
        solution, dense, part = call(
            functools.partial(leaf_kernel, width, first, last),
            "leaves",
            (
                shaped((leaves, order, loads)),
                shaped((2, chips, width, loads)),
                shaped((separator, loads)),
            ),
            [SM] * 3 + [VM] * (len(operands) - 3),
            [
                pltpu.VMEM((separator, loads), F32),
                pltpu.VMEM((order, 2 * loads), BF16),
                pltpu.VMEM((leaves * order, 2 * loads), BF16),
            ]
            + ([pltpu.VMEM((parts * width, loads), F32)] if first else []),
            limit=12,
            flops=8 * leaves * order * loads * (order + 2 * separator),
            moved=16 * MIB,
        )(*operands)

        def surface(pick):
            return call(
                functools.partial(surface_kernel, width),
                "surface",
                shaped((chips, width + share, loads)),
                [SM] * 2 + [VM] * (4 + len(pieces)),
                [pltpu.VMEM((columns, 2 * loads), BF16)],
                limit=8,
                flops=4 * rows * columns * loads,
                moved=6 * MIB,
            )(pick, group, bem_hi, bem_lo, *pieces, dense, part)

        swapped = lax.ppermute(surface(other_id), "sub", swap)
        payload = surface(mine_id) + swapped
        if first:
            payload, sch_hi, sch_lo = lax.optimization_barrier((payload, sch_hi, sch_lo))
        got = over_chips(payload)
        if not last:
            wide, field = call(
                functools.partial(total_kernel, width),
                "total",
                (shaped((chips, width + share, loads)), shaped((width, loads))),
                [VM] * 2,
                moved=2 * MIB,
            )(got, surf_load)
    pressure, sep_rows = call(
        functools.partial(final_kernel, width),
        "final",
        (shaped((width, loads)), shaped((share, loads))),
        [VM] * 2,
        moved=MIB,
    )(got, surf_load)
    return (solution[None], sep_rows[None], pressure)


def solution(mesh):
    return jax.shard_map(
        on_device,
        mesh=mesh,
        in_specs=(
            P("grp", "sub"),
            P("grp", "sub", None, None),
            P("grp", "sub", None, None),
            P("grp", None, "sub"),
            P("grp", "sub", None, None),
            P("grp", None, None),
            P(("grp", "sub"), None),
            P(("grp", "sub"), None),
            P("grp", "sub", None, None),
            P("grp", "sub", None, None),
            P("grp", "sub"),
            P("grp", "sub"),
            P("grp", "sub", None, None),
        ),
        out_specs=(P("grp", "sub", None, None), P("grp", "sub", None), P(("grp", "sub"), None)),
        check_vma=False,
    )
```

time: 277 us -> 186 us (0.67); the launches traced: 272 us -> 185 us
  matrix products: 82.9 us -> 0 us
  Pallas kernels: 0 us -> 31.4 us
  local copies, waits for them, and re-layouts: 31.3 us -> 9.12 us
  between operations: 15 us -> 0.96 us
  blocking collectives: 58.8 us -> 69.6 us
  other arithmetic: 11 us -> 5.05 us
  waiting for transfers between devices: 46.3 us -> 40.5 us
    dot_general x21 -> x0, matrix products: 82.9 us -> none  [mm(): jnp.einsum(spec, a, b, precision=PREC, preferred_element_type=jnp.float32)]
    all_to_all x5 -> x0, waiting for transfers between devices: 39.7 us -> none  [the longest x3 20 us: on_device(): lax.all_to_all(jnp.broadcast_to(pressure[None], (lax.axis_size('grp'), *p...]
    ppermute x6 -> x22, waiting for transfers between devices: 5.9 us -> 40.5 us  [the longest x17 39 us: doubled(): lax.ppermute(held, axis, [(i, i ^ step) for i in range(size)])]
    pallas_call x0 -> x16, Pallas kernels: none -> 31.4 us  [the longest x3 16.2 us: on_device(): call(functools.partial(leaf_kernel, width, first, last), 'leaves', (shape...]
    ppermute x6 -> x22, starting transfers between devices: 1.15 us -> 28.6 us  [the longest x17 28.3 us: doubled(): lax.ppermute(held, axis, [(i, i ^ step) for i in range(size)])]
    all_to_all x5 -> x0, starting transfers between devices: 25.8 us -> none  [the longest x3 18 us: on_device(): lax.all_to_all(jnp.broadcast_to(pressure[None], (lax.axis_size('grp'), *p...]
    all_to_all x4 -> x5, blocking collectives: 58.8 us -> 69.6 us  [over_chips(): lax.all_to_all(x, 'sub', 0, 0, axis_index_groups=same_core, tiled=True)]
    mul x7 -> x0, local copies, waits for them, and re-layouts: 5.01 us -> none  [the longest x3 2.93 us: on_device(): solution = mm('jrc,jcl->jrl', leaf_inverse[0], rhs * row_mask) * row_mask]
  transfers between devices with their start and end apart: 12 -> 22, of which waited for: 7 -> 13; matrix products, arithmetic and copies ran while one was open for 17% -> 3% of each run, Pallas kernels for 0% -> 15%
where the time goes in v1:
time: 186 us; the launch traced here: 185 us
  blocking collectives  69.6 us (37%)
  waiting for transfers between devices  40.5 us (22%)
  Pallas kernels  31.4 us (17%)
  starting transfers between devices  28.6 us (15%)
  local copies, waits for them, and re-layouts  9.12 us (5%)
  other arithmetic  5.05 us (3%)
    all_to_all x5, blocking collectives, over_chips(): lax.all_to_all(x, 'sub', 0, 0, axis_index_groups=same_core, tiled=True)  69.6 us
    ppermute x17, waiting for transfers between devices, doubled(): lax.ppermute(held, axis, [(i, i ^ step) for i in range(size)])  39 us
    ppermute x17, starting transfers between devices, doubled(): lax.ppermute(held, axis, [(i, i ^ step) for i in range(size)])  28.3 us
    pallas_call x3, Pallas kernels, on_device(): call(functools.partial(leaf_kernel, width, first, last), 'leaves', (shape...  16.2 us
    pallas_call x6, Pallas kernels, surface(): call(functools.partial(surface_kernel, width), 'surface', shaped((chips,...  8.01 us
    unnamed x19, local copies, waits for them, and re-layouts  7.36 us
    pallas_call x3, Pallas kernels, split_call(): call(body, name, tuple((shaped(s, BF16) for s in outs)), [AN], [pltpu.VME...  5.96 us
  transfers between devices with their start and end apart: 22, of which 13 were waited for; matrix products, arithmetic and copies ran while one was open for 3% of the time, Pallas kernels for 15%

profile of v1, /device:TPU:0, one launch (start us, length us, event | category | flops | bytes accessed | tf_op | source)
XLA Modules:
  0.0 185.1 jit_solution(9061814622472351634)
XLA Ops:
  0.6 2.1 %collective-permute-start.3 = (f32[128,128]{1,0:T(8,128)}, f32[128,128]{1,0:T(8,128)S(1)}, u32[]{:S(2)}, u32[]{:S(2)}) collective-permute-start(f32[128,128]{1,0:T(8,128)} %rest_0_.5), channel_id=1, source_target_pairs={{0,2},{1,3},{2,0},{3,1},{4,6},{5,7},{6,4},{7,5},{8,10},{9,11},{10,... | collective-permute-start | bytes 196616 | tf_op jit(solution)/shard_map/ppermute | solution.py:287
  2.7 3.6 %collective-permute-start = (f32[128,128]{1,0:T(8,128)}, f32[128,128]{1,0:T(8,128)S(1)}, u32[]{:S(2)}, u32[]{:S(2)}) collective-permute-start(f32[128,128]{1,0:T(8,128)} %rest_0_.5), channel_id=1, source_target_pairs={{0,64},{16,80},{32,96},{48,112},{64,0},{80,16},{96,32},{112,48},{1... | collective-permute-start | bytes 196616 | tf_op jit(solution)/shard_map/ppermute | solution.py:287
  6.3 3.4 %collective-permute-done.rest_1_ = f32[128,128]{1,0:T(8,128)S(1)} collective-permute-done((f32[128,128]{1,0:T(8,128)}, f32[128,128]{1,0:T(8,128)S(1)}, u32[]{:S(2)}, u32[]{:S(2)}) %collective-permute-start) | collective-permute-done | bytes 65568 | tf_op jit(solution)/shard_map/ppermute | solution.py:287
  13.7 1.9 %collective-permute-done.4.rest_2_ = f32[256,128]{1,0:T(8,128)S(1)} collective-permute-done((f32[256,128]{1,0:T(8,128)S(1)}, f32[256,128]{1,0:T(8,128)S(1)}, u32[]{:S(2)}, u32[]{:S(2)}) %collective-permute-start.4) | collective-permute-done | bytes 131104 | tf_op jit(solution)/shard_map/ppermute | solution.py:287
  18.1 2.3 %collective-permute-start.5 = (f32[512,128]{1,0:T(8,128)S(1)}, f32[512,128]{1,0:T(8,128)S(1)}, u32[]{:S(2)}, u32[]{:S(2)}) collective-permute-start(f32[512,128]{1,0:T(8,128)S(1)} %get-tuple-element.63), channel_id=1, source_target_pairs={{0,12},{1,13},{2,14},{3,15},{4,8},{5,9},{6,10},{7,11},{8,4},{9,5},... | collective-permute-start | bytes 786440 | tf_op jit(solution)/shard_map/ppermute | solution.py:287
  20.3 5.4 %collective-permute-done.5.rest_3_ = f32[512,128]{1,0:T(8,128)S(1)} collective-permute-done((f32[512,128]{1,0:T(8,128)S(1)}, f32[512,128]{1,0:T(8,128)S(1)}, u32[]{:S(2)}, u32[]{:S(2)}) %collective-permute-start.5) | collective-permute-done | bytes 262176 | tf_op jit(solution)/shard_map/ppermute | solution.py:287
  31.1 2.2 %copy-done.3 = f32[1,2,1024,512]{3,2,1,0:T(8,128)S(1)} copy-done((f32[1,2,1024,512]{3,2,1,0:T(8,128)S(1)}, f32[1,2,1024,512]{3,2,1,0:T(8,128)}, u32[]{:S(2)}) %copy-start.3) | copy-done | bytes 4194328
  33.2 2.1 %split_coupling.1 = (bf16[2048,512]{1,0:T(8,128)(2,1)S(1)}, bf16[2048,512]{1,0:T(8,128)(2,1)S(1)}, bf16[512,2048]{1,0:T(8,128)(2,1)S(1)}, bf16[512,2048]{1,0:T(8,128)(2,1)S(1)}) custom-call(f32[2048,512]{1,0:T(8,128)S(1)} %bitcast.26), custom_call_target="tpu_custom_call" | custom-call | bytes 4194304 | tf_op jit(solution)/shard_map/split_coupling/pallas_call | solution.py:112
  35.4 3.4 %copy-done = f32[2048,1024]{1,0:T(8,128)S(1)} copy-done((f32[2048,1024]{1,0:T(8,128)S(1)}, f32[2048,1024]{1,0:T(8,128)}, u32[]{:S(2)}) %copy-start) | copy-done | bytes 8388632
  38.8 2.1 %split_surface.1 = (bf16[2,1024,1024]{2,1,0:T(8,128)(2,1)S(1)}, bf16[2,1024,1024]{2,1,0:T(8,128)(2,1)S(1)}) custom-call(f32[2048,1024]{1,0:T(8,128)S(1)} %copy-done), custom_call_target="tpu_custom_call" | custom-call | bytes 8388608 | tf_op jit(solution)/shard_map/split_surface/pallas_call | solution.py:112
  42.2 1.7 split_leaf.1
  44.1 5.9 %collective-permute-done.9.rest_2_ = f32[64,512]{1,0:T(8,128)S(1)} collective-permute-done((f32[64,512]{1,0:T(8,128)S(1)}, f32[64,512]{1,0:T(8,128)S(1)}, u32[]{:S(2)}, u32[]{:S(2)}) %collective-permute-start.9) | collective-permute-done | bytes 131104 | tf_op jit(solution)/shard_map/ppermute | solution.py:287
  49.9 2.3 %collective-permute-start.10 = (f32[128,512]{1,0:T(8,128)S(1)}, f32[128,512]{1,0:T(8,128)S(1)}, u32[]{:S(2)}, u32[]{:S(2)}) collective-permute-start(f32[128,512]{1,0:T(8,128)S(1)} %pad_maximum_fusion.4), channel_id=1, source_target_pairs={{0,12},{1,13},{2,14},{3,15},{4,8},{5,9},{6,10},{7,11},{8,4},{9,5},... | collective-permute-start | bytes 786440 | tf_op jit(solution)/shard_map/ppermute | solution.py:287
  52.2 2.8 %collective-permute-start.2 = (f32[512,128]{1,0:T(8,128)S(1)}, f32[512,128]{1,0:T(8,128)S(1)}, u32[]{:S(2)}, u32[]{:S(2)}) collective-permute-start(f32[512,128]{1,0:T(8,128)S(1)} %get-tuple-element.64), channel_id=1, source_target_pairs={{0,48},{16,32},{32,16},{48,0},{64,112},{80,96},{96,80},{112,64},{1... | collective-permute-start | bytes 786440 | tf_op jit(solution)/shard_map/ppermute | solution.py:287
  55.0 4.3 %leaves.3 = (f32[2,1024,128]{2,1,0:T(8,128)}, f32[2,8,128,128]{3,2,1,0:T(8,128)S(1)}, f32[512,128]{1,0:T(8,128)S(1)}) custom-call(s32[1]{0:T(128)} %bitcast.here_ref, s32[16]{0:T(128)S(1)} %reshape.56.owner_ref, s32[2]{0:T(128)S(1)} %bitcast.35, f32[2,1024,128]{2,1,0:T(8,128)S(1)} %bitcast.23, f32[128,16]{1,0:T(8,128)S(1)} %get-tuple-element.68.flux_t, ...), custom_call_target="tpu_custom_call" | custom-call | flops 4294967296 | bytes 16777216 | tf_op jit(solution)/shard_map/leaves/pallas_call | solution.py:335
  59.3 1.8 collective-permute-done.2.rest_3_
  63.1 2.2 %collective-permute-done.11.rest_4_ = f32[256,512]{1,0:T(8,128)S(1)} collective-permute-done((f32[256,512]{1,0:T(8,128)S(1)}, f32[256,512]{1,0:T(8,128)S(1)}, u32[]{:S(2)}, u32[]{:S(2)}) %collective-permute-start.11) | collective-permute-done | bytes 524320 | tf_op jit(solution)/shard_map/ppermute | solution.py:287
  67.2 14.3 %all_to_all.25.got = f32[8,160,128]{2,1,0:T(8,128)S(1)} all-to-all(f32[8,160,128]{2,1,0:T(8,128)S(1)} %add.9), channel_id=1, replica_groups={{0,2,4,6,8,10,12,14},{1,3,5,7,9,11,13,15},{16,18,20,22,24,26,28,30},{17..., dimensions={0} | all-to-all | bytes 1310720 | tf_op jit(solution)/shard_map/all_to_all | solution.py:280
  81.6 13.5 %all_to_all.26.rest_4_ = f32[8,160,128]{2,1,0:T(8,128)S(1)} all-to-all(f32[8,160,128]{2,1,0:T(8,128)S(1)} %get-tuple-element.48), channel_id=1, replica_groups={{0,2,4,6,8,10,12,14},{1,3,5,7,9,11,13,15},{16,18,20,22,24,26,28,30},{17..., dimensions={0} | all-to-all | bytes 1310720 | tf_op jit(solution)/shard_map/all_to_all | solution.py:280
  95.0 2.6 %collective-permute-start.12 = (f32[128,128]{1,0:T(8,128)S(1)}, f32[128,128]{1,0:T(8,128)S(1)}, u32[]{:S(2)}, u32[]{:S(2)}) collective-permute-start(f32[128,128]{1,0:T(8,128)S(1)} %get-tuple-element.50.rest_0_), channel_id=1, source_target_pairs={{0,64},{16,80},{32,96},{48,112},{64,0},{80,16},{96,32},{112,48},{1... | collective-permute-start | bytes 196616 | tf_op jit(solution)/shard_map/ppermute | solution.py:287
  97.6 3.4 %collective-permute-done.12.rest_1_ = f32[128,128]{1,0:T(8,128)S(1)} collective-permute-done((f32[128,128]{1,0:T(8,128)S(1)}, f32[128,128]{1,0:T(8,128)S(1)}, u32[]{:S(2)}, u32[]{:S(2)}) %collective-permute-start.12) | collective-permute-done | bytes 65568 | tf_op jit(solution)/shard_map/ppermute | solution.py:287
  101.4 4.8 %collective-permute-done.13.rest_2_ = f32[256,128]{1,0:T(8,128)S(1)} collective-permute-done((f32[256,128]{1,0:T(8,128)S(1)}, f32[256,128]{1,0:T(8,128)S(1)}, u32[]{:S(2)}, u32[]{:S(2)}) %collective-permute-start.13) | collective-permute-done | bytes 131104 | tf_op jit(solution)/shard_map/ppermute | solution.py:287
  106.3 3.1 %collective-permute-start.14 = (f32[512,128]{1,0:T(8,128)S(1)}, f32[512,128]{1,0:T(8,128)S(1)}, u32[]{:S(2)}, u32[]{:S(2)}) collective-permute-start(f32[512,128]{1,0:T(8,128)S(1)} %pad_maximum_fusion.5), channel_id=1, source_target_pairs={{0,48},{16,32},{32,16},{48,0},{64,112},{80,96},{96,80},{112,64},{1... | collective-permute-start | bytes 786440 | tf_op jit(solution)/shard_map/ppermute | solution.py:287
  109.3 5.7 %leaves.4 = (f32[2,1024,128]{2,1,0:T(8,128)}, f32[2,8,128,128]{3,2,1,0:T(8,128)S(1)}, f32[512,128]{1,0:T(8,128)S(1)}) custom-call(s32[1]{0:T(128)} %bitcast.here_ref, s32[16]{0:T(128)S(1)} %reshape.56.owner_ref, s32[2]{0:T(128)S(1)} %bitcast.36, f32[2,1024,128]{2,1,0:T(8,128)S(1)} %bitcast.24, f32[128,16]{1,0:T(8,128)S(1)} %get-tuple-element.68.flux_t, ...), custom_call_target="tpu_custom_call" | custom-call | flops 4294967296 | bytes 16777216 | tf_op jit(solution)/shard_map/leaves/pallas_call | solution.py:335
  118.7 14.3 %all_to_all.27.got = f32[8,160,128]{2,1,0:T(8,128)S(1)} all-to-all(f32[8,160,128]{2,1,0:T(8,128)S(1)} %add.10), channel_id=1, replica_groups={{0,2,4,6,8,10,12,14},{1,3,5,7,9,11,13,15},{16,18,20,22,24,26,28,30},{17..., dimensions={0} | all-to-all | bytes 1310720 | tf_op jit(solution)/shard_map/all_to_all | solution.py:280
  133.1 13.2 %all_to_all.28.rest_4_ = f32[8,160,128]{2,1,0:T(8,128)S(1)} all-to-all(f32[8,160,128]{2,1,0:T(8,128)S(1)} %get-tuple-element.54), channel_id=1, replica_groups={{0,2,4,6,8,10,12,14},{1,3,5,7,9,11,13,15},{16,18,20,22,24,26,28,30},{17..., dimensions={0} | all-to-all | bytes 1310720 | tf_op jit(solution)/shard_map/all_to_all | solution.py:280
  146.3 2.6 %collective-permute-start.18 = (f32[128,128]{1,0:T(8,128)S(1)}, f32[128,128]{1,0:T(8,128)S(1)}, u32[]{:S(2)}, u32[]{:S(2)}) collective-permute-start(f32[128,128]{1,0:T(8,128)S(1)} %get-tuple-element.58.rest_0_), channel_id=1, source_target_pairs={{0,64},{16,80},{32,96},{48,112},{64,0},{80,16},{96,32},{112,48},{1... | collective-permute-start | bytes 196616 | tf_op jit(solution)/shard_map/ppermute | solution.py:287
  148.8 3.4 %collective-permute-done.18.rest_1_ = f32[128,128]{1,0:T(8,128)S(1)} collective-permute-done((f32[128,128]{1,0:T(8,128)S(1)}, f32[128,128]{1,0:T(8,128)S(1)}, u32[]{:S(2)}, u32[]{:S(2)}) %collective-permute-start.18) | collective-permute-done | bytes 65568 | tf_op jit(solution)/shard_map/ppermute | solution.py:287
  152.4 5.1 %collective-permute-done.19.rest_2_ = f32[256,128]{1,0:T(8,128)S(1)} collective-permute-done((f32[256,128]{1,0:T(8,128)S(1)}, f32[256,128]{1,0:T(8,128)S(1)}, u32[]{:S(2)}, u32[]{:S(2)}) %collective-permute-start.19) | collective-permute-done | bytes 131104 | tf_op jit(solution)/shard_map/ppermute | solution.py:287
  157.5 2.8 %collective-permute-start.20 = (f32[512,128]{1,0:T(8,128)S(1)}, f32[512,128]{1,0:T(8,128)S(1)}, u32[]{:S(2)}, u32[]{:S(2)}) collective-permute-start(f32[512,128]{1,0:T(8,128)S(1)} %pad_maximum_fusion.6), channel_id=1, source_target_pairs={{0,48},{16,32},{32,16},{48,0},{64,112},{80,96},{96,80},{112,64},{1... | collective-permute-start | bytes 786440 | tf_op jit(solution)/shard_map/ppermute | solution.py:287
  160.4 6.1 %leaves.5 = (f32[2,1024,128]{2,1,0:T(8,128)}, f32[2,8,128,128]{3,2,1,0:T(8,128)S(1)}, f32[512,128]{1,0:T(8,128)S(1)}) custom-call(s32[1]{0:T(128)} %bitcast.here_ref, s32[16]{0:T(128)S(1)} %reshape.56.owner_ref, s32[2]{0:T(128)S(1)} %bitcast.37, f32[2,1024,128]{2,1,0:T(8,128)S(1)} %bitcast.25, f32[128,16]{1,0:T(8,128)S(1)} %get-tuple-element.68.flux_t, ...), custom_call_target="tpu_custom_call" | custom-call | flops 4294967296 | bytes 16777216 | tf_op jit(solution)/shard_map/leaves/pallas_call | solution.py:335
  170.1 14.3 %all_to_all.29.got = f32[8,160,128]{2,1,0:T(8,128)S(1)} all-to-all(f32[8,160,128]{2,1,0:T(8,128)S(1)} %add.11), channel_id=1, replica_groups={{0,2,4,6,8,10,12,14},{1,3,5,7,9,11,13,15},{16,18,20,22,24,26,28,30},{17..., dimensions={0} | all-to-all | bytes 1310720 | tf_op jit(solution)/shard_map/all_to_all | solution.py:280
  (72 shorter events, 25.5 us)
Async XLA Ops:
  0.6 5.7 %collective-permute-start.3 = (f32[128,128]{1,0:T(8,128)}, f32[128,128]{1,0:T(8,128)S(1)}, u32[]{:S(2)}, u32[]{:S(2)}) collective-permute-start(f32[128,128]{1,0:T(8,128)} %rest_0_.5), channel_id=1, source_target_pairs={{0,2},{1,3},{2,0},{3,1},{4,6},{5,7},{6,4},{7,5},{8,10},{9,11},{10,... | collective-permute-start | bytes 196616 | tf_op jit(solution)/shard_map/ppermute | solution.py:287
  2.7 7.0 %collective-permute-start = (f32[128,128]{1,0:T(8,128)}, f32[128,128]{1,0:T(8,128)S(1)}, u32[]{:S(2)}, u32[]{:S(2)}) collective-permute-start(f32[128,128]{1,0:T(8,128)} %rest_0_.5), channel_id=1, source_target_pairs={{0,64},{16,80},{32,96},{48,112},{64,0},{80,16},{96,32},{112,48},{1... | collective-permute-start | bytes 196616 | tf_op jit(solution)/shard_map/ppermute | solution.py:287
  10.6 5.0 %collective-permute-start.4 = (f32[256,128]{1,0:T(8,128)S(1)}, f32[256,128]{1,0:T(8,128)S(1)}, u32[]{:S(2)}, u32[]{:S(2)}) collective-permute-start(f32[256,128]{1,0:T(8,128)S(1)} %get-tuple-element.65), channel_id=1, source_target_pairs={{0,4},{1,5},{2,6},{3,7},{4,0},{5,1},{6,2},{7,3},{8,12},{9,13},{10,... | collective-permute-start | bytes 393224 | tf_op jit(solution)/shard_map/ppermute | solution.py:287
  12.2 5.0 %collective-permute-start.1 = (f32[256,128]{1,0:T(8,128)S(1)}, f32[256,128]{1,0:T(8,128)S(1)}, u32[]{:S(2)}, u32[]{:S(2)}) collective-permute-start(f32[256,128]{1,0:T(8,128)S(1)} %get-tuple-element.66), channel_id=1, source_target_pairs={{0,16},{16,0},{32,48},{48,32},{64,80},{80,64},{96,112},{112,96},{1... | collective-permute-start | bytes 393224 | tf_op jit(solution)/shard_map/ppermute | solution.py:287
  18.1 7.7 %collective-permute-start.5 = (f32[512,128]{1,0:T(8,128)S(1)}, f32[512,128]{1,0:T(8,128)S(1)}, u32[]{:S(2)}, u32[]{:S(2)}) collective-permute-start(f32[512,128]{1,0:T(8,128)S(1)} %get-tuple-element.63), channel_id=1, source_target_pairs={{0,12},{1,13},{2,14},{3,15},{4,8},{5,9},{6,10},{7,11},{8,4},{9,5},... | collective-permute-start | bytes 786440 | tf_op jit(solution)/shard_map/ppermute | solution.py:287
  20.3 23.6 %collective-permute-start.8 = (f32[32,512]{1,0:T(8,128)}, f32[32,512]{1,0:T(8,128)S(1)}, u32[]{:S(2)}, u32[]{:S(2)}) collective-permute-start(f32[32,512]{1,0:T(8,128)} %bitcast.30), channel_id=1, source_target_pairs={{0,2},{1,3},{2,0},{3,1},{4,6},{5,7},{6,4},{7,5},{8,10},{9,11},{10,... | collective-permute-start | bytes 196616 | tf_op jit(solution)/shard_map/ppermute | solution.py:287
  26.6 28.3 %collective-permute-start.6 = (f32[1024,128]{1,0:T(8,128)S(1)}, f32[1024,128]{1,0:T(8,128)S(1)}, u32[]{:S(2)}, u32[]{:S(2)}) collective-permute-start(f32[1024,128]{1,0:T(8,128)S(1)} %pad_maximum_fusion), channel_id=1, source_target_pairs={{0,1},{1,0},{2,3},{3,2},{4,5},{5,4},{6,7},{7,6},{8,9},{9,8},{10,11... | collective-permute-start | bytes 1572872 | tf_op jit(solution)/shard_map/ppermute | solution.py:287
  31.0 2.2 %copy-start.3 = (f32[1,2,1024,512]{3,2,1,0:T(8,128)S(1)}, f32[1,2,1024,512]{3,2,1,0:T(8,128)}, u32[]{:S(2)}) copy-start(f32[1,2,1024,512]{3,2,1,0:T(8,128)} %param.15) | copy-start | bytes 12582916
  35.4 3.4 %copy-start = (f32[2048,1024]{1,0:T(8,128)S(1)}, f32[2048,1024]{1,0:T(8,128)}, u32[]{:S(2)}) copy-start(f32[2048,1024]{1,0:T(8,128)} %src.1) | copy-start | bytes 25165828
  38.8 3.4 %copy-start.1 = (f32[1,2,1024,1024]{3,2,1,0:T(8,128)S(1)}, f32[1,2,1024,1024]{3,2,1,0:T(8,128)}, u32[]{:S(2)}) copy-start(f32[1,2,1024,1024]{3,2,1,0:T(8,128)} %param.14) | copy-start | bytes 25165828
  42.1 1.8 copy-start.6
  42.1 12.8 %copy-start.2 = (f32[1,2,1024,128]{3,2,1,0:T(8,128)S(1)}, f32[1,2,1024,128]{3,2,1,0:T(8,128)}, u32[]{:S(2)}) copy-start(f32[1,2,1024,128]{3,2,1,0:T(8,128)} %param.17) | copy-start | bytes 3145732
  42.1 12.8 %copy-start.4 = (f32[128,128]{1,0:T(8,128)S(1)}, f32[128,128]{1,0:T(8,128)}, u32[]{:S(2)}) copy-start(f32[128,128]{1,0:T(8,128)} %rest_0_.5) | copy-start | bytes 196612
  42.1 12.8 %copy-start.5 = (f32[1,512,128]{2,1,0:T(8,128)S(1)}, f32[1,512,128]{2,1,0:T(8,128)}, u32[]{:S(2)}) copy-start(f32[1,512,128]{2,1,0:T(8,128)} %param.18) | copy-start | bytes 786436
  42.1 12.8 %copy-start.8 = (s32[1,2]{1,0:T(1,128)S(1)}, s32[1,2]{1,0:T(1,128)}, u32[]{:S(2)}) copy-start(s32[1,2]{1,0:T(1,128)} %param.23) | copy-start | bytes 28
  43.9 6.0 %collective-permute-start.9 = (f32[64,512]{1,0:T(8,128)S(1)}, f32[64,512]{1,0:T(8,128)S(1)}, u32[]{:S(2)}, u32[]{:S(2)}) collective-permute-start(f32[64,512]{1,0:T(8,128)S(1)} %pad_maximum_fusion.9), channel_id=1, source_target_pairs={{0,4},{1,5},{2,6},{3,7},{4,0},{5,1},{6,2},{7,3},{8,12},{9,13},{10,... | collective-permute-start | bytes 393224 | tf_op jit(solution)/shard_map/ppermute | solution.py:287
  49.9 12.6 %collective-permute-start.10 = (f32[128,512]{1,0:T(8,128)S(1)}, f32[128,512]{1,0:T(8,128)S(1)}, u32[]{:S(2)}, u32[]{:S(2)}) collective-permute-start(f32[128,512]{1,0:T(8,128)S(1)} %pad_maximum_fusion.4), channel_id=1, source_target_pairs={{0,12},{1,13},{2,14},{3,15},{4,8},{5,9},{6,10},{7,11},{8,4},{9,5},... | collective-permute-start | bytes 786440 | tf_op jit(solution)/shard_map/ppermute | solution.py:287
  52.2 8.9 %collective-permute-start.2 = (f32[512,128]{1,0:T(8,128)S(1)}, f32[512,128]{1,0:T(8,128)S(1)}, u32[]{:S(2)}, u32[]{:S(2)}) collective-permute-start(f32[512,128]{1,0:T(8,128)S(1)} %get-tuple-element.64), channel_id=1, source_target_pairs={{0,48},{16,32},{32,16},{48,0},{64,112},{80,96},{96,80},{112,64},{1... | collective-permute-start | bytes 786440 | tf_op jit(solution)/shard_map/ppermute | solution.py:287
  62.4 4.7 %collective-permute-start.7 = (f32[8,160,128]{2,1,0:T(8,128)S(1)}, f32[8,160,128]{2,1,0:T(8,128)S(1)}, u32[]{:S(2)}, u32[]{:S(2)}) collective-permute-start(f32[8,160,128]{2,1,0:T(8,128)S(1)} %surface.7), channel_id=1, source_target_pairs={{0,1},{1,0},{2,3},{3,2},{4,5},{5,4},{6,7},{7,6},{8,9},{9,8},{10,11... | collective-permute-start | bytes 1966088 | tf_op jit(solution)/shard_map/ppermute | solution.py:367
  62.5 2.8 %collective-permute-start.11 = (f32[256,512]{1,0:T(8,128)S(1)}, f32[256,512]{1,0:T(8,128)S(1)}, u32[]{:S(2)}, u32[]{:S(2)}) collective-permute-start(f32[256,512]{1,0:T(8,128)S(1)} %pad_maximum_fusion.1), channel_id=1, source_target_pairs={{0,1},{1,0},{2,3},{3,2},{4,5},{5,4},{6,7},{7,6},{8,9},{9,8},{10,11... | collective-permute-start | bytes 1572872 | tf_op jit(solution)/shard_map/ppermute | solution.py:287
  65.7 15.8 %copy-start.7 = (f32[128,128]{1,0:T(8,128)S(1)}, f32[128,128]{1,0:T(8,128)}, u32[]{:S(2)}) copy-start(f32[128,128]{1,0:T(8,128)} %load.5) | copy-start | bytes 196612
  95.0 14.3 %collective-permute-start.15 = (f32[8,160,128]{2,1,0:T(8,128)S(1)}, f32[8,160,128]{2,1,0:T(8,128)S(1)}, u32[]{:S(2)}, u32[]{:S(2)}) collective-permute-start(f32[8,160,128]{2,1,0:T(8,128)S(1)} %all_to_all.26.rest_4_), channel_id=1, source_target_pairs={{0,1},{1,0},{2,3},{3,2},{4,5},{5,4},{6,7},{7,6},{8,9},{9,8},{10,11... | collective-permute-start | bytes 1966088 | tf_op jit(solution)/shard_map/ppermute | solution.py:320
  95.0 6.0 %collective-permute-start.12 = (f32[128,128]{1,0:T(8,128)S(1)}, f32[128,128]{1,0:T(8,128)S(1)}, u32[]{:S(2)}, u32[]{:S(2)}) collective-permute-start(f32[128,128]{1,0:T(8,128)S(1)} %get-tuple-element.50.rest_0_), channel_id=1, source_target_pairs={{0,64},{16,80},{32,96},{48,112},{64,0},{80,16},{96,32},{112,48},{1... | collective-permute-start | bytes 196616 | tf_op jit(solution)/shard_map/ppermute | solution.py:287
  101.1 5.2 %collective-permute-start.13 = (f32[256,128]{1,0:T(8,128)S(1)}, f32[256,128]{1,0:T(8,128)S(1)}, u32[]{:S(2)}, u32[]{:S(2)}) collective-permute-start(f32[256,128]{1,0:T(8,128)S(1)} %pad_maximum_fusion.10), channel_id=1, source_target_pairs={{0,16},{16,0},{32,48},{48,32},{64,80},{80,64},{96,112},{112,96},{1... | collective-permute-start | bytes 393224 | tf_op jit(solution)/shard_map/ppermute | solution.py:287
  106.3 8.8 %collective-permute-start.14 = (f32[512,128]{1,0:T(8,128)S(1)}, f32[512,128]{1,0:T(8,128)S(1)}, u32[]{:S(2)}, u32[]{:S(2)}) collective-permute-start(f32[512,128]{1,0:T(8,128)S(1)} %pad_maximum_fusion.5), channel_id=1, source_target_pairs={{0,48},{16,32},{32,16},{48,0},{64,112},{80,96},{96,80},{112,64},{1... | collective-permute-start | bytes 786440 | tf_op jit(solution)/shard_map/ppermute | solution.py:287
  116.5 2.2 %collective-permute-start.16 = (f32[8,160,128]{2,1,0:T(8,128)S(1)}, f32[8,160,128]{2,1,0:T(8,128)S(1)}, u32[]{:S(2)}, u32[]{:S(2)}) collective-permute-start(f32[8,160,128]{2,1,0:T(8,128)S(1)} %surface.9), channel_id=1, source_target_pairs={{0,1},{1,0},{2,3},{3,2},{4,5},{5,4},{6,7},{7,6},{8,9},{9,8},{10,11... | collective-permute-start | bytes 1966088 | tf_op jit(solution)/shard_map/ppermute | solution.py:367
  146.3 14.1 %collective-permute-start.17 = (f32[8,160,128]{2,1,0:T(8,128)S(1)}, f32[8,160,128]{2,1,0:T(8,128)S(1)}, u32[]{:S(2)}, u32[]{:S(2)}) collective-permute-start(f32[8,160,128]{2,1,0:T(8,128)S(1)} %all_to_all.28.rest_4_), channel_id=1, source_target_pairs={{0,1},{1,0},{2,3},{3,2},{4,5},{5,4},{6,7},{7,6},{8,9},{9,8},{10,11... | collective-permute-start | bytes 1966088 | tf_op jit(solution)/shard_map/ppermute | solution.py:320
  146.3 6.0 %collective-permute-start.18 = (f32[128,128]{1,0:T(8,128)S(1)}, f32[128,128]{1,0:T(8,128)S(1)}, u32[]{:S(2)}, u32[]{:S(2)}) collective-permute-start(f32[128,128]{1,0:T(8,128)S(1)} %get-tuple-element.58.rest_0_), channel_id=1, source_target_pairs={{0,64},{16,80},{32,96},{48,112},{64,0},{80,16},{96,32},{112,48},{1... | collective-permute-start | bytes 196616 | tf_op jit(solution)/shard_map/ppermute | solution.py:287
  152.3 5.2 %collective-permute-start.19 = (f32[256,128]{1,0:T(8,128)S(1)}, f32[256,128]{1,0:T(8,128)S(1)}, u32[]{:S(2)}, u32[]{:S(2)}) collective-permute-start(f32[256,128]{1,0:T(8,128)S(1)} %pad_maximum_fusion.11), channel_id=1, source_target_pairs={{0,16},{16,0},{32,48},{48,32},{64,80},{80,64},{96,112},{112,96},{1... | collective-permute-start | bytes 393224 | tf_op jit(solution)/shard_map/ppermute | solution.py:287
  157.5 9.0 %collective-permute-start.20 = (f32[512,128]{1,0:T(8,128)S(1)}, f32[512,128]{1,0:T(8,128)S(1)}, u32[]{:S(2)}, u32[]{:S(2)}) collective-permute-start(f32[512,128]{1,0:T(8,128)S(1)} %pad_maximum_fusion.6), channel_id=1, source_target_pairs={{0,48},{16,32},{32,16},{48,0},{64,112},{80,96},{96,80},{112,64},{1... | collective-permute-start | bytes 786440 | tf_op jit(solution)/shard_map/ppermute | solution.py:287
  167.8 2.2 %collective-permute-start.21 = (f32[8,160,128]{2,1,0:T(8,128)S(1)}, f32[8,160,128]{2,1,0:T(8,128)S(1)}, u32[]{:S(2)}, u32[]{:S(2)}) collective-permute-start(f32[8,160,128]{2,1,0:T(8,128)S(1)} %surface.11), channel_id=1, source_target_pairs={{0,1},{1,0},{2,3},{3,2},{4,5},{5,4},{6,7},{7,6},{8,9},{9,8},{10,11... | collective-permute-start | bytes 1966088 | tf_op jit(solution)/shard_map/ppermute | solution.py:367

commit v2 on v1

--- a/solution.py
+++ b/solution.py
@@ -16,7 +16,6 @@
 
 
 GRP_STEPS = (4, 1, 3)
-SUB_STEPS = (2, 4, 12, 1)
 
 
 def origins(steps):
@@ -78,7 +77,7 @@
             copy(i + slots, i % slots).start()
 
 
-def split_rows(tile, src, hi_ref, lo_ref, buf, sems):
+def split_rows(tile, token, src, hi_ref, lo_ref, buf, sems):
     def use(i, x):
         rows = slice(i * tile, (i + 1) * tile)
         hi_ref[rows], lo_ref[rows] = parted(x)
@@ -86,7 +85,7 @@
     streamed(src, buf, sems, tile, use)
 
 
-def split_cores(tile, width, src, hi_ref, lo_ref, buf, sems):
+def split_cores(tile, width, token, src, hi_ref, lo_ref, buf, sems):
     def use(i, x):
         for b in range(tile // width):
             block = i * (tile // width) + b
@@ -98,7 +97,7 @@
     streamed(src, buf, sems, tile, use)
 
 
-def split_turned(tile, src, hi_ref, lo_ref, hi_t_ref, lo_t_ref, buf, sems):
+def split_turned(tile, token, src, hi_ref, lo_ref, hi_t_ref, lo_t_ref, buf, sems):
     def use(i, x):
         rows = slice(i * tile, (i + 1) * tile)
         hi_ref[rows], lo_ref[rows] = parted(x)
@@ -107,63 +106,68 @@
     streamed(src, buf, sems, tile, use)
 
 
-def split_call(x, body, name, outs, tile):
+def split_call(token, x, body, name, outs, tile):
     slots = 4
     return call(
         body,
         name,
         tuple(shaped(s, BF16) for s in outs),
-        [AN],
+        [SM, AN],
         [pltpu.VMEM((slots, tile, x.shape[1]), F32), pltpu.SemaphoreType.DMA((slots,))],
         limit=8,
         moved=4 * x.size,
-    )(x)
-
-
-def laid(pieces, steps, here, whole):
-    rows = pieces[0].shape[0]
-    block = 0
-    for piece in pieces:
-        for i in range(piece.shape[0] // rows):
-            at = pl.multiple_of((here ^ origins(steps)[block]) * rows, rows)
-            whole[pl.ds(at, rows)] = piece[i * rows : (i + 1) * rows]
-            block += 1
-
-
-def turn_kernel(here_ref, *rest):
-    *pieces, hi_ref, lo_ref, whole = rest
-    laid(pieces, SUB_STEPS, here_ref[0], whole)
+    )(token, x)
+
+
+def start_kernel(width, field, schur_t, wide):
+    share, columns = schur_t.shape
+    for chip in range(wide.shape[0]):
+        wide[chip, :width] = field[...]
+        for q in range(columns // width):
+            rows = slice(width + q * share, width + (q + 1) * share)
+            wide[chip, rows] = schur_t[:, q * width : (q + 1) * width]
+
+
+def turn_kernel(width, core_ref, mine, other, hi_ref, lo_ref, whole):
+    chips = mine.shape[0]
+    columns = whole.shape[1]
+    share = whole.shape[0] // (2 * chips)
+    core = core_ref[0]
+    for chip in range(chips):
+        at = 2 * chip * share
+        for q in range(columns // width):
+            rows = slice(width + q * share, width + (q + 1) * share)
+            to = slice(q * width, (q + 1) * width)
+            a, b = mine[chip, rows], other[chip, rows]
+            whole[at : at + share, to] = jnp.where(core == 0, a, b)
+            whole[at + share : at + 2 * share, to] = jnp.where(core == 0, b, a)
     hi_ref[...], lo_ref[...] = parted(whole[...].T)
 
 
 def leaf_kernel(
     width, first, last,
-    here_ref, owner_ref, size_ref,
-    load, flux_t, trace_t, inv_hi, inv_lo, cpl_t_hi, cpl_t_lo, sep_load,
+    here_ref, owner_ref, size_ref, count_ref,
+    load, flux_weight, trace_weight, inv_hi, inv_lo, cpl_t_hi, cpl_t_lo, sep_load, mine, other,
     *rest,
 ):
-    if first:
-        *rest, field = rest
-    *rest, sol, dense, part, gathered, wide, wide_sol = rest
+    if not first:
+        cpl_hi, cpl_lo, sch_hi, sch_lo, *rest = rest
+    sol, dense, part, gathered, wide, wide_sol = rest
     leaves, order, loads = load.shape
     blocks = order // width
     chips = dense.shape[1]
     share = part.shape[0] // (2 * chips)
     here = here_ref[0]
     core = here % 2
-
-    if first:
-        laid(rest, SUB_STEPS, here, field)
-
-        def surface(o):
-            return field[pl.ds(pl.multiple_of(o * width, width), width)]
-
-    else:
-        cpl_hi, cpl_lo, sch_hi, sch_lo, mine, other = rest
-
-        def surface(o):
-            chip = o // 2
-            return jnp.where(o - 2 * chip == core, mine[chip, :width], other[chip, :width])
+    flux_t, trace_t = flux_weight[...].T, trace_weight[...].T
+
+    def scale(turned, j, k):
+        e = j * blocks + k
+        return jnp.where(k < count_ref[0, j], turned[:, e : e + 1], 0.0)
+
+    def surface(o):
+        chip = o // 2
+        return jnp.where(o - 2 * chip == core, mine[chip, :width], other[chip, :width])
 
     if not first:
         for chip in range(chips):
@@ -178,24 +182,22 @@
         if not first:
             pulled = product(cpl_hi[rows], cpl_lo[rows], sep_wide)
         for k in range(blocks):
-            e = j * blocks + k
-            o = owner_ref[e]
+            o = owner_ref[j * blocks + k]
             at = slice(k * width, (k + 1) * width)
-            rhs = load[j, at] - surface(o) * flux_t[:, e : e + 1]
+            rhs = load[j, at] - surface(o) * scale(flux_t, j, k)
             if not first:
                 rhs = rhs - pulled[at]
             row = k * width + lax.broadcasted_iota(jnp.int32, (width, loads), 0)
-            wide[at] = widened(jnp.where(row < size_ref[j], rhs, 0.0))
+            wide[at] = widened(jnp.where(row < size_ref[0, j], rhs, 0.0))
         got = product(inv_hi[rows], inv_lo[rows], wide[...])
         for k in range(blocks):
-            e = j * blocks + k
-            o = owner_ref[e]
+            o = owner_ref[j * blocks + k]
             chip = o // 2
             at = slice(k * width, (k + 1) * width)
             row = k * width + lax.broadcasted_iota(jnp.int32, (width, loads), 0)
-            block = jnp.where(row < size_ref[j], got[at], 0.0)
+            block = jnp.where(row < size_ref[0, j], got[at], 0.0)
             sol[j, at] = block
-            dense[o - 2 * chip, chip] += block * trace_t[:, e : e + 1]
+            dense[o - 2 * chip, chip] += block * scale(trace_t, j, k)
             wide_sol[j * order + k * width : j * order + (k + 1) * width] = widened(block)
     left = jnp.where(here == 0, sep_load[...], 0.0) - product(
         cpl_t_hi[...], cpl_t_lo[...], wide_sol[...]
@@ -223,24 +225,27 @@
         out[chip, width:] = part[pl.ds(at, share)]
 
 
-def total_kernel(width, got, load, wide, again):
-    chips = got.shape[0]
-    total = got[0]
-    for chip in range(1, chips):
-        total = total + got[chip]
-    field = load[...] + total[:width]
-    for chip in range(chips):
-        wide[chip, :width] = field
-        wide[chip, width:] = total[width:]
-    again[...] = field
+def summed(got, rows):
+    total = got[0, rows]
+    for chip in range(1, got.shape[0]):
+        total = total + got[chip, rows]
+    return total
+
+
+def field_kernel(width, got, load, field):
+    field[...] = load[...] + summed(got, slice(0, width))
+
+
+def wide_kernel(width, got, field, wide):
+    rest = summed(got, slice(width, None))
+    for chip in range(wide.shape[0]):
+        wide[chip, :width] = field[...]
+        wide[chip, width:] = rest
 
 
 def final_kernel(width, got, load, field, separator):
-    total = got[0]
-    for chip in range(1, got.shape[0]):
-        total = total + got[chip]
-    field[...] = load[...] + total[:width]
-    separator[...] = total[width:]
+    field[...] = load[...] + summed(got, slice(0, width))
+    separator[...] = summed(got, slice(width, None))
 
 
 def on_device(
@@ -259,6 +264,7 @@
     block_owner,
 ):
     parts = lax.axis_size("sub")
+    groups = lax.axis_size("grp")
     here = lax.axis_index("sub")
     core = lax.rem(here, 2).astype(jnp.int32)
     mine_id, other_id = core.reshape(1), (1 - core).reshape(1)
@@ -279,59 +285,61 @@
     def over_chips(x):
         return lax.all_to_all(x, "sub", 0, 0, axis_index_groups=same_core, tiled=True)
 
-    def doubled(x, axis, steps):
-        size = lax.axis_size(axis)
-        pieces = [x]
-        for step in steps:
-            held = pieces[0] if len(pieces) == 1 else jnp.concatenate(pieces, axis=0)
-            pieces.append(lax.ppermute(held, axis, [(i, i ^ step) for i in range(size)]))
-        return pieces
+    def more(pieces, step):
+        held = jnp.concatenate(pieces, axis=0) if len(pieces) > 1 else pieces[0]
+        return [*pieces, lax.ppermute(held, "grp", [(i, i ^ step) for i in range(groups)])]
 
     inv = leaf_inverse.reshape(leaves * order, order)
     cpl = coupling.reshape(leaves * order, separator)
-    inv_hi, inv_lo = split_call(
-        inv, functools.partial(split_rows, 256), "split_leaf", [inv.shape] * 2, 256
+    field = surf_start
+    wide = call(
+        functools.partial(start_kernel, width),
+        "start",
+        shaped((chips, 2 * width, loads)),
+        [VM] * 2,
+        moved=MIB,
+    )(surf_start, schur_inverse[0].T)
+    wide, here_id, mine_id, other_id, group, owner = lax.optimization_barrier(
+        (wide, here_id, mine_id, other_id, group, block_owner.reshape(entries))
     )
-    cpl_hi, cpl_lo, cpl_t_hi, cpl_t_lo = split_call(
-        cpl, functools.partial(split_turned, 256), "split_coupling",
-        [cpl.shape] * 2 + [cpl.shape[::-1]] * 2, 256,
-    )
-    bem_hi, bem_lo = split_call(
-        bem_tiles, functools.partial(split_cores, 2 * width, width), "split_surface",
-        [(2, rows // 2, columns)] * 2, 2 * width,
-    )
-    active = (
-        (jnp.arange(blocks, dtype=jnp.int32)[None, :] < block_counts[0][:, None])
-        .astype(F32)
-        .reshape(entries, 1)
-    )
-    owner = block_owner.reshape(entries)
-    sizes = leaf_sizes.reshape(leaves)
-    flux_t = (flux_weight.reshape(entries, width) * active).T
-    trace_t = (trace_weight.reshape(entries, width) * active).T
-    field = surf_start
     for sweep in range(SWEEPS):
         first, last = sweep == 0, sweep == SWEEPS - 1
+        pieces = [field]
         if first:
-            known = doubled(surf_start, "sub", SUB_STEPS)
+            mine = over_chips(wide)
         else:
+            pieces = more(pieces, GRP_STEPS[0])
+            wide, *pieces = lax.optimization_barrier((wide, *pieces))
             mine = over_chips(wide)
-            mine, field = lax.optimization_barrier((mine, field))
-            known = [mine, lax.ppermute(mine, "sub", swap)]
-        pieces = doubled(field, "grp", GRP_STEPS)
+        mine, token, *pieces = lax.optimization_barrier((mine, here_id, *pieces))
+        for step in GRP_STEPS[len(pieces) - 1 :]:
+            pieces = more(pieces, step)
+        other = lax.ppermute(mine, "sub", swap)
         if first:
-            schur_pieces = doubled(schur_inverse[0].T, "sub", SUB_STEPS)
+            inv_hi, inv_lo = split_call(
+                token, inv, functools.partial(split_rows, 256), "split_leaf", [inv.shape] * 2, 256
+            )
+            cpl_hi, cpl_lo, cpl_t_hi, cpl_t_lo = split_call(
+                token, cpl, functools.partial(split_turned, 256), "split_coupling",
+                [cpl.shape] * 2 + [cpl.shape[::-1]] * 2, 256,
+            )
+            bem_hi, bem_lo = split_call(
+                token, bem_tiles, functools.partial(split_cores, 2 * width, width),
+                "split_surface", [(2, rows // 2, columns)] * 2, 2 * width,
+            )
             sch_hi, sch_lo = call(
-                turn_kernel, "split_schur", (shaped((separator, separator), BF16),) * 2,
-                [SM] + [VM] * len(schur_pieces),
+                functools.partial(turn_kernel, width),
+                "split_schur",
+                (shaped((separator, separator), BF16),) * 2,
+                [SM] + [VM] * 2,
                 [pltpu.VMEM((separator, separator), F32)],
                 moved=8 * separator * separator,
-            )(here_id, *schur_pieces)
-        operands = [here_id, owner, sizes, leaf_load[0], flux_t, trace_t]
-        operands += [inv_hi, inv_lo, cpl_t_hi, cpl_t_lo, sep_load[0]]
+            )(mine_id, mine, other)
+        operands = [here_id, owner, leaf_sizes, block_counts, leaf_load[0]]
+        operands += [w.reshape(entries, width) for w in (flux_weight, trace_weight)]
+        operands += [inv_hi, inv_lo, cpl_t_hi, cpl_t_lo, sep_load[0], mine, other]
         if not first:
             operands += [cpl_hi, cpl_lo, sch_hi, sch_lo]
-        operands += known
         solution, dense, part = call(
             functools.partial(leaf_kernel, width, first, last),
             "leaves",
@@ -340,13 +348,12 @@
                 shaped((2, chips, width, loads)),
                 shaped((separator, loads)),
             ),
-            [SM] * 3 + [VM] * (len(operands) - 3),
+            [SM] * 4 + [VM] * (len(operands) - 4),
             [
                 pltpu.VMEM((separator, loads), F32),
                 pltpu.VMEM((order, 2 * loads), BF16),
                 pltpu.VMEM((leaves * order, 2 * loads), BF16),
-            ]
-            + ([pltpu.VMEM((parts * width, loads), F32)] if first else []),
+            ],
             limit=12,
             flops=8 * leaves * order * loads * (order + 2 * separator),
             moved=16 * MIB,
@@ -370,13 +377,17 @@
             payload, sch_hi, sch_lo = lax.optimization_barrier((payload, sch_hi, sch_lo))
         got = over_chips(payload)
         if not last:
-            wide, field = call(
-                functools.partial(total_kernel, width),
-                "total",
-                (shaped((chips, width + share, loads)), shaped((width, loads))),
+            field = call(
+                functools.partial(field_kernel, width), "field", shaped((width, loads)), [VM] * 2,
+                moved=MIB,
+            )(got, surf_load)
+            wide = call(
+                functools.partial(wide_kernel, width),
+                "wide",
+                shaped((chips, width + share, loads)),
                 [VM] * 2,
                 moved=2 * MIB,
-            )(got, surf_load)
+            )(got, field)
     pressure, sep_rows = call(
         functools.partial(final_kernel, width),
         "final",

time: 186 us -> 177 us (0.952)
  blocking collectives: 69.6 us -> 88.3 us
  waiting for transfers between devices: 40.5 us -> 26.1 us
  starting transfers between devices: 28.6 us -> 19.4 us
  other arithmetic: 5.05 us -> 2.47 us
    all_to_all x5 -> x6, blocking collectives: 69.6 us -> 88.3 us  [over_chips(): lax.all_to_all(x, 'sub', 0, 0, axis_index_groups=same_core, tiled=True)]
    ppermute x19 -> x12, waiting for transfers between devices: 39 us -> 24.2 us  [the longest x9 24.2 us: more(): lax.ppermute(held, 'grp', [(i, i ^ step) for i in range(groups)])]
    ppermute x19 -> x12, starting transfers between devices: 28.3 us -> 18.9 us  [the longest x9 18.9 us: more(): lax.ppermute(held, 'grp', [(i, i ^ step) for i in range(groups)])]
    unnamed x19 -> x29, local copies, waits for them, and re-layouts: 7.36 us -> 8.24 us
    pallas_call x6 -> x9, Pallas kernels: 6.5 us -> 6.52 us  [the longest x3 5.96 us: split_call(): call(body, name, tuple((shaped(s, BF16) for s in outs)), [SM, AN], [pltpu...]
  transfers between devices with their start and end apart: 22 -> 15, of which waited for: 13 -> 11; matrix products, arithmetic and copies ran while one was open for 3% -> 1% of each run, Pallas kernels for 15% -> 15%
where the time goes in v2:
time: 177 us
  blocking collectives  88.3 us (50%)
  Pallas kernels  31.2 us (18%)
  waiting for transfers between devices  26.1 us (15%)
  starting transfers between devices  19.4 us (11%)
  local copies, waits for them, and re-layouts  8.33 us (5%)
  other arithmetic  2.47 us (1%)
    all_to_all x6, blocking collectives, over_chips(): lax.all_to_all(x, 'sub', 0, 0, axis_index_groups=same_core, tiled=True)  88.3 us
    ppermute x9, waiting for transfers between devices, more(): lax.ppermute(held, 'grp', [(i, i ^ step) for i in range(groups)])  24.2 us
    ppermute x9, starting transfers between devices, more(): lax.ppermute(held, 'grp', [(i, i ^ step) for i in range(groups)])  18.9 us
    pallas_call x3, Pallas kernels, on_device(): call(functools.partial(leaf_kernel, width, first, last), 'leaves', (shape...  16.1 us
    unnamed x29, local copies, waits for them, and re-layouts  8.24 us
    pallas_call x6, Pallas kernels, surface(): call(functools.partial(surface_kernel, width), 'surface', shaped((chips,...  7.97 us
    pallas_call x3, Pallas kernels, split_call(): call(body, name, tuple((shaped(s, BF16) for s in outs)), [SM, AN], [pltpu...  5.96 us
  transfers between devices with their start and end apart: 15, of which 11 were waited for; matrix products, arithmetic and copies ran while one was open for 1% of the time, Pallas kernels for 15%

profile of v2, /device:TPU:0, one launch (start us, length us, event | category | flops | bytes accessed | tf_op | source)
XLA Modules:
  0.0 176.8 jit_solution(9922075484966059273)
XLA Ops:
  1.2 1.3 reduce.3
  4.3 21.3 %all_to_all.30.mine = f32[8,256,128]{2,1,0:T(8,128)S(1)} all-to-all(f32[8,256,128]{2,1,0:T(8,128)S(1)} %start.1), channel_id=1, replica_groups={{0,2,4,6,8,10,12,14},{1,3,5,7,9,11,13,15},{16,18,20,22,24,26,28,30},{17..., dimensions={0} | all-to-all | bytes 2097152 | tf_op jit(solution)/shard_map/all_to_all | solution.py:286
  25.7 3.6 %collective-permute-start = (f32[128,128]{1,0:T(8,128)S(1)}, f32[128,128]{1,0:T(8,128)S(1)}, u32[]{:S(2)}, u32[]{:S(2)}) collective-permute-start(f32[128,128]{1,0:T(8,128)S(1)} %copy-done.4), channel_id=1, source_target_pairs={{0,64},{16,80},{32,96},{48,112},{64,0},{80,16},{96,32},{112,48},{1... | collective-permute-start | bytes 196616 | tf_op jit(solution)/shard_map/ppermute | solution.py:290
  29.2 2.8 %collective-permute-done.rest_1_ = f32[128,128]{1,0:T(8,128)S(1)} collective-permute-done((f32[128,128]{1,0:T(8,128)S(1)}, f32[128,128]{1,0:T(8,128)S(1)}, u32[]{:S(2)}, u32[]{:S(2)}) %collective-permute-start) | collective-permute-done | bytes 65568 | tf_op jit(solution)/shard_map/ppermute | solution.py:290
  32.8 1.6 collective-permute-start.1
  34.4 2.2 %copy-done.2 = f32[1,2,1024,512]{3,2,1,0:T(8,128)S(1)} copy-done((f32[1,2,1024,512]{3,2,1,0:T(8,128)S(1)}, f32[1,2,1024,512]{3,2,1,0:T(8,128)}, u32[]{:S(2)}) %copy-start.2) | copy-done | bytes 4194328
  36.6 2.1 %split_coupling.1 = (bf16[2048,512]{1,0:T(8,128)(2,1)S(1)}, bf16[2048,512]{1,0:T(8,128)(2,1)S(1)}, bf16[512,2048]{1,0:T(8,128)(2,1)S(1)}, bf16[512,2048]{1,0:T(8,128)(2,1)S(1)}) custom-call(s32[1]{0:T(128)} %bitcast.2.token.here_ref, f32[2048,512]{1,0:T(8,128)S(1)} %bitcast.22), custom_call_target="tpu_custom_call" | custom-call | bytes 4194304 | tf_op jit(solution)/shard_map/split_coupling/pallas_call | solution.py:111
  38.8 3.4 %copy-done.1 = f32[1,2,1024,1024]{3,2,1,0:T(8,128)S(1)} copy-done((f32[1,2,1024,1024]{3,2,1,0:T(8,128)S(1)}, f32[1,2,1024,1024]{3,2,1,0:T(8,128)}, u32[]{:S(2)}) %copy-start.1) | copy-done | bytes 8388632
  42.1 1.7 split_leaf.1
  44.4 2.1 %split_surface.1 = (bf16[2,1024,1024]{2,1,0:T(8,128)(2,1)S(1)}, bf16[2,1024,1024]{2,1,0:T(8,128)(2,1)S(1)}) custom-call(s32[1]{0:T(128)} %bitcast.2.token.here_ref, f32[2048,1024]{1,0:T(8,128)S(1)} %bitcast.21), custom_call_target="tpu_custom_call" | custom-call | bytes 8388608 | tf_op jit(solution)/shard_map/split_surface/pallas_call | solution.py:111
  46.5 2.2 %collective-permute-start.2 = (f32[512,128]{1,0:T(8,128)S(1)}, f32[512,128]{1,0:T(8,128)S(1)}, u32[]{:S(2)}, u32[]{:S(2)}) collective-permute-start(f32[512,128]{1,0:T(8,128)S(1)} %pad_maximum_fusion), channel_id=1, source_target_pairs={{0,48},{16,32},{32,16},{48,0},{64,112},{80,96},{96,80},{112,64},{1... | collective-permute-start | bytes 786440 | tf_op jit(solution)/shard_map/ppermute | solution.py:290
  48.8 4.4 %leaves.3 = (f32[2,1024,128]{2,1,0:T(8,128)}, f32[2,8,128,128]{3,2,1,0:T(8,128)S(1)}, f32[512,128]{1,0:T(8,128)S(1)}) custom-call(s32[1]{0:T(128)} %bitcast.2.token.here_ref, s32[16]{0:T(128)S(1)} %reshape.41.owner_ref, s32[1,2]{1,0:T(1,128)S(1)} %copy-done.10, s32[1,2]{1,0:T(1,128)S(1)} %copy-done.11, f32[2,1024,128]{2,1,0:T(8,128)S(1)} %bitcast.16, ...), custom_call_target="tpu_custom_call" | custom-call | flops 4294967296 | bytes 16777216 | tf_op jit(solution)/shard_map/leaves/pallas_call | solution.py:343
  53.1 2.5 %collective-permute-done.2.rest_3_ = f32[512,128]{1,0:T(8,128)S(1)} collective-permute-done((f32[512,128]{1,0:T(8,128)S(1)}, f32[512,128]{1,0:T(8,128)S(1)}, u32[]{:S(2)}, u32[]{:S(2)}) %collective-permute-start.2) | collective-permute-done | bytes 262176 | tf_op jit(solution)/shard_map/ppermute | solution.py:290
  57.7 1.3 surface.6
  59.4 14.3 %all_to_all.31.got = f32[8,160,128]{2,1,0:T(8,128)S(1)} all-to-all(f32[8,160,128]{2,1,0:T(8,128)S(1)} %add.9), channel_id=1, replica_groups={{0,2,4,6,8,10,12,14},{1,3,5,7,9,11,13,15},{16,18,20,22,24,26,28,30},{17..., dimensions={0} | all-to-all | bytes 1310720 | tf_op jit(solution)/shard_map/all_to_all | solution.py:286
  73.8 3.4 %collective-permute-start.5 = (f32[128,128]{1,0:T(8,128)S(1)}, f32[128,128]{1,0:T(8,128)S(1)}, u32[]{:S(2)}, u32[]{:S(2)}) collective-permute-start(f32[128,128]{1,0:T(8,128)S(1)} %field.4.rest_0_), channel_id=1, source_target_pairs={{0,64},{16,80},{32,96},{48,112},{64,0},{80,16},{96,32},{112,48},{1... | collective-permute-start | bytes 196616 | tf_op jit(solution)/shard_map/ppermute | solution.py:290
  77.2 2.4 %collective-permute-done.5.rest_1_ = f32[128,128]{1,0:T(8,128)S(1)} collective-permute-done((f32[128,128]{1,0:T(8,128)S(1)}, f32[128,128]{1,0:T(8,128)S(1)}, u32[]{:S(2)}, u32[]{:S(2)}) %collective-permute-start.5) | collective-permute-done | bytes 65568 | tf_op jit(solution)/shard_map/ppermute | solution.py:290
  79.6 12.1 %all_to_all.32.mine = f32[8,160,128]{2,1,0:T(8,128)S(1)} all-to-all(f32[8,160,128]{2,1,0:T(8,128)S(1)} %wide.2), channel_id=1, replica_groups={{0,2,4,6,8,10,12,14},{1,3,5,7,9,11,13,15},{16,18,20,22,24,26,28,30},{17..., dimensions={0} | all-to-all | bytes 1310720 | tf_op jit(solution)/shard_map/all_to_all | solution.py:286
  91.8 5.9 %collective-permute-done.6.rest_2_ = f32[256,128]{1,0:T(8,128)S(1)} collective-permute-done((f32[256,128]{1,0:T(8,128)S(1)}, f32[256,128]{1,0:T(8,128)S(1)}, u32[]{:S(2)}, u32[]{:S(2)}) %collective-permute-start.6) | collective-permute-done | bytes 131104 | tf_op jit(solution)/shard_map/ppermute | solution.py:290
  97.7 2.2 %collective-permute-start.7 = (f32[512,128]{1,0:T(8,128)S(1)}, f32[512,128]{1,0:T(8,128)S(1)}, u32[]{:S(2)}, u32[]{:S(2)}) collective-permute-start(f32[512,128]{1,0:T(8,128)S(1)} %pad_maximum_fusion.1), channel_id=1, source_target_pairs={{0,48},{16,32},{32,16},{48,0},{64,112},{80,96},{96,80},{112,64},{1... | collective-permute-start | bytes 786440 | tf_op jit(solution)/shard_map/ppermute | solution.py:290
  99.9 5.7 %leaves.4 = (f32[2,1024,128]{2,1,0:T(8,128)}, f32[2,8,128,128]{3,2,1,0:T(8,128)S(1)}, f32[512,128]{1,0:T(8,128)S(1)}) custom-call(s32[1]{0:T(128)} %bitcast.2.token.here_ref, s32[16]{0:T(128)S(1)} %reshape.41.owner_ref, s32[1,2]{1,0:T(1,128)S(1)} %copy-done.10, s32[1,2]{1,0:T(1,128)S(1)} %copy-done.11, f32[2,1024,128]{2,1,0:T(8,128)S(1)} %bitcast.17, ...), custom_call_target="tpu_custom_call" | custom-call | flops 4294967296 | bytes 16777216 | tf_op jit(solution)/shard_map/leaves/pallas_call | solution.py:343
  105.6 1.4 collective-permute-done.7.rest_3_
  108.4 1.3 surface.8
  110.5 14.3 %all_to_all.33.got = f32[8,160,128]{2,1,0:T(8,128)S(1)} all-to-all(f32[8,160,128]{2,1,0:T(8,128)S(1)} %add.10), channel_id=1, replica_groups={{0,2,4,6,8,10,12,14},{1,3,5,7,9,11,13,15},{16,18,20,22,24,26,28,30},{17..., dimensions={0} | all-to-all | bytes 1310720 | tf_op jit(solution)/shard_map/all_to_all | solution.py:286
  124.9 3.4 %collective-permute-start.10 = (f32[128,128]{1,0:T(8,128)S(1)}, f32[128,128]{1,0:T(8,128)S(1)}, u32[]{:S(2)}, u32[]{:S(2)}) collective-permute-start(f32[128,128]{1,0:T(8,128)S(1)} %field.5.rest_0_), channel_id=1, source_target_pairs={{0,64},{16,80},{32,96},{48,112},{64,0},{80,16},{96,32},{112,48},{1... | collective-permute-start | bytes 196616 | tf_op jit(solution)/shard_map/ppermute | solution.py:290
  128.3 2.4 %collective-permute-done.10.rest_1_ = f32[128,128]{1,0:T(8,128)S(1)} collective-permute-done((f32[128,128]{1,0:T(8,128)S(1)}, f32[128,128]{1,0:T(8,128)S(1)}, u32[]{:S(2)}, u32[]{:S(2)}) %collective-permute-start.10) | collective-permute-done | bytes 65568 | tf_op jit(solution)/shard_map/ppermute | solution.py:290
  130.7 12.1 %all_to_all.34.mine = f32[8,160,128]{2,1,0:T(8,128)S(1)} all-to-all(f32[8,160,128]{2,1,0:T(8,128)S(1)} %wide.3), channel_id=1, replica_groups={{0,2,4,6,8,10,12,14},{1,3,5,7,9,11,13,15},{16,18,20,22,24,26,28,30},{17..., dimensions={0} | all-to-all | bytes 1310720 | tf_op jit(solution)/shard_map/all_to_all | solution.py:286
  143.1 5.9 %collective-permute-done.12.rest_2_ = f32[256,128]{1,0:T(8,128)S(1)} collective-permute-done((f32[256,128]{1,0:T(8,128)S(1)}, f32[256,128]{1,0:T(8,128)S(1)}, u32[]{:S(2)}, u32[]{:S(2)}) %collective-permute-start.12) | collective-permute-done | bytes 131104 | tf_op jit(solution)/shard_map/ppermute | solution.py:290
  149.0 2.2 %collective-permute-start.13 = (f32[512,128]{1,0:T(8,128)S(1)}, f32[512,128]{1,0:T(8,128)S(1)}, u32[]{:S(2)}, u32[]{:S(2)}) collective-permute-start(f32[512,128]{1,0:T(8,128)S(1)} %pad_maximum_fusion.2), channel_id=1, source_target_pairs={{0,48},{16,32},{32,16},{48,0},{64,112},{80,96},{96,80},{112,64},{1... | collective-permute-start | bytes 786440 | tf_op jit(solution)/shard_map/ppermute | solution.py:290
  151.2 6.0 %leaves.5 = (f32[2,1024,128]{2,1,0:T(8,128)}, f32[2,8,128,128]{3,2,1,0:T(8,128)S(1)}, f32[512,128]{1,0:T(8,128)S(1)}) custom-call(s32[1]{0:T(128)} %bitcast.2.token.here_ref, s32[16]{0:T(128)S(1)} %reshape.41.owner_ref, s32[1,2]{1,0:T(1,128)S(1)} %copy-done.10, s32[1,2]{1,0:T(1,128)S(1)} %copy-done.11, f32[2,1024,128]{2,1,0:T(8,128)S(1)} %bitcast.18, ...), custom_call_target="tpu_custom_call" | custom-call | flops 4294967296 | bytes 16777216 | tf_op jit(solution)/shard_map/leaves/pallas_call | solution.py:343
  159.7 1.3 surface.10
  161.8 14.3 %all_to_all.35.got = f32[8,160,128]{2,1,0:T(8,128)S(1)} all-to-all(f32[8,160,128]{2,1,0:T(8,128)S(1)} %add.11), channel_id=1, replica_groups={{0,2,4,6,8,10,12,14},{1,3,5,7,9,11,13,15},{16,18,20,22,24,26,28,30},{17..., dimensions={0} | all-to-all | bytes 1310720 | tf_op jit(solution)/shard_map/all_to_all | solution.py:286
  (64 shorter events, 12.8 us)
Async XLA Ops:
  2.6 0.8 copy-start.4
  3.4 0.8 copy-start.9
  4.3 39.6 %slice-start = ((s8[8388608]{0:T(1024)(128)(4,1)}), s8[4194304]{0:T(1024)(128)(4,1)S(1)}, s32[]{:S(2)}) async-start(s8[8388608]{0:T(1024)(128)(4,1)} %bitcast.20), calls=%async_computation.6 | async-start | bytes 8388608
  25.6 23.1 %collective-permute-start.3 = (f32[8,256,128]{2,1,0:T(8,128)S(1)}, f32[8,256,128]{2,1,0:T(8,128)S(1)}, u32[]{:S(2)}, u32[]{:S(2)}) collective-permute-start(f32[8,256,128]{2,1,0:T(8,128)S(1)} %all_to_all.30.mine), channel_id=1, source_target_pairs={{0,1},{1,0},{2,3},{3,2},{4,5},{5,4},{6,7},{7,6},{8,9},{9,8},{10,11... | collective-permute-start | bytes 3145736 | tf_op jit(solution)/shard_map/ppermute | solution.py:317
  25.7 6.3 %collective-permute-start = (f32[128,128]{1,0:T(8,128)S(1)}, f32[128,128]{1,0:T(8,128)S(1)}, u32[]{:S(2)}, u32[]{:S(2)}) collective-permute-start(f32[128,128]{1,0:T(8,128)S(1)} %copy-done.4), channel_id=1, source_target_pairs={{0,64},{16,80},{32,96},{48,112},{64,0},{80,16},{96,32},{112,48},{1... | collective-permute-start | bytes 196616 | tf_op jit(solution)/shard_map/ppermute | solution.py:290
  32.8 13.6 %collective-permute-start.1 = (f32[256,128]{1,0:T(8,128)S(1)}, f32[256,128]{1,0:T(8,128)S(1)}, u32[]{:S(2)}, u32[]{:S(2)}) collective-permute-start(f32[256,128]{1,0:T(8,128)S(1)} %pad_maximum_fusion.3), channel_id=1, source_target_pairs={{0,16},{16,0},{32,48},{48,32},{64,80},{80,64},{96,112},{112,96},{1... | collective-permute-start | bytes 393224 | tf_op jit(solution)/shard_map/ppermute | solution.py:290
  34.4 2.2 %copy-start.2 = (f32[1,2,1024,512]{3,2,1,0:T(8,128)S(1)}, f32[1,2,1024,512]{3,2,1,0:T(8,128)}, u32[]{:S(2)}) copy-start(f32[1,2,1024,512]{3,2,1,0:T(8,128)} %param.15) | copy-start | bytes 12582916
  38.7 3.4 %copy-start.1 = (f32[1,2,1024,1024]{3,2,1,0:T(8,128)S(1)}, f32[1,2,1024,1024]{3,2,1,0:T(8,128)}, u32[]{:S(2)}) copy-start(f32[1,2,1024,1024]{3,2,1,0:T(8,128)} %param.14) | copy-start | bytes 25165828
  42.1 2.2 %slice-start.1 = ((s8[8388608]{0:T(1024)(128)(4,1)}), s8[4194304]{0:T(1024)(128)(4,1)S(1)}, s32[]{:S(2)}) async-start(s8[8388608]{0:T(1024)(128)(4,1)} %bitcast.20), calls=%async_computation.7 | async-start | bytes 8388608
  44.3 2.2 %copy-start.5 = (f32[128,128]{1,0:T(8,128)S(1)}, f32[128,128]{1,0:T(8,128)}, u32[]{:S(2)}) copy-start(f32[128,128]{1,0:T(8,128)} %rest_0_.1) | copy-start | bytes 196612
  44.3 4.4 %copy-start = (f32[1,2,1024,128]{3,2,1,0:T(8,128)S(1)}, f32[1,2,1024,128]{3,2,1,0:T(8,128)}, u32[]{:S(2)}) copy-start(f32[1,2,1024,128]{3,2,1,0:T(8,128)} %param.17) | copy-start | bytes 3145732
  44.3 4.4 %copy-start.3 = (f32[1,512,128]{2,1,0:T(8,128)S(1)}, f32[1,512,128]{2,1,0:T(8,128)}, u32[]{:S(2)}) copy-start(f32[1,512,128]{2,1,0:T(8,128)} %param.18) | copy-start | bytes 786436
  44.3 4.4 %copy-start.7 = (f32[1,2,8,128]{3,2,1,0:T(8,128)S(1)}, f32[1,2,8,128]{3,2,1,0:T(8,128)}, u32[]{:S(2)}) copy-start(f32[1,2,8,128]{3,2,1,0:T(8,128)} %param.21) | copy-start | bytes 24580
  44.3 4.4 %copy-start.8 = (f32[1,2,8,128]{3,2,1,0:T(8,128)S(1)}, f32[1,2,8,128]{3,2,1,0:T(8,128)}, u32[]{:S(2)}) copy-start(f32[1,2,8,128]{3,2,1,0:T(8,128)} %param.22) | copy-start | bytes 24580
  44.3 4.4 %copy-start.10 = (s32[1,2]{1,0:T(1,128)S(1)}, s32[1,2]{1,0:T(1,128)}, u32[]{:S(2)}) copy-start(s32[1,2]{1,0:T(1,128)} %size_ref.5) | copy-start | bytes 28
  44.4 4.4 %copy-start.11 = (s32[1,2]{1,0:T(1,128)S(1)}, s32[1,2]{1,0:T(1,128)}, u32[]{:S(2)}) copy-start(s32[1,2]{1,0:T(1,128)} %count_ref.5) | copy-start | bytes 28
  46.5 9.2 %collective-permute-start.2 = (f32[512,128]{1,0:T(8,128)S(1)}, f32[512,128]{1,0:T(8,128)S(1)}, u32[]{:S(2)}, u32[]{:S(2)}) collective-permute-start(f32[512,128]{1,0:T(8,128)S(1)} %pad_maximum_fusion), channel_id=1, source_target_pairs={{0,48},{16,32},{32,16},{48,0},{64,112},{80,96},{96,80},{112,64},{1... | collective-permute-start | bytes 786440 | tf_op jit(solution)/shard_map/ppermute | solution.py:290
  57.0 2.4 %collective-permute-start.4 = (f32[8,160,128]{2,1,0:T(8,128)S(1)}, f32[8,160,128]{2,1,0:T(8,128)S(1)}, u32[]{:S(2)}, u32[]{:S(2)}) collective-permute-start(f32[8,160,128]{2,1,0:T(8,128)S(1)} %surface.7), channel_id=1, source_target_pairs={{0,1},{1,0},{2,3},{3,2},{4,5},{5,4},{6,7},{7,6},{8,9},{9,8},{10,11... | collective-permute-start | bytes 1966088 | tf_op jit(solution)/shard_map/ppermute | solution.py:374
  57.6 16.1 %copy-start.6 = (f32[128,128]{1,0:T(8,128)S(1)}, f32[128,128]{1,0:T(8,128)}, u32[]{:S(2)}) copy-start(f32[128,128]{1,0:T(8,128)} %load.5) | copy-start | bytes 196612
  73.8 5.8 %collective-permute-start.5 = (f32[128,128]{1,0:T(8,128)S(1)}, f32[128,128]{1,0:T(8,128)S(1)}, u32[]{:S(2)}, u32[]{:S(2)}) collective-permute-start(f32[128,128]{1,0:T(8,128)S(1)} %field.4.rest_0_), channel_id=1, source_target_pairs={{0,64},{16,80},{32,96},{48,112},{64,0},{80,16},{96,32},{112,48},{1... | collective-permute-start | bytes 196616 | tf_op jit(solution)/shard_map/ppermute | solution.py:290
  91.7 8.2 %collective-permute-start.8 = (f32[8,160,128]{2,1,0:T(8,128)S(1)}, f32[8,160,128]{2,1,0:T(8,128)S(1)}, u32[]{:S(2)}, u32[]{:S(2)}) collective-permute-start(f32[8,160,128]{2,1,0:T(8,128)S(1)} %all_to_all.32.mine), channel_id=1, source_target_pairs={{0,1},{1,0},{2,3},{3,2},{4,5},{5,4},{6,7},{7,6},{8,9},{9,8},{10,11... | collective-permute-start | bytes 1966088 | tf_op jit(solution)/shard_map/ppermute | solution.py:317
  91.7 6.0 %collective-permute-start.6 = (f32[256,128]{1,0:T(8,128)S(1)}, f32[256,128]{1,0:T(8,128)S(1)}, u32[]{:S(2)}, u32[]{:S(2)}) collective-permute-start(f32[256,128]{1,0:T(8,128)S(1)} %pad_maximum_fusion.4), channel_id=1, source_target_pairs={{0,16},{16,0},{32,48},{48,32},{64,80},{80,64},{96,112},{112,96},{1... | collective-permute-start | bytes 393224 | tf_op jit(solution)/shard_map/ppermute | solution.py:290
  97.7 9.2 %collective-permute-start.7 = (f32[512,128]{1,0:T(8,128)S(1)}, f32[512,128]{1,0:T(8,128)S(1)}, u32[]{:S(2)}, u32[]{:S(2)}) collective-permute-start(f32[512,128]{1,0:T(8,128)S(1)} %pad_maximum_fusion.1), channel_id=1, source_target_pairs={{0,48},{16,32},{32,16},{48,0},{64,112},{80,96},{96,80},{112,64},{1... | collective-permute-start | bytes 786440 | tf_op jit(solution)/shard_map/ppermute | solution.py:290
  108.3 2.2 %collective-permute-start.9 = (f32[8,160,128]{2,1,0:T(8,128)S(1)}, f32[8,160,128]{2,1,0:T(8,128)S(1)}, u32[]{:S(2)}, u32[]{:S(2)}) collective-permute-start(f32[8,160,128]{2,1,0:T(8,128)S(1)} %surface.9), channel_id=1, source_target_pairs={{0,1},{1,0},{2,3},{3,2},{4,5},{5,4},{6,7},{7,6},{8,9},{9,8},{10,11... | collective-permute-start | bytes 1966088 | tf_op jit(solution)/shard_map/ppermute | solution.py:374
  124.9 5.8 %collective-permute-start.10 = (f32[128,128]{1,0:T(8,128)S(1)}, f32[128,128]{1,0:T(8,128)S(1)}, u32[]{:S(2)}, u32[]{:S(2)}) collective-permute-start(f32[128,128]{1,0:T(8,128)S(1)} %field.5.rest_0_), channel_id=1, source_target_pairs={{0,64},{16,80},{32,96},{48,112},{64,0},{80,16},{96,32},{112,48},{1... | collective-permute-start | bytes 196616 | tf_op jit(solution)/shard_map/ppermute | solution.py:290
  142.8 8.4 %collective-permute-start.11 = (f32[8,160,128]{2,1,0:T(8,128)S(1)}, f32[8,160,128]{2,1,0:T(8,128)S(1)}, u32[]{:S(2)}, u32[]{:S(2)}) collective-permute-start(f32[8,160,128]{2,1,0:T(8,128)S(1)} %all_to_all.34.mine), channel_id=1, source_target_pairs={{0,1},{1,0},{2,3},{3,2},{4,5},{5,4},{6,7},{7,6},{8,9},{9,8},{10,11... | collective-permute-start | bytes 1966088 | tf_op jit(solution)/shard_map/ppermute | solution.py:317
  142.8 6.2 %collective-permute-start.12 = (f32[256,128]{1,0:T(8,128)S(1)}, f32[256,128]{1,0:T(8,128)S(1)}, u32[]{:S(2)}, u32[]{:S(2)}) collective-permute-start(f32[256,128]{1,0:T(8,128)S(1)} %pad_maximum_fusion.5), channel_id=1, source_target_pairs={{0,16},{16,0},{32,48},{48,32},{64,80},{80,64},{96,112},{112,96},{1... | collective-permute-start | bytes 393224 | tf_op jit(solution)/shard_map/ppermute | solution.py:290
  149.0 9.2 %collective-permute-start.13 = (f32[512,128]{1,0:T(8,128)S(1)}, f32[512,128]{1,0:T(8,128)S(1)}, u32[]{:S(2)}, u32[]{:S(2)}) collective-permute-start(f32[512,128]{1,0:T(8,128)S(1)} %pad_maximum_fusion.2), channel_id=1, source_target_pairs={{0,48},{16,32},{32,16},{48,0},{64,112},{80,96},{96,80},{112,64},{1... | collective-permute-start | bytes 786440 | tf_op jit(solution)/shard_map/ppermute | solution.py:290
  159.6 2.2 %collective-permute-start.14 = (f32[8,160,128]{2,1,0:T(8,128)S(1)}, f32[8,160,128]{2,1,0:T(8,128)S(1)}, u32[]{:S(2)}, u32[]{:S(2)}) collective-permute-start(f32[8,160,128]{2,1,0:T(8,128)S(1)} %surface.11), channel_id=1, source_target_pairs={{0,1},{1,0},{2,3},{3,2},{4,5},{5,4},{6,7},{7,6},{8,9},{9,8},{10,11... | collective-permute-start | bytes 1966088 | tf_op jit(solution)/shard_map/ppermute | solution.py:374

commit v3 on v2

v3 whole, which is shorter than its diff:
```python
import functools

import jax
import jax.numpy as jnp
from jax import lax
from jax.experimental import pallas as pl
from jax.experimental.pallas import tpu as pltpu
from jax.sharding import PartitionSpec as P

SWEEPS = 3
F32, BF16 = jnp.float32, jnp.bfloat16
VM = pl.BlockSpec(memory_space=pltpu.VMEM)
SM = pl.BlockSpec(memory_space=pltpu.SMEM)
HB = pl.BlockSpec(memory_space=pltpu.HBM)
MIB = 2**20


FIRST_STEP = 4
NEXT_STEPS = (1, 3, 2)


def origins():
    return [origin for step in (0, *NEXT_STEPS) for origin in (step, step ^ FIRST_STEP)]


def call(body, name, out, ins, scratch=(), limit=6, flops=0, moved=0):
    return pl.pallas_call(
        body,
        out_shape=out,
        in_specs=ins,
        out_specs=jax.tree.map(lambda _: VM, out),
        scratch_shapes=list(scratch),
        compiler_params=pltpu.CompilerParams(vmem_limit_bytes=limit * MIB),
        cost_estimate=pl.CostEstimate(flops=flops, bytes_accessed=moved, transcendentals=0),
        name=name,
    )


def shaped(shape, dtype=F32):
    return jax.ShapeDtypeStruct(shape, dtype)


def parted(x):
    hi = x.astype(BF16)
    return hi, (x - hi.astype(F32)).astype(BF16)


def widened(x):
    return jnp.concatenate(parted(x), axis=1)


def dot(a, b):
    return jnp.dot(a, b, preferred_element_type=F32)


def product(hi, lo, wide):
    n = wide.shape[1] // 2
    both = dot(hi, wide)
    return both[:, :n] + both[:, n:] + dot(lo, wide[:, :n])


def start_kernel(width, field, schur_t, wide):
    share, columns = schur_t.shape
    for chip in range(wide.shape[0]):
        wide[chip, :width] = field[...]
        for q in range(columns // width):
            rows = slice(width + q * share, width + (q + 1) * share)
            wide[chip, rows] = schur_t[:, q * width : (q + 1) * width]


def turn_kernel(width, core_ref, mine, other, hi_ref, lo_ref, whole):
    chips = mine.shape[0]
    columns = whole.shape[1]
    share = whole.shape[0] // (2 * chips)
    core = core_ref[0]
    for chip in range(chips):
        at = 2 * chip * share
        for q in range(columns // width):
            rows = slice(width + q * share, width + (q + 1) * share)
            to = slice(q * width, (q + 1) * width)
            a, b = mine[chip, rows], other[chip, rows]
            whole[at : at + share, to] = jnp.where(core == 0, a, b)
            whole[at + share : at + 2 * share, to] = jnp.where(core == 0, b, a)
    hi_ref[...], lo_ref[...] = parted(whole[...].T)


def leaf_kernel(
    width, first, last,
    here_ref, owner_ref, size_ref, count_ref,
    load, flux_weight, trace_weight, sep_load, mine, other, *rest,
):
    if first:
        inv, cpl, sol, dense, part, *rest = rest
        inv_hi, inv_lo, cpl_hi, cpl_lo, cpl_t_hi, cpl_t_lo, *rest = rest
        wide, wide_sol, inv_buf, cpl_buf, inv_sems, cpl_sems = rest
    else:
        inv_hi, inv_lo, cpl_t_hi, cpl_t_lo, cpl_hi, cpl_lo, sch_hi, sch_lo, *rest = rest
        sol, dense, part, wide, wide_sol, gathered = rest
    leaves, order, loads = load.shape
    blocks = order // width
    chips = dense.shape[1]
    share = part.shape[0] // (2 * chips)
    here = here_ref[0]
    core = here % 2
    flux_t, trace_t = flux_weight[...].T, trace_weight[...].T
    tile = order // 2 if first else order

    def tiles(src, buf, sems):
        return [
            pltpu.make_async_copy(src.at[pl.ds(i * tile, tile)], buf.at[i], sems.at[i])
            for i in range(src.shape[0] // tile)
        ]

    if first:
        inv_copies, cpl_copies = tiles(inv, inv_buf, inv_sems), tiles(cpl, cpl_buf, cpl_sems)
        for copy in inv_copies + cpl_copies:
            copy.start()

    def scale(turned, j, k):
        e = j * blocks + k
        return jnp.where(k < count_ref[0, j], turned[:, e : e + 1], 0.0)

    def live(j, k, x):
        row = k * width + lax.broadcasted_iota(jnp.int32, (width, loads), 0)
        return jnp.where(row < size_ref[0, j], x, 0.0)

    def surface(o):
        chip = o // 2
        return jnp.where(o - 2 * chip == core, mine[chip, :width], other[chip, :width])

    if not first:
        for chip in range(chips):
            a, b = mine[chip, width:], other[chip, width:]
            at = 2 * chip * share
            gathered[at : at + share] = jnp.where(core == 0, a, b)
            gathered[at + share : at + 2 * share] = jnp.where(core == 0, b, a)
        sep_wide = widened(product(sch_hi[...], sch_lo[...], widened(gathered[...])))
    dense[...] = jnp.zeros_like(dense)
    for j in range(leaves):
        if not first:
            rows = slice(j * order, (j + 1) * order)
            pulled = product(cpl_hi[rows], cpl_lo[rows], sep_wide)
        for k in range(blocks):
            at = slice(k * width, (k + 1) * width)
            rhs = load[j, at] - surface(owner_ref[0, j, 0, k]) * scale(flux_t, j, k)
            if not first:
                rhs = rhs - pulled[at]
            wide[j, at] = widened(live(j, k, rhs))
        for t in range(order // tile):
            start = j * order + t * tile
            rows = slice(start, start + tile)
            if first:
                i = start // tile
                inv_copies[i].wait()
                hi, lo = parted(inv_buf[i])
                inv_hi[rows], inv_lo[rows] = hi, lo
                got = product(hi, lo, wide[j])
            else:
                got = product(inv_hi[rows], inv_lo[rows], wide[j])
            for b in range(tile // width):
                k = t * (tile // width) + b
                o = owner_ref[0, j, 0, k]
                chip = o // 2
                block = live(j, k, got[b * width : (b + 1) * width])
                sol[j, k * width : (k + 1) * width] = block
                dense[o - 2 * chip, chip] += block * scale(trace_t, j, k)
                at = slice(start + b * width, start + (b + 1) * width)
                wide_sol[at] = widened(block)
    left = jnp.where(here == 0, sep_load[...], 0.0)
    if first:
        for i, copy in enumerate(cpl_copies):
            copy.wait()
            rows = slice(i * tile, (i + 1) * tile)
            cpl_hi[rows], cpl_lo[rows] = parted(cpl_buf[i])
            hi, lo = parted(cpl_buf[i].T)
            cpl_t_hi[:, rows], cpl_t_lo[:, rows] = hi, lo
            left = left - product(hi, lo, wide_sol[rows])
    else:
        left = left - product(cpl_t_hi[...], cpl_t_lo[...], wide_sol[...])
    if last:
        left = product(sch_hi[...], sch_lo[...], widened(left))
    part[...] = left


def surface_kernel(width, first, pick_ref, group_ref, *rest):
    if first:
        src, *rest, out, hi_ref, lo_ref, wide, buf, sems = rest
    else:
        hi_ref, lo_ref, *rest, out, wide = rest
    *pieces, dense, part = rest
    pick = pick_ref[0]
    chips = out.shape[0]
    share = part.shape[0] // (2 * chips)
    parts = buf.shape[0] if first else 1
    tile = chips * width // parts

    def copies(i):
        found = []
        for b in range(tile // width):
            at = pl.multiple_of((2 * (i * (tile // width) + b) + pick) * width, width)
            found.append(
                pltpu.make_async_copy(
                    src.at[pl.ds(at, width)], buf.at[i, pl.ds(b * width, width)], sems.at[i, b]
                )
            )
        return found

    if first:
        flying = [copies(i) for i in range(parts)]
        for group in flying:
            for copy in group:
                copy.start()
    block = 0
    for piece in pieces:
        for i in range(piece.shape[0] // width):
            at = pl.multiple_of((group_ref[0] ^ origins()[block]) * width, width)
            wide[pl.ds(at, width)] = widened(piece[i * width : (i + 1) * width])
            block += 1
    for i in range(parts):
        rows = slice(i * tile, (i + 1) * tile)
        if first:
            for copy in flying[i]:
                copy.wait()
            hi, lo = parted(buf[i])
            hi_ref[rows], lo_ref[rows] = hi, lo
            got = product(hi, lo, wide[...])
        else:
            got = product(hi_ref[rows], lo_ref[rows], wide[...])
        for b in range(tile // width):
            chip = i * (tile // width) + b
            out[chip, :width] = dense[pick, chip] + got[b * width : (b + 1) * width]
            at = pl.multiple_of((2 * chip + pick) * share, share)
            out[chip, width:] = part[pl.ds(at, share)]


def summed(got, rows):
    total = got[0, rows]
    for chip in range(1, got.shape[0]):
        total = total + got[chip, rows]
    return total


def field_kernel(width, got, load, field):
    field[...] = load[...] + summed(got, slice(0, width))


def wide_kernel(width, got, field, wide):
    rest = summed(got, slice(width, None))
    for chip in range(wide.shape[0]):
        wide[chip, :width] = field[...]
        wide[chip, width:] = rest


def final_kernel(width, got, load, field, separator):
    field[...] = load[...] + summed(got, slice(0, width))
    separator[...] = summed(got, slice(width, None))


def on_device(
    bem_tiles,
    leaf_inverse,
    coupling,
    schur_inverse,
    leaf_load,
    sep_load,
    surf_load,
    surf_start,
    flux_weight,
    trace_weight,
    leaf_sizes,
    block_counts,
    block_owner,
):
    parts = lax.axis_size("sub")
    groups = lax.axis_size("grp")
    here = lax.axis_index("sub")
    core = lax.rem(here, 2).astype(jnp.int32)
    mine_id, other_id = core.reshape(1), (1 - core).reshape(1)
    here_id = here.astype(jnp.int32).reshape(1)
    group = lax.axis_index("grp").astype(jnp.int32).reshape(1)
    chips = parts // 2
    width, loads = surf_load.shape
    leaves, order = leaf_inverse.shape[1:3]
    blocks = order // width
    entries = leaves * blocks
    separator = schur_inverse.shape[1]
    share = schur_inverse.shape[2]
    rows = bem_tiles.shape[0]
    columns = bem_tiles.shape[1]
    same_core = [[2 * c + k for c in range(chips)] for k in range(2)]
    swap = [(i, i ^ 1) for i in range(parts)]

    def over_chips(x):
        return lax.all_to_all(x, "sub", 0, 0, axis_index_groups=same_core, tiled=True)

    def exchanged(x, step):
        return lax.ppermute(x, "grp", [(i, i ^ step) for i in range(groups)])

    inv = leaf_inverse.reshape(leaves * order, order)
    cpl = coupling.reshape(leaves * order, separator)
    field = surf_start
    wide = call(
        functools.partial(start_kernel, width),
        "start",
        shaped((chips, 2 * width, loads)),
        [VM] * 2,
        moved=MIB,
    )(surf_start, schur_inverse[0].T)
    wide, here_id, mine_id, other_id, group, owner = lax.optimization_barrier(
        (wide, here_id, mine_id, other_id, group, block_owner.transpose(0, 1, 3, 2))
    )
    for sweep in range(SWEEPS):
        first, last = sweep == 0, sweep == SWEEPS - 1
        beyond = exchanged(field, FIRST_STEP)
        wide, beyond = lax.optimization_barrier((wide, beyond))
        mine = over_chips(wide)
        mine, field, beyond = lax.optimization_barrier((mine, field, beyond))
        pair = jnp.concatenate([field, beyond], axis=0)
        pieces = [pair] + [exchanged(pair, step) for step in NEXT_STEPS]
        other = lax.ppermute(mine, "sub", swap)
        operands = [here_id, owner, leaf_sizes, block_counts, leaf_load[0]]
        operands += [w.reshape(entries, width) for w in (flux_weight, trace_weight)]
        operands += [sep_load[0], mine, other]
        outs = [
            shaped((leaves, order, loads)),
            shaped((2, chips, width, loads)),
            shaped((separator, loads)),
        ]
        scratch = [
            pltpu.VMEM((leaves, order, 2 * loads), BF16),
            pltpu.VMEM((leaves * order, 2 * loads), BF16),
        ]
        if first:
            sch_hi, sch_lo = call(
                functools.partial(turn_kernel, width),
                "split_schur",
                (shaped((separator, separator), BF16),) * 2,
                [SM] + [VM] * 2,
                [pltpu.VMEM((separator, separator), F32)],
                moved=8 * separator * separator,
            )(mine_id, mine, other)
            matrices = [pltpu.with_memory_space_constraint(m, pltpu.HBM) for m in (inv, cpl)]
            outs += [shaped(inv.shape, BF16)] * 2 + [shaped(cpl.shape, BF16)] * 2
            outs += [shaped(cpl.shape[::-1], BF16)] * 2
            scratch += [
                pltpu.VMEM((2 * leaves, order // 2, order), F32),
                pltpu.VMEM((2 * leaves, order // 2, separator), F32),
                pltpu.SemaphoreType.DMA((2 * leaves,)),
                pltpu.SemaphoreType.DMA((2 * leaves,)),
            ]
        else:
            matrices = [inv_hi, inv_lo, cpl_t_hi, cpl_t_lo, cpl_hi, cpl_lo, sch_hi, sch_lo]
            scratch += [pltpu.VMEM((separator, loads), F32)]
        solution, dense, part, *made = call(
            functools.partial(leaf_kernel, width, first, last),
            "leaves",
            tuple(outs),
            [SM] * 4 + [VM] * (len(operands) - 4) + [HB if first else VM] * len(matrices),
            scratch,
            limit=24 if first else 12,
            flops=8 * leaves * order * loads * (order + 2 * separator),
            moved=16 * MIB,
        )(*operands, *matrices)
        if first:
            inv_hi, inv_lo, cpl_hi, cpl_lo, cpl_t_hi, cpl_t_lo = made

        def surface(pick, matrix):
            half = (rows // 2, columns)
            payload = shaped((chips, width + share, loads))
            scratch = [pltpu.VMEM((columns, 2 * loads), BF16)]
            if first:
                scratch += [
                    pltpu.VMEM((2, rows // 4, columns), F32),
                    pltpu.SemaphoreType.DMA((2, chips // 2)),
                ]
            return call(
                functools.partial(surface_kernel, width, first),
                "surface",
                (payload, shaped(half, BF16), shaped(half, BF16)) if first else (payload,),
                [SM] * 2 + [HB if first else VM] * len(matrix) + [VM] * (2 + len(pieces)),
                scratch,
                limit=14 if first else 8,
                flops=4 * rows * columns * loads,
                moved=6 * MIB,
            )(pick, group, *matrix, *pieces, dense, part)

        if first:
            bem_other, bem_mine = [bem_tiles], [bem_tiles]
        away, *made_other = surface(other_id, bem_other)
        swapped = lax.ppermute(away, "sub", swap)
        stay, *made_mine = surface(mine_id, bem_mine)
        payload = stay + swapped
        if first:
            bem_other, bem_mine = made_other, made_mine
            payload, sch_hi, sch_lo = lax.optimization_barrier((payload, sch_hi, sch_lo))
        got = over_chips(payload)
        if not last:
            field = call(
                functools.partial(field_kernel, width), "field", shaped((width, loads)), [VM] * 2,
                moved=MIB,
            )(got, surf_load)
            wide = call(
                functools.partial(wide_kernel, width),
                "wide",
                shaped((chips, width + share, loads)),
                [VM] * 2,
                moved=2 * MIB,
            )(got, field)
    pressure, sep_rows = call(
        functools.partial(final_kernel, width),
        "final",
        (shaped((width, loads)), shaped((share, loads))),
        [VM] * 2,
        moved=MIB,
    )(got, surf_load)
    return (solution[None], sep_rows[None], pressure)


def solution(mesh):
    return jax.shard_map(
        on_device,
        mesh=mesh,
        in_specs=(
            P("grp", "sub"),
            P("grp", "sub", None, None),
            P("grp", "sub", None, None),
            P("grp", None, "sub"),
            P("grp", "sub", None, None),
            P("grp", None, None),
            P(("grp", "sub"), None),
            P(("grp", "sub"), None),
            P("grp", "sub", None, None),
            P("grp", "sub", None, None),
            P("grp", "sub"),
            P("grp", "sub"),
            P("grp", "sub", None, None),
        ),
        out_specs=(P("grp", "sub", None, None), P("grp", "sub", None), P(("grp", "sub"), None)),
        check_vma=False,
    )
```

time: 177 us -> 156 us (0.88)
  waiting for transfers between devices: 26.1 us -> 6.68 us
  local copies, waits for them, and re-layouts: 8.33 us -> 1.8 us
  starting transfers between devices: 19.4 us -> 25.7 us
  other arithmetic: 2.47 us -> 0.22 us
    ppermute x12 -> x15, waiting for transfers between devices: 26.1 us -> 6.67 us  [the longest x12 5.19 us: exchanged(): return lax.ppermute(x, 'grp', [(i, i ^ step) for i in range(groups)])]
    unnamed x29, local copies, waits for them, and re-layouts: 8.24 us -> 1.77 us
    ppermute x12 -> x15, starting transfers between devices: 19.3 us -> 25.7 us  [the longest x12 25.3 us: exchanged(): return lax.ppermute(x, 'grp', [(i, i ^ step) for i in range(groups)])]
    pallas_call x12 -> x9, Pallas kernels: 30 us -> 30.7 us  [the longest x3 21.5 us: on_device(): call(functools.partial(leaf_kernel, width, first, last), 'leaves', tuple(...]
  transfers between devices with their start and end apart: 15 -> 18, of which waited for: 11 -> 6; matrix products, arithmetic and copies ran while one was open for 1% -> 0% of each run, Pallas kernels for 15% -> 17%
where the time goes in v3:
time: 156 us; the launch traced here: 155 us
  blocking collectives  87.3 us (56%)
  Pallas kernels  32 us (21%)
  starting transfers between devices  25.7 us (16%)
  waiting for transfers between devices  6.68 us (4%)
  local copies, waits for them, and re-layouts  1.8 us (1%)
    all_to_all x6, blocking collectives, over_chips(): lax.all_to_all(x, 'sub', 0, 0, axis_index_groups=same_core, tiled=True)  87.3 us
    ppermute x12, starting transfers between devices, exchanged(): return lax.ppermute(x, 'grp', [(i, i ^ step) for i in range(groups)])  25.3 us
    pallas_call x3, Pallas kernels, on_device(): call(functools.partial(leaf_kernel, width, first, last), 'leaves', tuple(...  21.5 us
    pallas_call x6, Pallas kernels, surface(): call(functools.partial(surface_kernel, width, first), 'surface', (payload...  9.2 us
    ppermute x12, waiting for transfers between devices, exchanged(): return lax.ppermute(x, 'grp', [(i, i ^ step) for i in range(groups)])  5.19 us
  transfers between devices with their start and end apart: 18, of which 6 were waited for; matrix products, arithmetic and copies ran while one was open for 0% of the time, Pallas kernels for 17%

profile of v3, /device:TPU:0, one launch (start us, length us, event | category | flops | bytes accessed | tf_op | source)
XLA Modules:
  0.0 154.7 jit_solution(14633315935010876017)
XLA Ops:
  0.7 4.0 %collective-permute-start = (f32[128,128]{1,0:T(8,128)}, f32[128,128]{1,0:T(8,128)S(1)}, u32[]{:S(2)}, u32[]{:S(2)}) collective-permute-start(f32[128,128]{1,0:T(8,128)} %field.3), channel_id=1, source_target_pairs={{0,64},{16,80},{32,96},{48,112},{64,0},{80,16},{96,32},{112,48},{1... | collective-permute-start | bytes 196616 | tf_op jit(solution)/shard_map/ppermute | solution.py:297
  4.7 0.9 copy-done.3
  5.6 0.8 copy-done.7
  6.5 0.6 collective-permute-done
  7.1 19.5 %all_to_all.30.mine = f32[8,256,128]{2,1,0:T(8,128)S(1)} all-to-all(f32[8,256,128]{2,1,0:T(8,128)S(1)} %start.1), channel_id=1, replica_groups={{0,2,4,6,8,10,12,14},{1,3,5,7,9,11,13,15},{16,18,20,22,24,26,28,30},{17..., dimensions={0} | all-to-all | bytes 2097152 | tf_op jit(solution)/shard_map/all_to_all | solution.py:294
  26.6 3.1 %collective-permute-start.3 = (f32[256,128]{1,0:T(8,128)S(1)}, f32[256,128]{1,0:T(8,128)S(1)}, u32[]{:S(2)}, u32[]{:S(2)}) collective-permute-start(f32[256,128]{1,0:T(8,128)S(1)} %constant_dynamic-update-slice_fusion.rest_1_), channel_id=1, source_target_pairs={{0,32},{16,48},{32,0},{48,16},{64,96},{80,112},{96,64},{112,80},{1... | collective-permute-start | bytes 393224 | tf_op jit(solution)/shard_map/ppermute | solution.py:297
  29.7 1.1 collective-permute-start.2
  31.0 9.8 %leaves.3 = (f32[2,1024,128]{2,1,0:T(8,128)}, f32[2,8,128,128]{3,2,1,0:T(8,128)S(1)}, f32[512,128]{1,0:T(8,128)S(1)}, bf16[2048,1024]{1,0:T(8,128)(2,1)S(1)}, bf...) custom-call(s32[1]{0:T(128)} %bitcast.2.here_ref, ...), custom_call_target="tpu_custom_call" | custom-call | flops 4294967296 | bytes 16777216 | tf_op jit(solution)/shard_map/leaves/pallas_call | solution.py:354
  40.8 1.9 %surface.7 = (f32[8,160,128]{2,1,0:T(8,128)S(1)}, bf16[1024,1024]{1,0:T(8,128)(2,1)S(1)}, bf16[1024,1024]{1,0:T(8,128)(2,1)S(1)}) custom-call(s32[1]{0:T(128)} %bitcast.4.pick_ref, s32[1]{0:T(128)} %bitcast.5.group_ref, f32[2048,1024]{1,0:T(8,128)S(1)} %bitcast.18, f32[256,128]{1,0:T(8,128)S(1)} %constant_dynamic-update-slice_fusion.rest_1_, ...), custom_call_target="tpu_custom_call" | custom-call | flops 1073741824 | bytes 6291456 | tf_op jit(solution)/shard_map/surface/pallas_call | solution.py:376
  43.4 1.9 %surface.6 = (f32[8,160,128]{2,1,0:T(8,128)S(1)}, bf16[1024,1024]{1,0:T(8,128)(2,1)S(1)}, bf16[1024,1024]{1,0:T(8,128)(2,1)S(1)}) custom-call(s32[1]{0:T(128)} %bitcast.3.pick_ref.core_ref, s32[1]{0:T(128)} %bitcast.5.group_ref, f32[2048,1024]{1,0:T(8,128)S(1)} %bitcast.18, f32[256,128]{1,0:T(8,128)S(1)} %constant_dynamic-update-slice_fusion.rest_1_, ...), custom_call_target="tpu_custom_call" | custom-call | flops 1073741824 | bytes 6291456 | tf_op jit(solution)/shard_map/surface/pallas_call | solution.py:376
  45.4 14.9 %all_to_all.31.got = f32[8,160,128]{2,1,0:T(8,128)S(1)} all-to-all(f32[8,160,128]{2,1,0:T(8,128)S(1)} %add.9), channel_id=1, replica_groups={{0,2,4,6,8,10,12,14},{1,3,5,7,9,11,13,15},{16,18,20,22,24,26,28,30},{17..., dimensions={0} | all-to-all | bytes 1310720 | tf_op jit(solution)/shard_map/all_to_all | solution.py:294
  60.4 3.7 %collective-permute-start.6 = (f32[128,128]{1,0:T(8,128)S(1)}, f32[128,128]{1,0:T(8,128)S(1)}, u32[]{:S(2)}, u32[]{:S(2)}) collective-permute-start(f32[128,128]{1,0:T(8,128)S(1)} %field.4), channel_id=1, source_target_pairs={{0,64},{16,80},{32,96},{48,112},{64,0},{80,16},{96,32},{112,48},{1... | collective-permute-start | bytes 196616 | tf_op jit(solution)/shard_map/ppermute | solution.py:297
  64.1 2.2 %collective-permute-done.6 = f32[128,128]{1,0:T(8,128)S(1)} collective-permute-done((f32[128,128]{1,0:T(8,128)S(1)}, f32[128,128]{1,0:T(8,128)S(1)}, u32[]{:S(2)}, u32[]{:S(2)}) %collective-permute-start.6) | collective-permute-done | bytes 65568 | tf_op jit(solution)/shard_map/ppermute | solution.py:297
  66.3 12.3 %all_to_all.32.mine = f32[8,160,128]{2,1,0:T(8,128)S(1)} all-to-all(f32[8,160,128]{2,1,0:T(8,128)S(1)} %wide.2), channel_id=1, replica_groups={{0,2,4,6,8,10,12,14},{1,3,5,7,9,11,13,15},{16,18,20,22,24,26,28,30},{17..., dimensions={0} | all-to-all | bytes 1310720 | tf_op jit(solution)/shard_map/all_to_all | solution.py:294
  78.7 3.6 %collective-permute-start.9 = (f32[256,128]{1,0:T(8,128)S(1)}, f32[256,128]{1,0:T(8,128)S(1)}, u32[]{:S(2)}, u32[]{:S(2)}) collective-permute-start(f32[256,128]{1,0:T(8,128)S(1)} %constant_dynamic-update-slice_fusion.2.rest_2_), channel_id=1, source_target_pairs={{0,32},{16,48},{32,0},{48,16},{64,96},{80,112},{96,64},{112,80},{1... | collective-permute-start | bytes 393224 | tf_op jit(solution)/shard_map/ppermute | solution.py:297
  82.3 1.1 collective-permute-start.8
  83.4 5.7 %leaves.4 = (f32[2,1024,128]{2,1,0:T(8,128)}, f32[2,8,128,128]{3,2,1,0:T(8,128)S(1)}, f32[512,128]{1,0:T(8,128)S(1)}) custom-call(s32[1]{0:T(128)} %bitcast.2.here_ref, s32[1,2,1,8]{3,2,1,0:T(1,128)S(1)} %bitcast.33, s32[1,2]{1,0:T(1,128)S(1)} %copy-done.9, s32[1,2]{1,0:T(1,128)S(1)} %copy-done.10, f32[2,1024,128]{2,1,0:T(8,128)S(1)} %bitcast.20, ...), custom_call_target="tpu_custom_call" | custom-call | flops 4294967296 | bytes 16777216 | tf_op jit(solution)/shard_map/leaves/pallas_call | solution.py:354
  89.3 1.3 surface.9
  90.7 1.3 surface.8
  92.0 0.7 collective-permute-done.11
  92.9 14.3 %all_to_all.33.got = f32[8,160,128]{2,1,0:T(8,128)S(1)} all-to-all(f32[8,160,128]{2,1,0:T(8,128)S(1)} %add.10), channel_id=1, replica_groups={{0,2,4,6,8,10,12,14},{1,3,5,7,9,11,13,15},{16,18,20,22,24,26,28,30},{17..., dimensions={0} | all-to-all | bytes 1310720 | tf_op jit(solution)/shard_map/all_to_all | solution.py:294
  107.2 3.9 %collective-permute-start.12 = (f32[128,128]{1,0:T(8,128)S(1)}, f32[128,128]{1,0:T(8,128)S(1)}, u32[]{:S(2)}, u32[]{:S(2)}) collective-permute-start(f32[128,128]{1,0:T(8,128)S(1)} %field.5), channel_id=1, source_target_pairs={{0,64},{16,80},{32,96},{48,112},{64,0},{80,16},{96,32},{112,48},{1... | collective-permute-start | bytes 196616 | tf_op jit(solution)/shard_map/ppermute | solution.py:297
  111.1 2.2 %collective-permute-done.12 = f32[128,128]{1,0:T(8,128)S(1)} collective-permute-done((f32[128,128]{1,0:T(8,128)S(1)}, f32[128,128]{1,0:T(8,128)S(1)}, u32[]{:S(2)}, u32[]{:S(2)}) %collective-permute-start.12) | collective-permute-done | bytes 65568 | tf_op jit(solution)/shard_map/ppermute | solution.py:297
  113.3 12.0 %all_to_all.34.mine = f32[8,160,128]{2,1,0:T(8,128)S(1)} all-to-all(f32[8,160,128]{2,1,0:T(8,128)S(1)} %wide.3), channel_id=1, replica_groups={{0,2,4,6,8,10,12,14},{1,3,5,7,9,11,13,15},{16,18,20,22,24,26,28,30},{17..., dimensions={0} | all-to-all | bytes 1310720 | tf_op jit(solution)/shard_map/all_to_all | solution.py:294
  125.4 3.5 %collective-permute-start.16 = (f32[256,128]{1,0:T(8,128)S(1)}, f32[256,128]{1,0:T(8,128)S(1)}, u32[]{:S(2)}, u32[]{:S(2)}) collective-permute-start(f32[256,128]{1,0:T(8,128)S(1)} %constant_dynamic-update-slice_fusion.4.rest_2_), channel_id=1, source_target_pairs={{0,32},{16,48},{32,0},{48,16},{64,96},{80,112},{96,64},{112,80},{1... | collective-permute-start | bytes 393224 | tf_op jit(solution)/shard_map/ppermute | solution.py:297
  128.9 1.1 collective-permute-start.15
  130.1 6.0 %leaves.5 = (f32[2,1024,128]{2,1,0:T(8,128)}, f32[2,8,128,128]{3,2,1,0:T(8,128)S(1)}, f32[512,128]{1,0:T(8,128)S(1)}) custom-call(s32[1]{0:T(128)} %bitcast.2.here_ref, s32[1,2,1,8]{3,2,1,0:T(1,128)S(1)} %bitcast.34, s32[1,2]{1,0:T(1,128)S(1)} %copy-done.9, s32[1,2]{1,0:T(1,128)S(1)} %copy-done.10, f32[2,1024,128]{2,1,0:T(8,128)S(1)} %bitcast.21, ...), custom_call_target="tpu_custom_call" | custom-call | flops 4294967296 | bytes 16777216 | tf_op jit(solution)/shard_map/leaves/pallas_call | solution.py:354
  136.1 1.3 surface.11
  137.6 1.3 surface.10
  138.9 0.7 collective-permute-done.17
  139.7 14.3 %all_to_all.35.got = f32[8,160,128]{2,1,0:T(8,128)S(1)} all-to-all(f32[8,160,128]{2,1,0:T(8,128)S(1)} %add.11), channel_id=1, replica_groups={{0,2,4,6,8,10,12,14},{1,3,5,7,9,11,13,15},{16,18,20,22,24,26,28,30},{17..., dimensions={0} | all-to-all | bytes 1310720 | tf_op jit(solution)/shard_map/all_to_all | solution.py:294
  154.0 0.7 final.1
  (62 shorter events, 1.5 us)
Async XLA Ops:
  0.6 30.3 %copy-start.1 = (f32[1,512,128]{2,1,0:T(8,128)S(1)}, f32[1,512,128]{2,1,0:T(8,128)}, u32[]{:S(2)}) copy-start(f32[1,512,128]{2,1,0:T(8,128)} %param.18) | copy-start | bytes 786436
  0.6 30.3 %copy-start = (f32[1,2,1024,128]{3,2,1,0:T(8,128)S(1)}, f32[1,2,1024,128]{3,2,1,0:T(8,128)}, u32[]{:S(2)}) copy-start(f32[1,2,1024,128]{3,2,1,0:T(8,128)} %param.17) | copy-start | bytes 3145732
  0.7 6.5 %collective-permute-start = (f32[128,128]{1,0:T(8,128)}, f32[128,128]{1,0:T(8,128)S(1)}, u32[]{:S(2)}, u32[]{:S(2)}) collective-permute-start(f32[128,128]{1,0:T(8,128)} %field.3), channel_id=1, source_target_pairs={{0,64},{16,80},{32,96},{48,112},{64,0},{80,16},{96,32},{112,48},{1... | collective-permute-start | bytes 196616 | tf_op jit(solution)/shard_map/ppermute | solution.py:297
  4.7 0.9 copy-start.3
  5.6 0.8 copy-start.7
  6.4 20.2 %copy-start.4 = (f32[128,128]{1,0:T(8,128)S(1)}, f32[128,128]{1,0:T(8,128)}, u32[]{:S(2)}) copy-start(f32[128,128]{1,0:T(8,128)} %field.3) | copy-start | bytes 196612
  6.4 24.5 %copy-start.5 = (f32[1,2,8,128]{3,2,1,0:T(8,128)S(1)}, f32[1,2,8,128]{3,2,1,0:T(8,128)}, u32[]{:S(2)}) copy-start(f32[1,2,8,128]{3,2,1,0:T(8,128)} %param.21) | copy-start | bytes 24580
  6.4 24.5 %copy-start.6 = (f32[1,2,8,128]{3,2,1,0:T(8,128)S(1)}, f32[1,2,8,128]{3,2,1,0:T(8,128)}, u32[]{:S(2)}) copy-start(f32[1,2,8,128]{3,2,1,0:T(8,128)} %param.22) | copy-start | bytes 24580
  6.4 24.5 %copy-start.8 = (s32[1,2,8,1]{2,3,1,0:T(1,128)S(1)}, s32[1,2,8,1]{2,3,1,0:T(1,128)}, u32[]{:S(2)}) copy-start(s32[1,2,8,1]{2,3,1,0:T(1,128)} %param.25) | copy-start | bytes 196
  6.4 24.5 %copy-start.9 = (s32[1,2]{1,0:T(1,128)S(1)}, s32[1,2]{1,0:T(1,128)}, u32[]{:S(2)}) copy-start(s32[1,2]{1,0:T(1,128)} %size_ref.5) | copy-start | bytes 28
  6.4 24.5 %copy-start.10 = (s32[1,2]{1,0:T(1,128)S(1)}, s32[1,2]{1,0:T(1,128)}, u32[]{:S(2)}) copy-start(s32[1,2]{1,0:T(1,128)} %count_ref.5) | copy-start | bytes 28
  26.6 4.3 %collective-permute-start.4 = (f32[8,256,128]{2,1,0:T(8,128)S(1)}, f32[8,256,128]{2,1,0:T(8,128)S(1)}, u32[]{:S(2)}, u32[]{:S(2)}) collective-permute-start(f32[8,256,128]{2,1,0:T(8,128)S(1)} %all_to_all.30.mine), channel_id=1, source_target_pairs={{0,1},{1,0},{2,3},{3,2},{4,5},{5,4},{6,7},{7,6},{8,9},{9,8},{10,11... | collective-permute-start | bytes 3145736 | tf_op jit(solution)/shard_map/ppermute | solution.py:320
  26.6 14.1 %collective-permute-start.3 = (f32[256,128]{1,0:T(8,128)S(1)}, f32[256,128]{1,0:T(8,128)S(1)}, u32[]{:S(2)}, u32[]{:S(2)}) collective-permute-start(f32[256,128]{1,0:T(8,128)S(1)} %constant_dynamic-update-slice_fusion.rest_1_), channel_id=1, source_target_pairs={{0,32},{16,48},{32,0},{48,16},{64,96},{80,112},{96,64},{112,80},{1... | collective-permute-start | bytes 393224 | tf_op jit(solution)/shard_map/ppermute | solution.py:297
  29.7 11.0 %collective-permute-start.2 = (f32[256,128]{1,0:T(8,128)S(1)}, f32[256,128]{1,0:T(8,128)S(1)}, u32[]{:S(2)}, u32[]{:S(2)}) collective-permute-start(f32[256,128]{1,0:T(8,128)S(1)} %constant_dynamic-update-slice_fusion.rest_1_), channel_id=1, source_target_pairs={{0,48},{16,32},{32,16},{48,0},{64,112},{80,96},{96,80},{112,64},{1... | collective-permute-start | bytes 393224 | tf_op jit(solution)/shard_map/ppermute | solution.py:297
  30.9 9.9 %collective-permute-start.1 = (f32[256,128]{1,0:T(8,128)S(1)}, f32[256,128]{1,0:T(8,128)S(1)}, u32[]{:S(2)}, u32[]{:S(2)}) collective-permute-start(f32[256,128]{1,0:T(8,128)S(1)} %constant_dynamic-update-slice_fusion.rest_1_), channel_id=1, source_target_pairs={{0,16},{16,0},{32,48},{48,32},{64,80},{80,64},{96,112},{112,96},{1... | collective-permute-start | bytes 393224 | tf_op jit(solution)/shard_map/ppermute | solution.py:297
  30.9 9.9 %slice-start = ((s8[8388608]{0:T(1024)(128)(4,1)}), s8[4194304]{0:T(1024)(128)(4,1)S(1)}, s32[]{:S(2)}) async-start(s8[8388608]{0:T(1024)(128)(4,1)} %bitcast.17), calls=%async_computation.6 | async-start | bytes 8388608
  31.0 9.9 %slice-start.1 = ((s8[8388608]{0:T(1024)(128)(4,1)}), s8[4194304]{0:T(1024)(128)(4,1)S(1)}, s32[]{:S(2)}) async-start(s8[8388608]{0:T(1024)(128)(4,1)} %bitcast.17), calls=%async_computation.7 | async-start | bytes 8388608
  42.8 2.6 %collective-permute-start.5 = (f32[8,160,128]{2,1,0:T(8,128)S(1)}, f32[8,160,128]{2,1,0:T(8,128)S(1)}, u32[]{:S(2)}, u32[]{:S(2)}) collective-permute-start(f32[8,160,128]{2,1,0:T(8,128)S(1)} %get-tuple-element.66), channel_id=1, source_target_pairs={{0,1},{1,0},{2,3},{3,2},{4,5},{5,4},{6,7},{7,6},{8,9},{9,8},{10,11... | collective-permute-start | bytes 1966088 | tf_op jit(solution)/shard_map/ppermute | solution.py:390
  45.3 15.0 %copy-start.2 = (f32[128,128]{1,0:T(8,128)S(1)}, f32[128,128]{1,0:T(8,128)}, u32[]{:S(2)}) copy-start(f32[128,128]{1,0:T(8,128)} %load.5) | copy-start | bytes 196612
  60.4 5.9 %collective-permute-start.6 = (f32[128,128]{1,0:T(8,128)S(1)}, f32[128,128]{1,0:T(8,128)S(1)}, u32[]{:S(2)}, u32[]{:S(2)}) collective-permute-start(f32[128,128]{1,0:T(8,128)S(1)} %field.4), channel_id=1, source_target_pairs={{0,64},{16,80},{32,96},{48,112},{64,0},{80,16},{96,32},{112,48},{1... | collective-permute-start | bytes 196616 | tf_op jit(solution)/shard_map/ppermute | solution.py:297
  78.6 4.8 %collective-permute-start.10 = (f32[8,160,128]{2,1,0:T(8,128)S(1)}, f32[8,160,128]{2,1,0:T(8,128)S(1)}, u32[]{:S(2)}, u32[]{:S(2)}) collective-permute-start(f32[8,160,128]{2,1,0:T(8,128)S(1)} %all_to_all.32.mine), channel_id=1, source_target_pairs={{0,1},{1,0},{2,3},{3,2},{4,5},{5,4},{6,7},{7,6},{8,9},{9,8},{10,11... | collective-permute-start | bytes 1966088 | tf_op jit(solution)/shard_map/ppermute | solution.py:320
  78.7 10.5 %collective-permute-start.9 = (f32[256,128]{1,0:T(8,128)S(1)}, f32[256,128]{1,0:T(8,128)S(1)}, u32[]{:S(2)}, u32[]{:S(2)}) collective-permute-start(f32[256,128]{1,0:T(8,128)S(1)} %constant_dynamic-update-slice_fusion.2.rest_2_), channel_id=1, source_target_pairs={{0,32},{16,48},{32,0},{48,16},{64,96},{80,112},{96,64},{112,80},{1... | collective-permute-start | bytes 393224 | tf_op jit(solution)/shard_map/ppermute | solution.py:297
  82.3 7.0 %collective-permute-start.8 = (f32[256,128]{1,0:T(8,128)S(1)}, f32[256,128]{1,0:T(8,128)S(1)}, u32[]{:S(2)}, u32[]{:S(2)}) collective-permute-start(f32[256,128]{1,0:T(8,128)S(1)} %constant_dynamic-update-slice_fusion.2.rest_2_), channel_id=1, source_target_pairs={{0,48},{16,32},{32,16},{48,0},{64,112},{80,96},{96,80},{112,64},{1... | collective-permute-start | bytes 393224 | tf_op jit(solution)/shard_map/ppermute | solution.py:297
  83.4 5.9 %collective-permute-start.7 = (f32[256,128]{1,0:T(8,128)S(1)}, f32[256,128]{1,0:T(8,128)S(1)}, u32[]{:S(2)}, u32[]{:S(2)}) collective-permute-start(f32[256,128]{1,0:T(8,128)S(1)} %constant_dynamic-update-slice_fusion.2.rest_2_), channel_id=1, source_target_pairs={{0,16},{16,0},{32,48},{48,32},{64,80},{80,64},{96,112},{112,96},{1... | collective-permute-start | bytes 393224 | tf_op jit(solution)/shard_map/ppermute | solution.py:297
  90.6 2.2 %collective-permute-start.11 = (f32[8,160,128]{2,1,0:T(8,128)S(1)}, f32[8,160,128]{2,1,0:T(8,128)S(1)}, u32[]{:S(2)}, u32[]{:S(2)}) collective-permute-start(f32[8,160,128]{2,1,0:T(8,128)S(1)} %surface.9), channel_id=1, source_target_pairs={{0,1},{1,0},{2,3},{3,2},{4,5},{5,4},{6,7},{7,6},{8,9},{9,8},{10,11... | collective-permute-start | bytes 1966088 | tf_op jit(solution)/shard_map/ppermute | solution.py:390
  107.2 6.1 %collective-permute-start.12 = (f32[128,128]{1,0:T(8,128)S(1)}, f32[128,128]{1,0:T(8,128)S(1)}, u32[]{:S(2)}, u32[]{:S(2)}) collective-permute-start(f32[128,128]{1,0:T(8,128)S(1)} %field.5), channel_id=1, source_target_pairs={{0,64},{16,80},{32,96},{48,112},{64,0},{80,16},{96,32},{112,48},{1... | collective-permute-start | bytes 196616 | tf_op jit(solution)/shard_map/ppermute | solution.py:297
  125.4 4.7 %collective-permute-start.13 = (f32[8,160,128]{2,1,0:T(8,128)S(1)}, f32[8,160,128]{2,1,0:T(8,128)S(1)}, u32[]{:S(2)}, u32[]{:S(2)}) collective-permute-start(f32[8,160,128]{2,1,0:T(8,128)S(1)} %all_to_all.34.mine), channel_id=1, source_target_pairs={{0,1},{1,0},{2,3},{3,2},{4,5},{5,4},{6,7},{7,6},{8,9},{9,8},{10,11... | collective-permute-start | bytes 1966088 | tf_op jit(solution)/shard_map/ppermute | solution.py:320
  125.4 10.7 %collective-permute-start.16 = (f32[256,128]{1,0:T(8,128)S(1)}, f32[256,128]{1,0:T(8,128)S(1)}, u32[]{:S(2)}, u32[]{:S(2)}) collective-permute-start(f32[256,128]{1,0:T(8,128)S(1)} %constant_dynamic-update-slice_fusion.4.rest_2_), channel_id=1, source_target_pairs={{0,32},{16,48},{32,0},{48,16},{64,96},{80,112},{96,64},{112,80},{1... | collective-permute-start | bytes 393224 | tf_op jit(solution)/shard_map/ppermute | solution.py:297
  128.9 7.2 %collective-permute-start.15 = (f32[256,128]{1,0:T(8,128)S(1)}, f32[256,128]{1,0:T(8,128)S(1)}, u32[]{:S(2)}, u32[]{:S(2)}) collective-permute-start(f32[256,128]{1,0:T(8,128)S(1)} %constant_dynamic-update-slice_fusion.4.rest_2_), channel_id=1, source_target_pairs={{0,48},{16,32},{32,16},{48,0},{64,112},{80,96},{96,80},{112,64},{1... | collective-permute-start | bytes 393224 | tf_op jit(solution)/shard_map/ppermute | solution.py:297
  130.1 6.1 %collective-permute-start.14 = (f32[256,128]{1,0:T(8,128)S(1)}, f32[256,128]{1,0:T(8,128)S(1)}, u32[]{:S(2)}, u32[]{:S(2)}) collective-permute-start(f32[256,128]{1,0:T(8,128)S(1)} %constant_dynamic-update-slice_fusion.4.rest_2_), channel_id=1, source_target_pairs={{0,16},{16,0},{32,48},{48,32},{64,80},{80,64},{96,112},{112,96},{1... | collective-permute-start | bytes 393224 | tf_op jit(solution)/shard_map/ppermute | solution.py:297
  137.5 2.2 %collective-permute-start.17 = (f32[8,160,128]{2,1,0:T(8,128)S(1)}, f32[8,160,128]{2,1,0:T(8,128)S(1)}, u32[]{:S(2)}, u32[]{:S(2)}) collective-permute-start(f32[8,160,128]{2,1,0:T(8,128)S(1)} %surface.11), channel_id=1, source_target_pairs={{0,1},{1,0},{2,3},{3,2},{4,5},{5,4},{6,7},{7,6},{8,9},{9,8},{10,11... | collective-permute-start | bytes 1966088 | tf_op jit(solution)/shard_map/ppermute | solution.py:390

commit v4 on v3

--- a/solution.py
+++ b/solution.py
@@ -59,13 +59,21 @@
     return both[:, :n] + both[:, n:] + dot(lo, wide[:, :n])
 
 
-def start_kernel(width, field, schur_t, wide):
+def start_kernel(width, field, schur_t, wide, field_buf, schur_buf, sems):
     share, columns = schur_t.shape
+    copies = [
+        pltpu.make_async_copy(field, field_buf, sems.at[0]),
+        pltpu.make_async_copy(schur_t, schur_buf, sems.at[1]),
+    ]
+    for copy in copies:
+        copy.start()
+    for copy in copies:
+        copy.wait()
     for chip in range(wide.shape[0]):
-        wide[chip, :width] = field[...]
+        wide[chip, :width] = field_buf[...]
         for q in range(columns // width):
             rows = slice(width + q * share, width + (q + 1) * share)
-            wide[chip, rows] = schur_t[:, q * width : (q + 1) * width]
+            wide[chip, rows] = schur_buf[:, q * width : (q + 1) * width]
 
 
 def turn_kernel(width, core_ref, mine, other, hi_ref, lo_ref, whole):
@@ -90,12 +98,12 @@
     load, flux_weight, trace_weight, sep_load, mine, other, *rest,
 ):
     if first:
-        inv, cpl, sol, dense, part, *rest = rest
+        inv, cpl, dense, part, *rest = rest
         inv_hi, inv_lo, cpl_hi, cpl_lo, cpl_t_hi, cpl_t_lo, *rest = rest
         wide, wide_sol, inv_buf, cpl_buf, inv_sems, cpl_sems = rest
     else:
         inv_hi, inv_lo, cpl_t_hi, cpl_t_lo, cpl_hi, cpl_lo, sch_hi, sch_lo, *rest = rest
-        sol, dense, part, wide, wide_sol, gathered = rest
+        *sol, dense, part, wide, wide_sol, gathered = rest
     leaves, order, loads = load.shape
     blocks = order // width
     chips = dense.shape[1]
@@ -103,17 +111,21 @@
     here = here_ref[0]
     core = here % 2
     flux_t, trace_t = flux_weight[...].T, trace_weight[...].T
-    tile = order // 2 if first else order
-
-    def tiles(src, buf, sems):
-        return [
-            pltpu.make_async_copy(src.at[pl.ds(i * tile, tile)], buf.at[i], sems.at[i])
-            for i in range(src.shape[0] // tile)
-        ]
+    half = order // 2
+    cuts = [half // 2, half, order] if first else [order]
+
+    def tiles(src, buf, sems, ends):
+        return {
+            end: pltpu.make_async_copy(src.at[pl.ds(start, end - start)], buf.at[pl.ds(start, end - start)], sems.at[i])
+            for i, (start, end) in enumerate(zip([0, *ends], ends))
+        }
 
     if first:
-        inv_copies, cpl_copies = tiles(inv, inv_buf, inv_sems), tiles(cpl, cpl_buf, cpl_sems)
-        for copy in inv_copies + cpl_copies:
+        inv_ends = [j * order + cut for j in range(leaves) for cut in cuts]
+        cpl_ends = [(i + 1) * half for i in range(2 * leaves)]
+        inv_copies = tiles(inv, inv_buf, inv_sems, inv_ends)
+        cpl_copies = tiles(cpl, cpl_buf, cpl_sems, cpl_ends)
+        for copy in [*inv_copies.values(), *cpl_copies.values()]:
             copy.start()
 
     def scale(turned, j, k):
@@ -146,33 +158,33 @@
             if not first:
                 rhs = rhs - pulled[at]
             wide[j, at] = widened(live(j, k, rhs))
-        for t in range(order // tile):
-            start = j * order + t * tile
-            rows = slice(start, start + tile)
+        for begin, end in zip([0, *cuts], cuts):
+            start = j * order + begin
+            rows = slice(start, j * order + end)
             if first:
-                i = start // tile
-                inv_copies[i].wait()
-                hi, lo = parted(inv_buf[i])
+                inv_copies[j * order + end].wait()
+                hi, lo = parted(inv_buf[rows])
                 inv_hi[rows], inv_lo[rows] = hi, lo
                 got = product(hi, lo, wide[j])
             else:
                 got = product(inv_hi[rows], inv_lo[rows], wide[j])
-            for b in range(tile // width):
-                k = t * (tile // width) + b
+            for b in range((end - begin) // width):
+                k = begin // width + b
                 o = owner_ref[0, j, 0, k]
                 chip = o // 2
                 block = live(j, k, got[b * width : (b + 1) * width])
-                sol[j, k * width : (k + 1) * width] = block
+                if last:
+                    sol[0][j, k * width : (k + 1) * width] = block
                 dense[o - 2 * chip, chip] += block * scale(trace_t, j, k)
                 at = slice(start + b * width, start + (b + 1) * width)
                 wide_sol[at] = widened(block)
     left = jnp.where(here == 0, sep_load[...], 0.0)
     if first:
-        for i, copy in enumerate(cpl_copies):
+        for end, copy in cpl_copies.items():
             copy.wait()
-            rows = slice(i * tile, (i + 1) * tile)
-            cpl_hi[rows], cpl_lo[rows] = parted(cpl_buf[i])
-            hi, lo = parted(cpl_buf[i].T)
+            rows = slice(end - half, end)
+            cpl_hi[rows], cpl_lo[rows] = parted(cpl_buf[rows])
+            hi, lo = parted(cpl_buf[rows].T)
             cpl_t_hi[:, rows], cpl_t_lo[:, rows] = hi, lo
             left = left - product(hi, lo, wide_sol[rows])
     else:
@@ -303,9 +315,14 @@
         functools.partial(start_kernel, width),
         "start",
         shaped((chips, 2 * width, loads)),
-        [VM] * 2,
+        [HB] * 2,
+        [
+            pltpu.VMEM((width, loads), F32),
+            pltpu.VMEM((share, separator), F32),
+            pltpu.SemaphoreType.DMA((2,)),
+        ],
         moved=MIB,
-    )(surf_start, schur_inverse[0].T)
+    )(*(pltpu.with_memory_space_constraint(x, pltpu.HBM) for x in (surf_start, schur_inverse[0].T)))
     wide, here_id, mine_id, other_id, group, owner = lax.optimization_barrier(
         (wide, here_id, mine_id, other_id, group, block_owner.transpose(0, 1, 3, 2))
     )
@@ -321,8 +338,8 @@
         operands = [here_id, owner, leaf_sizes, block_counts, leaf_load[0]]
         operands += [w.reshape(entries, width) for w in (flux_weight, trace_weight)]
         operands += [sep_load[0], mine, other]
-        outs = [
-            shaped((leaves, order, loads)),
+        outs = [shaped((leaves, order, loads))] if last else []
+        outs += [
             shaped((2, chips, width, loads)),
             shaped((separator, loads)),
         ]
@@ -343,15 +360,15 @@
             outs += [shaped(inv.shape, BF16)] * 2 + [shaped(cpl.shape, BF16)] * 2
             outs += [shaped(cpl.shape[::-1], BF16)] * 2
             scratch += [
-                pltpu.VMEM((2 * leaves, order // 2, order), F32),
-                pltpu.VMEM((2 * leaves, order // 2, separator), F32),
-                pltpu.SemaphoreType.DMA((2 * leaves,)),
+                pltpu.VMEM(inv.shape, F32),
+                pltpu.VMEM(cpl.shape, F32),
+                pltpu.SemaphoreType.DMA((3 * leaves,)),
                 pltpu.SemaphoreType.DMA((2 * leaves,)),
             ]
         else:
             matrices = [inv_hi, inv_lo, cpl_t_hi, cpl_t_lo, cpl_hi, cpl_lo, sch_hi, sch_lo]
             scratch += [pltpu.VMEM((separator, loads), F32)]
-        solution, dense, part, *made = call(
+        made = call(
             functools.partial(leaf_kernel, width, first, last),
             "leaves",
             tuple(outs),
@@ -362,7 +379,9 @@
             moved=16 * MIB,
         )(*operands, *matrices)
         if first:
-            inv_hi, inv_lo, cpl_hi, cpl_lo, cpl_t_hi, cpl_t_lo = made
+            dense, part, inv_hi, inv_lo, cpl_hi, cpl_lo, cpl_t_hi, cpl_t_lo = made
+        else:
+            *solution, dense, part = made
 
         def surface(pick, matrix):
             half = (rows // 2, columns)
@@ -413,7 +432,7 @@
         [VM] * 2,
         moved=MIB,
     )(got, surf_load)
-    return (solution[None], sep_rows[None], pressure)
+    return (solution[0][None], sep_rows[None], pressure)
 
 
 def solution(mesh):

time: 156 us -> 155 us (level)
  local copies, waits for them, and re-layouts: 1.8 us -> 0.09 us
    unnamed x29 -> x25, local copies, waits for them, and re-layouts: 1.77 us -> 0.06 us
  transfers between devices with their start and end apart: 18 -> 18, of which waited for: 6 -> 6; matrix products, arithmetic and copies ran while one was open for 0% -> 0% of each run, Pallas kernels for 17% -> 18%
where the time goes in v4:
time: 155 us
  blocking collectives  87.4 us (56%)
  Pallas kernels  32.6 us (21%)
  starting transfers between devices  25.7 us (17%)
  waiting for transfers between devices  7.54 us (5%)
    all_to_all x6, blocking collectives, over_chips(): lax.all_to_all(x, 'sub', 0, 0, axis_index_groups=same_core, tiled=True)  87.4 us
    ppermute x12, starting transfers between devices, exchanged(): return lax.ppermute(x, 'grp', [(i, i ^ step) for i in range(groups)])  25.2 us
    pallas_call x3, Pallas kernels, on_device(): call(functools.partial(leaf_kernel, width, first, last), 'leaves', tuple(...  21.3 us
    pallas_call x6, Pallas kernels, surface(): call(functools.partial(surface_kernel, width, first), 'surface', (payload...  9.2 us
    ppermute x12, waiting for transfers between devices, exchanged(): return lax.ppermute(x, 'grp', [(i, i ^ step) for i in range(groups)])  6.05 us
  transfers between devices with their start and end apart: 18, of which 6 were waited for; matrix products, arithmetic and copies ran while one was open for 0% of the time, Pallas kernels for 18%

profile of v4, /device:TPU:0, one launch (start us, length us, event | category | flops | bytes accessed | tf_op | source)
XLA Modules:
  0.0 154.5 jit_solution(9289939420527588412)
XLA Ops:
  0.7 4.0 %collective-permute-start = (f32[128,128]{1,0:T(8,128)}, f32[128,128]{1,0:T(8,128)S(1)}, u32[]{:S(2)}, u32[]{:S(2)}) collective-permute-start(f32[128,128]{1,0:T(8,128)} %field.3), channel_id=1, source_target_pairs={{0,64},{16,80},{32,96},{48,112},{64,0},{80,16},{96,32},{112,48},{1... | collective-permute-start | bytes 196616 | tf_op jit(solution)/shard_map/ppermute | solution.py:309
  4.8 1.0 start.1
  5.7 1.5 collective-permute-done
  7.2 19.5 %all_to_all.30.mine = f32[8,256,128]{2,1,0:T(8,128)S(1)} all-to-all(f32[8,256,128]{2,1,0:T(8,128)S(1)} %start.1), channel_id=1, replica_groups={{0,2,4,6,8,10,12,14},{1,3,5,7,9,11,13,15},{16,18,20,22,24,26,28,30},{17..., dimensions={0} | all-to-all | bytes 2097152 | tf_op jit(solution)/shard_map/all_to_all | solution.py:306
  26.7 3.1 %collective-permute-start.3 = (f32[256,128]{1,0:T(8,128)S(1)}, f32[256,128]{1,0:T(8,128)S(1)}, u32[]{:S(2)}, u32[]{:S(2)}) collective-permute-start(f32[256,128]{1,0:T(8,128)S(1)} %constant_dynamic-update-slice_fusion.rest_1_), channel_id=1, source_target_pairs={{0,32},{16,48},{32,0},{48,16},{64,96},{80,112},{96,64},{112,80},{1... | collective-permute-start | bytes 393224 | tf_op jit(solution)/shard_map/ppermute | solution.py:309
  29.8 1.1 collective-permute-start.2
  31.0 9.6 %leaves.3 = (f32[2,8,128,128]{3,2,1,0:T(8,128)S(1)}, f32[512,128]{1,0:T(8,128)S(1)}, bf16[2048,1024]{1,0:T(8,128)(2,1)S(1)}, bf16[2048,1024]{1,0:T(8,128)(2,1)S(...) custom-call(s32[1]{0:T(128)} %bitcast.2.here_ref, ...), custom_call_target="tpu_custom_call" | custom-call | flops 4294967296 | bytes 16777216 | tf_op jit(solution)/shard_map/leaves/pallas_call | solution.py:371
  40.7 1.9 %surface.7 = (f32[8,160,128]{2,1,0:T(8,128)S(1)}, bf16[1024,1024]{1,0:T(8,128)(2,1)S(1)}, bf16[1024,1024]{1,0:T(8,128)(2,1)S(1)}) custom-call(s32[1]{0:T(128)} %bitcast.4.pick_ref, s32[1]{0:T(128)} %bitcast.5.group_ref, f32[2048,1024]{1,0:T(8,128)S(1)} %bitcast.18, f32[256,128]{1,0:T(8,128)S(1)} %constant_dynamic-update-slice_fusion.rest_1_, ...), custom_call_target="tpu_custom_call" | custom-call | flops 1073741824 | bytes 6291456 | tf_op jit(solution)/shard_map/surface/pallas_call | solution.py:395
  42.9 0.3 split_schur.1
  43.3 1.9 %surface.6 = (f32[8,160,128]{2,1,0:T(8,128)S(1)}, bf16[1024,1024]{1,0:T(8,128)(2,1)S(1)}, bf16[1024,1024]{1,0:T(8,128)(2,1)S(1)}) custom-call(s32[1]{0:T(128)} %bitcast.3.pick_ref.core_ref, s32[1]{0:T(128)} %bitcast.5.group_ref, f32[2048,1024]{1,0:T(8,128)S(1)} %bitcast.18, f32[256,128]{1,0:T(8,128)S(1)} %constant_dynamic-update-slice_fusion.rest_1_, ...), custom_call_target="tpu_custom_call" | custom-call | flops 1073741824 | bytes 6291456 | tf_op jit(solution)/shard_map/surface/pallas_call | solution.py:395
  45.3 14.9 %all_to_all.31.got = f32[8,160,128]{2,1,0:T(8,128)S(1)} all-to-all(f32[8,160,128]{2,1,0:T(8,128)S(1)} %add.9), channel_id=1, replica_groups={{0,2,4,6,8,10,12,14},{1,3,5,7,9,11,13,15},{16,18,20,22,24,26,28,30},{17..., dimensions={0} | all-to-all | bytes 1310720 | tf_op jit(solution)/shard_map/all_to_all | solution.py:306
  60.2 3.7 %collective-permute-start.6 = (f32[128,128]{1,0:T(8,128)S(1)}, f32[128,128]{1,0:T(8,128)S(1)}, u32[]{:S(2)}, u32[]{:S(2)}) collective-permute-start(f32[128,128]{1,0:T(8,128)S(1)} %field.4), channel_id=1, source_target_pairs={{0,64},{16,80},{32,96},{48,112},{64,0},{80,16},{96,32},{112,48},{1... | collective-permute-start | bytes 196616 | tf_op jit(solution)/shard_map/ppermute | solution.py:309
  63.9 2.2 %collective-permute-done.6 = f32[128,128]{1,0:T(8,128)S(1)} collective-permute-done((f32[128,128]{1,0:T(8,128)S(1)}, f32[128,128]{1,0:T(8,128)S(1)}, u32[]{:S(2)}, u32[]{:S(2)}) %collective-permute-start.6) | collective-permute-done | bytes 65568 | tf_op jit(solution)/shard_map/ppermute | solution.py:309
  66.1 12.4 %all_to_all.32.mine = f32[8,160,128]{2,1,0:T(8,128)S(1)} all-to-all(f32[8,160,128]{2,1,0:T(8,128)S(1)} %wide.2), channel_id=1, replica_groups={{0,2,4,6,8,10,12,14},{1,3,5,7,9,11,13,15},{16,18,20,22,24,26,28,30},{17..., dimensions={0} | all-to-all | bytes 1310720 | tf_op jit(solution)/shard_map/all_to_all | solution.py:306
  78.5 3.6 %collective-permute-start.9 = (f32[256,128]{1,0:T(8,128)S(1)}, f32[256,128]{1,0:T(8,128)S(1)}, u32[]{:S(2)}, u32[]{:S(2)}) collective-permute-start(f32[256,128]{1,0:T(8,128)S(1)} %constant_dynamic-update-slice_fusion.2.rest_2_), channel_id=1, source_target_pairs={{0,32},{16,48},{32,0},{48,16},{64,96},{80,112},{96,64},{112,80},{1... | collective-permute-start | bytes 393224 | tf_op jit(solution)/shard_map/ppermute | solution.py:309
  82.1 1.1 collective-permute-start.8
  83.3 5.7 %leaves.4 = (f32[2,8,128,128]{3,2,1,0:T(8,128)S(1)}, f32[512,128]{1,0:T(8,128)S(1)}) custom-call(s32[1]{0:T(128)} %bitcast.2.here_ref, s32[1,2,1,8]{3,2,1,0:T(1,128)S(1)} %bitcast.32, s32[1,2]{1,0:T(1,128)S(1)} %copy-done.6, s32[1,2]{1,0:T(1,128)S(1)} %copy-done.7, f32[2,1024,128]{2,1,0:T(8,128)S(1)} %bitcast.20, f32[16,128]{1,0:T(8,128)S(1)} %bitcast.26, ...), custom_call_target="tpu_custom_call" | custom-call | flops 4294967296 | bytes 16777216 | tf_op jit(solution)/shard_map/leaves/pallas_call | solution.py:371
  89.1 1.3 surface.9
  90.6 1.3 surface.8
  91.9 0.7 collective-permute-done.11
  92.7 14.3 %all_to_all.33.got = f32[8,160,128]{2,1,0:T(8,128)S(1)} all-to-all(f32[8,160,128]{2,1,0:T(8,128)S(1)} %add.10), channel_id=1, replica_groups={{0,2,4,6,8,10,12,14},{1,3,5,7,9,11,13,15},{16,18,20,22,24,26,28,30},{17..., dimensions={0} | all-to-all | bytes 1310720 | tf_op jit(solution)/shard_map/all_to_all | solution.py:306
  107.1 3.9 %collective-permute-start.12 = (f32[128,128]{1,0:T(8,128)S(1)}, f32[128,128]{1,0:T(8,128)S(1)}, u32[]{:S(2)}, u32[]{:S(2)}) collective-permute-start(f32[128,128]{1,0:T(8,128)S(1)} %field.5), channel_id=1, source_target_pairs={{0,64},{16,80},{32,96},{48,112},{64,0},{80,16},{96,32},{112,48},{1... | collective-permute-start | bytes 196616 | tf_op jit(solution)/shard_map/ppermute | solution.py:309
  111.0 2.2 %collective-permute-done.12 = f32[128,128]{1,0:T(8,128)S(1)} collective-permute-done((f32[128,128]{1,0:T(8,128)S(1)}, f32[128,128]{1,0:T(8,128)S(1)}, u32[]{:S(2)}, u32[]{:S(2)}) %collective-permute-start.12) | collective-permute-done | bytes 65568 | tf_op jit(solution)/shard_map/ppermute | solution.py:309
  113.2 12.0 %all_to_all.34.mine = f32[8,160,128]{2,1,0:T(8,128)S(1)} all-to-all(f32[8,160,128]{2,1,0:T(8,128)S(1)} %wide.3), channel_id=1, replica_groups={{0,2,4,6,8,10,12,14},{1,3,5,7,9,11,13,15},{16,18,20,22,24,26,28,30},{17..., dimensions={0} | all-to-all | bytes 1310720 | tf_op jit(solution)/shard_map/all_to_all | solution.py:306
  125.3 3.5 %collective-permute-start.16 = (f32[256,128]{1,0:T(8,128)S(1)}, f32[256,128]{1,0:T(8,128)S(1)}, u32[]{:S(2)}, u32[]{:S(2)}) collective-permute-start(f32[256,128]{1,0:T(8,128)S(1)} %constant_dynamic-update-slice_fusion.4.rest_2_), channel_id=1, source_target_pairs={{0,32},{16,48},{32,0},{48,16},{64,96},{80,112},{96,64},{112,80},{1... | collective-permute-start | bytes 393224 | tf_op jit(solution)/shard_map/ppermute | solution.py:309
  128.8 1.1 collective-permute-start.15
  129.9 6.0 %leaves.5 = (f32[2,1024,128]{2,1,0:T(8,128)}, f32[2,8,128,128]{3,2,1,0:T(8,128)S(1)}, f32[512,128]{1,0:T(8,128)S(1)}) custom-call(s32[1]{0:T(128)} %bitcast.2.here_ref, s32[1,2,1,8]{3,2,1,0:T(1,128)S(1)} %bitcast.33, s32[1,2]{1,0:T(1,128)S(1)} %copy-done.6, s32[1,2]{1,0:T(1,128)S(1)} %copy-done.7, f32[2,1024,128]{2,1,0:T(8,128)S(1)} %bitcast.21, ...), custom_call_target="tpu_custom_call" | custom-call | flops 4294967296 | bytes 16777216 | tf_op jit(solution)/shard_map/leaves/pallas_call | solution.py:371
  136.0 1.3 surface.11
  137.4 1.3 surface.10
  138.8 0.7 collective-permute-done.17
  139.6 14.3 %all_to_all.35.got = f32[8,160,128]{2,1,0:T(8,128)S(1)} all-to-all(f32[8,160,128]{2,1,0:T(8,128)S(1)} %add.11), channel_id=1, replica_groups={{0,2,4,6,8,10,12,14},{1,3,5,7,9,11,13,15},{16,18,20,22,24,26,28,30},{17..., dimensions={0} | all-to-all | bytes 1310720 | tf_op jit(solution)/shard_map/all_to_all | solution.py:306
  153.9 0.7 final.1
  (58 shorter events, 1.1 us)
Async XLA Ops:
  0.6 26.0 %copy-start.8 = (f32[128,128]{1,0:T(8,128)S(1)}, f32[128,128]{1,0:T(8,128)}, u32[]{:S(2)}) copy-start(f32[128,128]{1,0:T(8,128)} %field.3) | copy-start | bytes 196612
  0.6 30.3 %copy-start.5 = (s32[1,2,8,1]{2,3,1,0:T(1,128)S(1)}, s32[1,2,8,1]{2,3,1,0:T(1,128)}, u32[]{:S(2)}) copy-start(s32[1,2,8,1]{2,3,1,0:T(1,128)} %param.25) | copy-start | bytes 196
  0.7 30.3 %copy-start.7 = (s32[1,2]{1,0:T(1,128)S(1)}, s32[1,2]{1,0:T(1,128)}, u32[]{:S(2)}) copy-start(s32[1,2]{1,0:T(1,128)} %count_ref.5) | copy-start | bytes 28
  0.7 30.3 %copy-start.6 = (s32[1,2]{1,0:T(1,128)S(1)}, s32[1,2]{1,0:T(1,128)}, u32[]{:S(2)}) copy-start(s32[1,2]{1,0:T(1,128)} %size_ref.5) | copy-start | bytes 28
  0.7 30.3 %copy-start.4 = (f32[1,2,8,128]{3,2,1,0:T(8,128)S(1)}, f32[1,2,8,128]{3,2,1,0:T(8,128)}, u32[]{:S(2)}) copy-start(f32[1,2,8,128]{3,2,1,0:T(8,128)} %param.22) | copy-start | bytes 24580
  0.7 30.3 %copy-start.3 = (f32[1,2,8,128]{3,2,1,0:T(8,128)S(1)}, f32[1,2,8,128]{3,2,1,0:T(8,128)}, u32[]{:S(2)}) copy-start(f32[1,2,8,128]{3,2,1,0:T(8,128)} %param.21) | copy-start | bytes 24580
  0.7 30.3 %copy-start.1 = (f32[1,512,128]{2,1,0:T(8,128)S(1)}, f32[1,512,128]{2,1,0:T(8,128)}, u32[]{:S(2)}) copy-start(f32[1,512,128]{2,1,0:T(8,128)} %param.18) | copy-start | bytes 786436
  0.7 30.3 %copy-start = (f32[1,2,1024,128]{3,2,1,0:T(8,128)S(1)}, f32[1,2,1024,128]{3,2,1,0:T(8,128)}, u32[]{:S(2)}) copy-start(f32[1,2,1024,128]{3,2,1,0:T(8,128)} %param.17) | copy-start | bytes 3145732
  0.7 6.5 %collective-permute-start = (f32[128,128]{1,0:T(8,128)}, f32[128,128]{1,0:T(8,128)S(1)}, u32[]{:S(2)}, u32[]{:S(2)}) collective-permute-start(f32[128,128]{1,0:T(8,128)} %field.3), channel_id=1, source_target_pairs={{0,64},{16,80},{32,96},{48,112},{64,0},{80,16},{96,32},{112,48},{1... | collective-permute-start | bytes 196616 | tf_op jit(solution)/shard_map/ppermute | solution.py:309
  26.7 4.3 %collective-permute-start.4 = (f32[8,256,128]{2,1,0:T(8,128)S(1)}, f32[8,256,128]{2,1,0:T(8,128)S(1)}, u32[]{:S(2)}, u32[]{:S(2)}) collective-permute-start(f32[8,256,128]{2,1,0:T(8,128)S(1)} %all_to_all.30.mine), channel_id=1, source_target_pairs={{0,1},{1,0},{2,3},{3,2},{4,5},{5,4},{6,7},{7,6},{8,9},{9,8},{10,11... | collective-permute-start | bytes 3145736 | tf_op jit(solution)/shard_map/ppermute | solution.py:337
  26.7 13.9 %collective-permute-start.3 = (f32[256,128]{1,0:T(8,128)S(1)}, f32[256,128]{1,0:T(8,128)S(1)}, u32[]{:S(2)}, u32[]{:S(2)}) collective-permute-start(f32[256,128]{1,0:T(8,128)S(1)} %constant_dynamic-update-slice_fusion.rest_1_), channel_id=1, source_target_pairs={{0,32},{16,48},{32,0},{48,16},{64,96},{80,112},{96,64},{112,80},{1... | collective-permute-start | bytes 393224 | tf_op jit(solution)/shard_map/ppermute | solution.py:309
  29.8 10.8 %collective-permute-start.2 = (f32[256,128]{1,0:T(8,128)S(1)}, f32[256,128]{1,0:T(8,128)S(1)}, u32[]{:S(2)}, u32[]{:S(2)}) collective-permute-start(f32[256,128]{1,0:T(8,128)S(1)} %constant_dynamic-update-slice_fusion.rest_1_), channel_id=1, source_target_pairs={{0,48},{16,32},{32,16},{48,0},{64,112},{80,96},{96,80},{112,64},{1... | collective-permute-start | bytes 393224 | tf_op jit(solution)/shard_map/ppermute | solution.py:309
  30.9 9.7 %collective-permute-start.1 = (f32[256,128]{1,0:T(8,128)S(1)}, f32[256,128]{1,0:T(8,128)S(1)}, u32[]{:S(2)}, u32[]{:S(2)}) collective-permute-start(f32[256,128]{1,0:T(8,128)S(1)} %constant_dynamic-update-slice_fusion.rest_1_), channel_id=1, source_target_pairs={{0,16},{16,0},{32,48},{48,32},{64,80},{80,64},{96,112},{112,96},{1... | collective-permute-start | bytes 393224 | tf_op jit(solution)/shard_map/ppermute | solution.py:309
  30.9 9.7 %slice-start = ((s8[8388608]{0:T(1024)(128)(4,1)}), s8[4194304]{0:T(1024)(128)(4,1)S(1)}, s32[]{:S(2)}) async-start(s8[8388608]{0:T(1024)(128)(4,1)} %bitcast.17), calls=%async_computation.6 | async-start | bytes 8388608
  31.0 9.6 %slice-start.1 = ((s8[8388608]{0:T(1024)(128)(4,1)}), s8[4194304]{0:T(1024)(128)(4,1)S(1)}, s32[]{:S(2)}) async-start(s8[8388608]{0:T(1024)(128)(4,1)} %bitcast.17), calls=%async_computation.7 | async-start | bytes 8388608
  42.6 2.6 %collective-permute-start.5 = (f32[8,160,128]{2,1,0:T(8,128)S(1)}, f32[8,160,128]{2,1,0:T(8,128)S(1)}, u32[]{:S(2)}, u32[]{:S(2)}) collective-permute-start(f32[8,160,128]{2,1,0:T(8,128)S(1)} %get-tuple-element.66), channel_id=1, source_target_pairs={{0,1},{1,0},{2,3},{3,2},{4,5},{5,4},{6,7},{7,6},{8,9},{9,8},{10,11... | collective-permute-start | bytes 1966088 | tf_op jit(solution)/shard_map/ppermute | solution.py:409
  45.2 15.0 %copy-start.2 = (f32[128,128]{1,0:T(8,128)S(1)}, f32[128,128]{1,0:T(8,128)}, u32[]{:S(2)}) copy-start(f32[128,128]{1,0:T(8,128)} %load.5) | copy-start | bytes 196612
  60.2 5.9 %collective-permute-start.6 = (f32[128,128]{1,0:T(8,128)S(1)}, f32[128,128]{1,0:T(8,128)S(1)}, u32[]{:S(2)}, u32[]{:S(2)}) collective-permute-start(f32[128,128]{1,0:T(8,128)S(1)} %field.4), channel_id=1, source_target_pairs={{0,64},{16,80},{32,96},{48,112},{64,0},{80,16},{96,32},{112,48},{1... | collective-permute-start | bytes 196616 | tf_op jit(solution)/shard_map/ppermute | solution.py:309
  78.5 4.8 %collective-permute-start.10 = (f32[8,160,128]{2,1,0:T(8,128)S(1)}, f32[8,160,128]{2,1,0:T(8,128)S(1)}, u32[]{:S(2)}, u32[]{:S(2)}) collective-permute-start(f32[8,160,128]{2,1,0:T(8,128)S(1)} %all_to_all.32.mine), channel_id=1, source_target_pairs={{0,1},{1,0},{2,3},{3,2},{4,5},{5,4},{6,7},{7,6},{8,9},{9,8},{10,11... | collective-permute-start | bytes 1966088 | tf_op jit(solution)/shard_map/ppermute | solution.py:337
  78.5 10.5 %collective-permute-start.9 = (f32[256,128]{1,0:T(8,128)S(1)}, f32[256,128]{1,0:T(8,128)S(1)}, u32[]{:S(2)}, u32[]{:S(2)}) collective-permute-start(f32[256,128]{1,0:T(8,128)S(1)} %constant_dynamic-update-slice_fusion.2.rest_2_), channel_id=1, source_target_pairs={{0,32},{16,48},{32,0},{48,16},{64,96},{80,112},{96,64},{112,80},{1... | collective-permute-start | bytes 393224 | tf_op jit(solution)/shard_map/ppermute | solution.py:309
  82.1 7.0 %collective-permute-start.8 = (f32[256,128]{1,0:T(8,128)S(1)}, f32[256,128]{1,0:T(8,128)S(1)}, u32[]{:S(2)}, u32[]{:S(2)}) collective-permute-start(f32[256,128]{1,0:T(8,128)S(1)} %constant_dynamic-update-slice_fusion.2.rest_2_), channel_id=1, source_target_pairs={{0,48},{16,32},{32,16},{48,0},{64,112},{80,96},{96,80},{112,64},{1... | collective-permute-start | bytes 393224 | tf_op jit(solution)/shard_map/ppermute | solution.py:309
  83.3 5.9 %collective-permute-start.7 = (f32[256,128]{1,0:T(8,128)S(1)}, f32[256,128]{1,0:T(8,128)S(1)}, u32[]{:S(2)}, u32[]{:S(2)}) collective-permute-start(f32[256,128]{1,0:T(8,128)S(1)} %constant_dynamic-update-slice_fusion.2.rest_2_), channel_id=1, source_target_pairs={{0,16},{16,0},{32,48},{48,32},{64,80},{80,64},{96,112},{112,96},{1... | collective-permute-start | bytes 393224 | tf_op jit(solution)/shard_map/ppermute | solution.py:309
  90.5 2.2 %collective-permute-start.11 = (f32[8,160,128]{2,1,0:T(8,128)S(1)}, f32[8,160,128]{2,1,0:T(8,128)S(1)}, u32[]{:S(2)}, u32[]{:S(2)}) collective-permute-start(f32[8,160,128]{2,1,0:T(8,128)S(1)} %surface.9), channel_id=1, source_target_pairs={{0,1},{1,0},{2,3},{3,2},{4,5},{5,4},{6,7},{7,6},{8,9},{9,8},{10,11... | collective-permute-start | bytes 1966088 | tf_op jit(solution)/shard_map/ppermute | solution.py:409
  107.1 6.1 %collective-permute-start.12 = (f32[128,128]{1,0:T(8,128)S(1)}, f32[128,128]{1,0:T(8,128)S(1)}, u32[]{:S(2)}, u32[]{:S(2)}) collective-permute-start(f32[128,128]{1,0:T(8,128)S(1)} %field.5), channel_id=1, source_target_pairs={{0,64},{16,80},{32,96},{48,112},{64,0},{80,16},{96,32},{112,48},{1... | collective-permute-start | bytes 196616 | tf_op jit(solution)/shard_map/ppermute | solution.py:309
  125.2 4.7 %collective-permute-start.13 = (f32[8,160,128]{2,1,0:T(8,128)S(1)}, f32[8,160,128]{2,1,0:T(8,128)S(1)}, u32[]{:S(2)}, u32[]{:S(2)}) collective-permute-start(f32[8,160,128]{2,1,0:T(8,128)S(1)} %all_to_all.34.mine), channel_id=1, source_target_pairs={{0,1},{1,0},{2,3},{3,2},{4,5},{5,4},{6,7},{7,6},{8,9},{9,8},{10,11... | collective-permute-start | bytes 1966088 | tf_op jit(solution)/shard_map/ppermute | solution.py:337
  125.3 10.7 %collective-permute-start.16 = (f32[256,128]{1,0:T(8,128)S(1)}, f32[256,128]{1,0:T(8,128)S(1)}, u32[]{:S(2)}, u32[]{:S(2)}) collective-permute-start(f32[256,128]{1,0:T(8,128)S(1)} %constant_dynamic-update-slice_fusion.4.rest_2_), channel_id=1, source_target_pairs={{0,32},{16,48},{32,0},{48,16},{64,96},{80,112},{96,64},{112,80},{1... | collective-permute-start | bytes 393224 | tf_op jit(solution)/shard_map/ppermute | solution.py:309
  128.8 7.2 %collective-permute-start.15 = (f32[256,128]{1,0:T(8,128)S(1)}, f32[256,128]{1,0:T(8,128)S(1)}, u32[]{:S(2)}, u32[]{:S(2)}) collective-permute-start(f32[256,128]{1,0:T(8,128)S(1)} %constant_dynamic-update-slice_fusion.4.rest_2_), channel_id=1, source_target_pairs={{0,48},{16,32},{32,16},{48,0},{64,112},{80,96},{96,80},{112,64},{1... | collective-permute-start | bytes 393224 | tf_op jit(solution)/shard_map/ppermute | solution.py:309
  129.9 6.1 %collective-permute-start.14 = (f32[256,128]{1,0:T(8,128)S(1)}, f32[256,128]{1,0:T(8,128)S(1)}, u32[]{:S(2)}, u32[]{:S(2)}) collective-permute-start(f32[256,128]{1,0:T(8,128)S(1)} %constant_dynamic-update-slice_fusion.4.rest_2_), channel_id=1, source_target_pairs={{0,16},{16,0},{32,48},{48,32},{64,80},{80,64},{96,112},{112,96},{1... | collective-permute-start | bytes 393224 | tf_op jit(solution)/shard_map/ppermute | solution.py:309
  137.3 2.2 %collective-permute-start.17 = (f32[8,160,128]{2,1,0:T(8,128)S(1)}, f32[8,160,128]{2,1,0:T(8,128)S(1)}, u32[]{:S(2)}, u32[]{:S(2)}) collective-permute-start(f32[8,160,128]{2,1,0:T(8,128)S(1)} %surface.11), channel_id=1, source_target_pairs={{0,1},{1,0},{2,3},{3,2},{4,5},{5,4},{6,7},{7,6},{8,9},{9,8},{10,11... | collective-permute-start | bytes 1966088 | tf_op jit(solution)/shard_map/ppermute | solution.py:409

commit v5 on v4

--- a/solution.py
+++ b/solution.py
@@ -194,12 +194,19 @@
     part[...] = left
 
 
-def surface_kernel(width, first, pick_ref, group_ref, *rest):
-    if first:
-        src, *rest, out, hi_ref, lo_ref, wide, buf, sems = rest
+def surface_kernel(width, first, made, pick_ref, group_ref, *rest):
+    if first:
+        src, *rest, buf, sems = rest
     else:
-        hi_ref, lo_ref, *rest, out, wide = rest
-    *pieces, dense, part = rest
+        hi_ref, lo_ref, *rest = rest
+    if made:
+        wide, dense, part, out, *rest = rest
+        pieces = []
+    else:
+        *pieces, dense, part, out, wide = rest[:-2] if first else rest
+        rest = rest[-2:]
+    if first:
+        hi_ref, lo_ref = rest
     pick = pick_ref[0]
     chips = out.shape[0]
     share = part.shape[0] // (2 * chips)
@@ -383,31 +390,33 @@
         else:
             *solution, dense, part = made
 
-        def surface(pick, matrix):
+        def surface(pick, matrix, column, made):
             half = (rows // 2, columns)
             payload = shaped((chips, width + share, loads))
-            scratch = [pltpu.VMEM((columns, 2 * loads), BF16)]
+            scratch = []
             if first:
-                scratch += [
+                scratch = [
                     pltpu.VMEM((2, rows // 4, columns), F32),
                     pltpu.SemaphoreType.DMA((2, chips // 2)),
                 ]
+            outs = [payload] + ([] if made else [shaped((columns, 2 * loads), BF16)])
+            outs += [shaped(half, BF16)] * 2 if first else []
             return call(
-                functools.partial(surface_kernel, width, first),
+                functools.partial(surface_kernel, width, first, made),
                 "surface",
-                (payload, shaped(half, BF16), shaped(half, BF16)) if first else (payload,),
-                [SM] * 2 + [HB if first else VM] * len(matrix) + [VM] * (2 + len(pieces)),
+                tuple(outs),
+                [SM] * 2 + [HB if first else VM] * len(matrix) + [VM] * (2 + len(column)),
                 scratch,
                 limit=14 if first else 8,
                 flops=4 * rows * columns * loads,
                 moved=6 * MIB,
-            )(pick, group, *matrix, *pieces, dense, part)
+            )(pick, group, *matrix, *column, dense, part)
 
         if first:
             bem_other, bem_mine = [bem_tiles], [bem_tiles]
-        away, *made_other = surface(other_id, bem_other)
+        away, split_column, *made_other = surface(other_id, bem_other, pieces, False)
         swapped = lax.ppermute(away, "sub", swap)
-        stay, *made_mine = surface(mine_id, bem_mine)
+        stay, *made_mine = surface(mine_id, bem_mine, [split_column], True)
         payload = stay + swapped
         if first:
             bem_other, bem_mine = made_other, made_mine

time: 155 us -> 155 us (level)
  no operation moved by 1% of the time
where the time goes in v5:
time: 155 us
  blocking collectives  87.6 us (57%)
  Pallas kernels  32.5 us (21%)
  starting transfers between devices  25.5 us (16%)
  waiting for transfers between devices  7.69 us (5%)
    all_to_all x6, blocking collectives, over_chips(): lax.all_to_all(x, 'sub', 0, 0, axis_index_groups=same_core, tiled=True)  87.6 us
    ppermute x12, starting transfers between devices, exchanged(): return lax.ppermute(x, 'grp', [(i, i ^ step) for i in range(groups)])  25 us
    pallas_call x3, Pallas kernels, on_device(): call(functools.partial(leaf_kernel, width, first, last), 'leaves', tuple(...  21.3 us
    pallas_call x6, Pallas kernels, surface(): call(functools.partial(surface_kernel, width, first, made), 'surface', tu...  9.01 us
    ppermute x12, waiting for transfers between devices, exchanged(): return lax.ppermute(x, 'grp', [(i, i ^ step) for i in range(groups)])  6.06 us
  transfers between devices with their start and end apart: 18, of which 6 were waited for; matrix products, arithmetic and copies ran while one was open for 0% of the time, Pallas kernels for 18%

profile of v5, /device:TPU:0, one launch (start us, length us, event | category | flops | bytes accessed | tf_op | source)
XLA Modules:
  0.0 154.5 jit_solution(11975281097566590731)
XLA Ops:
  0.7 4.0 %collective-permute-start = (f32[128,128]{1,0:T(8,128)}, f32[128,128]{1,0:T(8,128)S(1)}, u32[]{:S(2)}, u32[]{:S(2)}) collective-permute-start(f32[128,128]{1,0:T(8,128)} %field.3), channel_id=1, source_target_pairs={{0,64},{16,80},{32,96},{48,112},{64,0},{80,16},{96,32},{112,48},{1... | collective-permute-start | bytes 196616 | tf_op jit(solution)/shard_map/ppermute | solution.py:316
  4.8 1.0 start.1
  5.7 1.5 collective-permute-done
  7.2 19.5 %all_to_all.30.mine = f32[8,256,128]{2,1,0:T(8,128)S(1)} all-to-all(f32[8,256,128]{2,1,0:T(8,128)S(1)} %start.1), channel_id=1, replica_groups={{0,2,4,6,8,10,12,14},{1,3,5,7,9,11,13,15},{16,18,20,22,24,26,28,30},{17..., dimensions={0} | all-to-all | bytes 2097152 | tf_op jit(solution)/shard_map/all_to_all | solution.py:313
  26.7 3.1 %collective-permute-start.3 = (f32[256,128]{1,0:T(8,128)S(1)}, f32[256,128]{1,0:T(8,128)S(1)}, u32[]{:S(2)}, u32[]{:S(2)}) collective-permute-start(f32[256,128]{1,0:T(8,128)S(1)} %constant_dynamic-update-slice_fusion.rest_1_), channel_id=1, source_target_pairs={{0,32},{16,48},{32,0},{48,16},{64,96},{80,112},{96,64},{112,80},{1... | collective-permute-start | bytes 393224 | tf_op jit(solution)/shard_map/ppermute | solution.py:316
  29.8 1.1 collective-permute-start.2
  31.0 9.6 %leaves.3 = (f32[2,8,128,128]{3,2,1,0:T(8,128)S(1)}, f32[512,128]{1,0:T(8,128)S(1)}, bf16[2048,1024]{1,0:T(8,128)(2,1)S(1)}, bf16[2048,1024]{1,0:T(8,128)(2,1)S(...) custom-call(s32[1]{0:T(128)} %bitcast.2.here_ref, ...), custom_call_target="tpu_custom_call" | custom-call | flops 4294967296 | bytes 16777216 | tf_op jit(solution)/shard_map/leaves/pallas_call | solution.py:378
  40.7 1.9 %surface.6 = (f32[8,160,128]{2,1,0:T(8,128)S(1)}, bf16[1024,256]{1,0:T(8,128)(2,1)S(1)}, bf16[1024,1024]{1,0:T(8,128)(2,1)S(1)}, bf16[1024,1024]{1,0:T(8,128)(2,1)S(1)}) custom-call(s32[1]{0:T(128)} %bitcast.4.pick_ref, s32[1]{0:T(128)} %bitcast.5.group_ref, f32[2048,1024]{1,0:T(8,128)S(1)} %bitcast.18, ...), custom_call_target="tpu_custom_call" | custom-call | flops 1073741824 | bytes 6291456 | tf_op jit(solution)/shard_map/surface/pallas_call | solution.py:404
  42.9 0.4 split_schur.1
  43.3 1.9 %surface.7 = (f32[8,160,128]{2,1,0:T(8,128)S(1)}, bf16[1024,1024]{1,0:T(8,128)(2,1)S(1)}, bf16[1024,1024]{1,0:T(8,128)(2,1)S(1)}) custom-call(s32[1]{0:T(128)} %bitcast.3.pick_ref.core_ref, s32[1]{0:T(128)} %bitcast.5.group_ref, f32[2048,1024]{1,0:T(8,128)S(1)} %bitcast.18, bf16[1024,256]{1,0:T(8,128)(2,1)S(1)} %get-tuple-element.68.rest_1_, ...), custom_call_target="tpu_custom_call" | custom-call | flops 1073741824 | bytes 6291456 | tf_op jit(solution)/shard_map/surface/pallas_call | solution.py:404
  45.3 14.9 %all_to_all.31.got = f32[8,160,128]{2,1,0:T(8,128)S(1)} all-to-all(f32[8,160,128]{2,1,0:T(8,128)S(1)} %add.9), channel_id=1, replica_groups={{0,2,4,6,8,10,12,14},{1,3,5,7,9,11,13,15},{16,18,20,22,24,26,28,30},{17..., dimensions={0} | all-to-all | bytes 1310720 | tf_op jit(solution)/shard_map/all_to_all | solution.py:313
  60.2 3.7 %collective-permute-start.6 = (f32[128,128]{1,0:T(8,128)S(1)}, f32[128,128]{1,0:T(8,128)S(1)}, u32[]{:S(2)}, u32[]{:S(2)}) collective-permute-start(f32[128,128]{1,0:T(8,128)S(1)} %field.4), channel_id=1, source_target_pairs={{0,64},{16,80},{32,96},{48,112},{64,0},{80,16},{96,32},{112,48},{1... | collective-permute-start | bytes 196616 | tf_op jit(solution)/shard_map/ppermute | solution.py:316
  63.9 2.2 %collective-permute-done.6 = f32[128,128]{1,0:T(8,128)S(1)} collective-permute-done((f32[128,128]{1,0:T(8,128)S(1)}, f32[128,128]{1,0:T(8,128)S(1)}, u32[]{:S(2)}, u32[]{:S(2)}) %collective-permute-start.6) | collective-permute-done | bytes 65568 | tf_op jit(solution)/shard_map/ppermute | solution.py:316
  66.1 12.4 %all_to_all.32.mine = f32[8,160,128]{2,1,0:T(8,128)S(1)} all-to-all(f32[8,160,128]{2,1,0:T(8,128)S(1)} %wide.2), channel_id=1, replica_groups={{0,2,4,6,8,10,12,14},{1,3,5,7,9,11,13,15},{16,18,20,22,24,26,28,30},{17..., dimensions={0} | all-to-all | bytes 1310720 | tf_op jit(solution)/shard_map/all_to_all | solution.py:313
  78.5 3.6 %collective-permute-start.9 = (f32[256,128]{1,0:T(8,128)S(1)}, f32[256,128]{1,0:T(8,128)S(1)}, u32[]{:S(2)}, u32[]{:S(2)}) collective-permute-start(f32[256,128]{1,0:T(8,128)S(1)} %constant_dynamic-update-slice_fusion.2.rest_2_), channel_id=1, source_target_pairs={{0,32},{16,48},{32,0},{48,16},{64,96},{80,112},{96,64},{112,80},{1... | collective-permute-start | bytes 393224 | tf_op jit(solution)/shard_map/ppermute | solution.py:316
  82.1 1.1 collective-permute-start.8
  83.2 5.7 %leaves.4 = (f32[2,8,128,128]{3,2,1,0:T(8,128)S(1)}, f32[512,128]{1,0:T(8,128)S(1)}) custom-call(s32[1]{0:T(128)} %bitcast.2.here_ref, s32[1,2,1,8]{3,2,1,0:T(1,128)S(1)} %bitcast.32, s32[1,2]{1,0:T(1,128)S(1)} %copy-done.6, s32[1,2]{1,0:T(1,128)S(1)} %copy-done.7, f32[2,1024,128]{2,1,0:T(8,128)S(1)} %bitcast.20, f32[16,128]{1,0:T(8,128)S(1)} %bitcast.26, ...), custom_call_target="tpu_custom_call" | custom-call | flops 4294967296 | bytes 16777216 | tf_op jit(solution)/shard_map/leaves/pallas_call | solution.py:378
  89.1 1.3 surface.8
  90.5 1.3 surface.9
  91.8 0.8 collective-permute-done.11
  92.7 14.3 %all_to_all.33.got = f32[8,160,128]{2,1,0:T(8,128)S(1)} all-to-all(f32[8,160,128]{2,1,0:T(8,128)S(1)} %add.10), channel_id=1, replica_groups={{0,2,4,6,8,10,12,14},{1,3,5,7,9,11,13,15},{16,18,20,22,24,26,28,30},{17..., dimensions={0} | all-to-all | bytes 1310720 | tf_op jit(solution)/shard_map/all_to_all | solution.py:313
  107.0 3.6 %collective-permute-start.12 = (f32[128,128]{1,0:T(8,128)S(1)}, f32[128,128]{1,0:T(8,128)S(1)}, u32[]{:S(2)}, u32[]{:S(2)}) collective-permute-start(f32[128,128]{1,0:T(8,128)S(1)} %field.5), channel_id=1, source_target_pairs={{0,64},{16,80},{32,96},{48,112},{64,0},{80,16},{96,32},{112,48},{1... | collective-permute-start | bytes 196616 | tf_op jit(solution)/shard_map/ppermute | solution.py:316
  110.7 2.2 %collective-permute-done.12 = f32[128,128]{1,0:T(8,128)S(1)} collective-permute-done((f32[128,128]{1,0:T(8,128)S(1)}, f32[128,128]{1,0:T(8,128)S(1)}, u32[]{:S(2)}, u32[]{:S(2)}) %collective-permute-start.12) | collective-permute-done | bytes 65568 | tf_op jit(solution)/shard_map/ppermute | solution.py:316
  112.9 12.3 %all_to_all.34.mine = f32[8,160,128]{2,1,0:T(8,128)S(1)} all-to-all(f32[8,160,128]{2,1,0:T(8,128)S(1)} %wide.3), channel_id=1, replica_groups={{0,2,4,6,8,10,12,14},{1,3,5,7,9,11,13,15},{16,18,20,22,24,26,28,30},{17..., dimensions={0} | all-to-all | bytes 1310720 | tf_op jit(solution)/shard_map/all_to_all | solution.py:313
  125.2 3.5 %collective-permute-start.16 = (f32[256,128]{1,0:T(8,128)S(1)}, f32[256,128]{1,0:T(8,128)S(1)}, u32[]{:S(2)}, u32[]{:S(2)}) collective-permute-start(f32[256,128]{1,0:T(8,128)S(1)} %constant_dynamic-update-slice_fusion.4.rest_2_), channel_id=1, source_target_pairs={{0,32},{16,48},{32,0},{48,16},{64,96},{80,112},{96,64},{112,80},{1... | collective-permute-start | bytes 393224 | tf_op jit(solution)/shard_map/ppermute | solution.py:316
  128.8 1.1 collective-permute-start.15
  129.9 6.0 %leaves.5 = (f32[2,1024,128]{2,1,0:T(8,128)}, f32[2,8,128,128]{3,2,1,0:T(8,128)S(1)}, f32[512,128]{1,0:T(8,128)S(1)}) custom-call(s32[1]{0:T(128)} %bitcast.2.here_ref, s32[1,2,1,8]{3,2,1,0:T(1,128)S(1)} %bitcast.33, s32[1,2]{1,0:T(1,128)S(1)} %copy-done.6, s32[1,2]{1,0:T(1,128)S(1)} %copy-done.7, f32[2,1024,128]{2,1,0:T(8,128)S(1)} %bitcast.21, ...), custom_call_target="tpu_custom_call" | custom-call | flops 4294967296 | bytes 16777216 | tf_op jit(solution)/shard_map/leaves/pallas_call | solution.py:378
  136.0 1.3 surface.10
  137.4 1.3 surface.11
  138.7 0.8 collective-permute-done.17
  139.6 14.3 %all_to_all.35.got = f32[8,160,128]{2,1,0:T(8,128)S(1)} all-to-all(f32[8,160,128]{2,1,0:T(8,128)S(1)} %add.11), channel_id=1, replica_groups={{0,2,4,6,8,10,12,14},{1,3,5,7,9,11,13,15},{16,18,20,22,24,26,28,30},{17..., dimensions={0} | all-to-all | bytes 1310720 | tf_op jit(solution)/shard_map/all_to_all | solution.py:313
  153.9 0.7 final.1
  (58 shorter events, 1.1 us)
Async XLA Ops:
  0.6 26.0 %copy-start.8 = (f32[128,128]{1,0:T(8,128)S(1)}, f32[128,128]{1,0:T(8,128)}, u32[]{:S(2)}) copy-start(f32[128,128]{1,0:T(8,128)} %field.3) | copy-start | bytes 196612
  0.6 30.3 %copy-start.5 = (s32[1,2,8,1]{2,3,1,0:T(1,128)S(1)}, s32[1,2,8,1]{2,3,1,0:T(1,128)}, u32[]{:S(2)}) copy-start(s32[1,2,8,1]{2,3,1,0:T(1,128)} %param.25) | copy-start | bytes 196
  0.7 30.3 %copy-start.7 = (s32[1,2]{1,0:T(1,128)S(1)}, s32[1,2]{1,0:T(1,128)}, u32[]{:S(2)}) copy-start(s32[1,2]{1,0:T(1,128)} %count_ref.5) | copy-start | bytes 28
  0.7 30.3 %copy-start.6 = (s32[1,2]{1,0:T(1,128)S(1)}, s32[1,2]{1,0:T(1,128)}, u32[]{:S(2)}) copy-start(s32[1,2]{1,0:T(1,128)} %size_ref.5) | copy-start | bytes 28
  0.7 30.3 %copy-start.4 = (f32[1,2,8,128]{3,2,1,0:T(8,128)S(1)}, f32[1,2,8,128]{3,2,1,0:T(8,128)}, u32[]{:S(2)}) copy-start(f32[1,2,8,128]{3,2,1,0:T(8,128)} %param.22) | copy-start | bytes 24580
  0.7 30.3 %copy-start.3 = (f32[1,2,8,128]{3,2,1,0:T(8,128)S(1)}, f32[1,2,8,128]{3,2,1,0:T(8,128)}, u32[]{:S(2)}) copy-start(f32[1,2,8,128]{3,2,1,0:T(8,128)} %param.21) | copy-start | bytes 24580
  0.7 30.3 %copy-start.1 = (f32[1,512,128]{2,1,0:T(8,128)S(1)}, f32[1,512,128]{2,1,0:T(8,128)}, u32[]{:S(2)}) copy-start(f32[1,512,128]{2,1,0:T(8,128)} %param.18) | copy-start | bytes 786436
  0.7 30.3 %copy-start = (f32[1,2,1024,128]{3,2,1,0:T(8,128)S(1)}, f32[1,2,1024,128]{3,2,1,0:T(8,128)}, u32[]{:S(2)}) copy-start(f32[1,2,1024,128]{3,2,1,0:T(8,128)} %param.17) | copy-start | bytes 3145732
  0.7 6.5 %collective-permute-start = (f32[128,128]{1,0:T(8,128)}, f32[128,128]{1,0:T(8,128)S(1)}, u32[]{:S(2)}, u32[]{:S(2)}) collective-permute-start(f32[128,128]{1,0:T(8,128)} %field.3), channel_id=1, source_target_pairs={{0,64},{16,80},{32,96},{48,112},{64,0},{80,16},{96,32},{112,48},{1... | collective-permute-start | bytes 196616 | tf_op jit(solution)/shard_map/ppermute | solution.py:316
  26.7 4.3 %collective-permute-start.4 = (f32[8,256,128]{2,1,0:T(8,128)S(1)}, f32[8,256,128]{2,1,0:T(8,128)S(1)}, u32[]{:S(2)}, u32[]{:S(2)}) collective-permute-start(f32[8,256,128]{2,1,0:T(8,128)S(1)} %all_to_all.30.mine), channel_id=1, source_target_pairs={{0,1},{1,0},{2,3},{3,2},{4,5},{5,4},{6,7},{7,6},{8,9},{9,8},{10,11... | collective-permute-start | bytes 3145736 | tf_op jit(solution)/shard_map/ppermute | solution.py:344
  26.7 13.9 %collective-permute-start.3 = (f32[256,128]{1,0:T(8,128)S(1)}, f32[256,128]{1,0:T(8,128)S(1)}, u32[]{:S(2)}, u32[]{:S(2)}) collective-permute-start(f32[256,128]{1,0:T(8,128)S(1)} %constant_dynamic-update-slice_fusion.rest_1_), channel_id=1, source_target_pairs={{0,32},{16,48},{32,0},{48,16},{64,96},{80,112},{96,64},{112,80},{1... | collective-permute-start | bytes 393224 | tf_op jit(solution)/shard_map/ppermute | solution.py:316
  29.8 10.8 %collective-permute-start.2 = (f32[256,128]{1,0:T(8,128)S(1)}, f32[256,128]{1,0:T(8,128)S(1)}, u32[]{:S(2)}, u32[]{:S(2)}) collective-permute-start(f32[256,128]{1,0:T(8,128)S(1)} %constant_dynamic-update-slice_fusion.rest_1_), channel_id=1, source_target_pairs={{0,48},{16,32},{32,16},{48,0},{64,112},{80,96},{96,80},{112,64},{1... | collective-permute-start | bytes 393224 | tf_op jit(solution)/shard_map/ppermute | solution.py:316
  30.9 9.7 %collective-permute-start.1 = (f32[256,128]{1,0:T(8,128)S(1)}, f32[256,128]{1,0:T(8,128)S(1)}, u32[]{:S(2)}, u32[]{:S(2)}) collective-permute-start(f32[256,128]{1,0:T(8,128)S(1)} %constant_dynamic-update-slice_fusion.rest_1_), channel_id=1, source_target_pairs={{0,16},{16,0},{32,48},{48,32},{64,80},{80,64},{96,112},{112,96},{1... | collective-permute-start | bytes 393224 | tf_op jit(solution)/shard_map/ppermute | solution.py:316
  30.9 9.7 %slice-start = ((s8[8388608]{0:T(1024)(128)(4,1)}), s8[4194304]{0:T(1024)(128)(4,1)S(1)}, s32[]{:S(2)}) async-start(s8[8388608]{0:T(1024)(128)(4,1)} %bitcast.17), calls=%async_computation.6 | async-start | bytes 8388608
  31.0 9.7 %slice-start.1 = ((s8[8388608]{0:T(1024)(128)(4,1)}), s8[4194304]{0:T(1024)(128)(4,1)S(1)}, s32[]{:S(2)}) async-start(s8[8388608]{0:T(1024)(128)(4,1)} %bitcast.17), calls=%async_computation.7 | async-start | bytes 8388608
  42.6 2.5 %collective-permute-start.5 = (f32[8,160,128]{2,1,0:T(8,128)S(1)}, f32[8,160,128]{2,1,0:T(8,128)S(1)}, u32[]{:S(2)}, u32[]{:S(2)}) collective-permute-start(f32[8,160,128]{2,1,0:T(8,128)S(1)} %get-tuple-element.74), channel_id=1, source_target_pairs={{0,1},{1,0},{2,3},{3,2},{4,5},{5,4},{6,7},{7,6},{8,9},{9,8},{10,11... | collective-permute-start | bytes 1966088 | tf_op jit(solution)/shard_map/ppermute | solution.py:418
  45.1 15.0 %copy-start.2 = (f32[128,128]{1,0:T(8,128)S(1)}, f32[128,128]{1,0:T(8,128)}, u32[]{:S(2)}) copy-start(f32[128,128]{1,0:T(8,128)} %load.5) | copy-start | bytes 196612
  60.2 5.9 %collective-permute-start.6 = (f32[128,128]{1,0:T(8,128)S(1)}, f32[128,128]{1,0:T(8,128)S(1)}, u32[]{:S(2)}, u32[]{:S(2)}) collective-permute-start(f32[128,128]{1,0:T(8,128)S(1)} %field.4), channel_id=1, source_target_pairs={{0,64},{16,80},{32,96},{48,112},{64,0},{80,16},{96,32},{112,48},{1... | collective-permute-start | bytes 196616 | tf_op jit(solution)/shard_map/ppermute | solution.py:316
  78.4 4.8 %collective-permute-start.10 = (f32[8,160,128]{2,1,0:T(8,128)S(1)}, f32[8,160,128]{2,1,0:T(8,128)S(1)}, u32[]{:S(2)}, u32[]{:S(2)}) collective-permute-start(f32[8,160,128]{2,1,0:T(8,128)S(1)} %all_to_all.32.mine), channel_id=1, source_target_pairs={{0,1},{1,0},{2,3},{3,2},{4,5},{5,4},{6,7},{7,6},{8,9},{9,8},{10,11... | collective-permute-start | bytes 1966088 | tf_op jit(solution)/shard_map/ppermute | solution.py:344
  78.5 10.4 %collective-permute-start.9 = (f32[256,128]{1,0:T(8,128)S(1)}, f32[256,128]{1,0:T(8,128)S(1)}, u32[]{:S(2)}, u32[]{:S(2)}) collective-permute-start(f32[256,128]{1,0:T(8,128)S(1)} %constant_dynamic-update-slice_fusion.2.rest_2_), channel_id=1, source_target_pairs={{0,32},{16,48},{32,0},{48,16},{64,96},{80,112},{96,64},{112,80},{1... | collective-permute-start | bytes 393224 | tf_op jit(solution)/shard_map/ppermute | solution.py:316
  82.1 7.0 %collective-permute-start.8 = (f32[256,128]{1,0:T(8,128)S(1)}, f32[256,128]{1,0:T(8,128)S(1)}, u32[]{:S(2)}, u32[]{:S(2)}) collective-permute-start(f32[256,128]{1,0:T(8,128)S(1)} %constant_dynamic-update-slice_fusion.2.rest_2_), channel_id=1, source_target_pairs={{0,48},{16,32},{32,16},{48,0},{64,112},{80,96},{96,80},{112,64},{1... | collective-permute-start | bytes 393224 | tf_op jit(solution)/shard_map/ppermute | solution.py:316
  83.2 5.8 %collective-permute-start.7 = (f32[256,128]{1,0:T(8,128)S(1)}, f32[256,128]{1,0:T(8,128)S(1)}, u32[]{:S(2)}, u32[]{:S(2)}) collective-permute-start(f32[256,128]{1,0:T(8,128)S(1)} %constant_dynamic-update-slice_fusion.2.rest_2_), channel_id=1, source_target_pairs={{0,16},{16,0},{32,48},{48,32},{64,80},{80,64},{96,112},{112,96},{1... | collective-permute-start | bytes 393224 | tf_op jit(solution)/shard_map/ppermute | solution.py:316
  90.4 2.2 %collective-permute-start.11 = (f32[8,160,128]{2,1,0:T(8,128)S(1)}, f32[8,160,128]{2,1,0:T(8,128)S(1)}, u32[]{:S(2)}, u32[]{:S(2)}) collective-permute-start(f32[8,160,128]{2,1,0:T(8,128)S(1)} %get-tuple-element.94), channel_id=1, source_target_pairs={{0,1},{1,0},{2,3},{3,2},{4,5},{5,4},{6,7},{7,6},{8,9},{9,8},{10,11... | collective-permute-start | bytes 1966088 | tf_op jit(solution)/shard_map/ppermute | solution.py:418
  107.0 5.9 %collective-permute-start.12 = (f32[128,128]{1,0:T(8,128)S(1)}, f32[128,128]{1,0:T(8,128)S(1)}, u32[]{:S(2)}, u32[]{:S(2)}) collective-permute-start(f32[128,128]{1,0:T(8,128)S(1)} %field.5), channel_id=1, source_target_pairs={{0,64},{16,80},{32,96},{48,112},{64,0},{80,16},{96,32},{112,48},{1... | collective-permute-start | bytes 196616 | tf_op jit(solution)/shard_map/ppermute | solution.py:316
  125.2 4.7 %collective-permute-start.13 = (f32[8,160,128]{2,1,0:T(8,128)S(1)}, f32[8,160,128]{2,1,0:T(8,128)S(1)}, u32[]{:S(2)}, u32[]{:S(2)}) collective-permute-start(f32[8,160,128]{2,1,0:T(8,128)S(1)} %all_to_all.34.mine), channel_id=1, source_target_pairs={{0,1},{1,0},{2,3},{3,2},{4,5},{5,4},{6,7},{7,6},{8,9},{9,8},{10,11... | collective-permute-start | bytes 1966088 | tf_op jit(solution)/shard_map/ppermute | solution.py:344
  125.2 10.7 %collective-permute-start.16 = (f32[256,128]{1,0:T(8,128)S(1)}, f32[256,128]{1,0:T(8,128)S(1)}, u32[]{:S(2)}, u32[]{:S(2)}) collective-permute-start(f32[256,128]{1,0:T(8,128)S(1)} %constant_dynamic-update-slice_fusion.4.rest_2_), channel_id=1, source_target_pairs={{0,32},{16,48},{32,0},{48,16},{64,96},{80,112},{96,64},{112,80},{1... | collective-permute-start | bytes 393224 | tf_op jit(solution)/shard_map/ppermute | solution.py:316
  128.8 7.2 %collective-permute-start.15 = (f32[256,128]{1,0:T(8,128)S(1)}, f32[256,128]{1,0:T(8,128)S(1)}, u32[]{:S(2)}, u32[]{:S(2)}) collective-permute-start(f32[256,128]{1,0:T(8,128)S(1)} %constant_dynamic-update-slice_fusion.4.rest_2_), channel_id=1, source_target_pairs={{0,48},{16,32},{32,16},{48,0},{64,112},{80,96},{96,80},{112,64},{1... | collective-permute-start | bytes 393224 | tf_op jit(solution)/shard_map/ppermute | solution.py:316
  129.9 6.1 %collective-permute-start.14 = (f32[256,128]{1,0:T(8,128)S(1)}, f32[256,128]{1,0:T(8,128)S(1)}, u32[]{:S(2)}, u32[]{:S(2)}) collective-permute-start(f32[256,128]{1,0:T(8,128)S(1)} %constant_dynamic-update-slice_fusion.4.rest_2_), channel_id=1, source_target_pairs={{0,16},{16,0},{32,48},{48,32},{64,80},{80,64},{96,112},{112,96},{1... | collective-permute-start | bytes 393224 | tf_op jit(solution)/shard_map/ppermute | solution.py:316
  137.3 2.2 %collective-permute-start.17 = (f32[8,160,128]{2,1,0:T(8,128)S(1)}, f32[8,160,128]{2,1,0:T(8,128)S(1)}, u32[]{:S(2)}, u32[]{:S(2)}) collective-permute-start(f32[8,160,128]{2,1,0:T(8,128)S(1)} %get-tuple-element.104), channel_id=1, source_target_pairs={{0,1},{1,0},{2,3},{3,2},{4,5},{5,4},{6,7},{7,6},{8,9},{9,8},{10,11... | collective-permute-start | bytes 1966088 | tf_op jit(solution)/shard_map/ppermute | solution.py:418
